TPU v7x, 128 devices: a whole 4x4x4 slice. The times are simulated.
128 devices in a mesh: feat: 8 (over z, y_lo), tile: 16 (over y_hi, x, core).
Axes of the slice: x: 4, y: 4 (y_hi: 2, y_lo: 2; y = y_hi * 2 + y_lo), z: 4, core: 2. Of those that a mesh axis runs over, the one named last changes fastest.
Arguments:
- images: bfloat16 [12288, 12288], P(('feat', 'tile')), may hold values from -6 to 6
- row_list: int32 [12288], P(('feat', 'tile')), may hold values from 0 to 95
- labels: int32 [12288], P(('feat', 'tile')), may hold values from 0 to 999
- filters: bfloat16 [6, 6, 3, 1024], replicated, may hold values from -0.625 to 0.625
- bias: float32 [1024], replicated, may hold values from -0.8 to 0.4
- tile_owner: int32 [136], replicated, may hold values from 0 to 15, as said below
Outputs:
- gram_tiles: float32 [320, 256, 256], P('tile', 'feat')
- cross: float32 [4096, 1000], P(('feat', 'tile'))
Inputs may be any that keep to these rules, and one draw needn't show every extreme that they name: `row_list`: each entry indexes the stored images of the device that holds that entry's position. `tile_owner`: no owner has more than 20 tiles, and one owner has exactly 20.
All inputs are finite; a program needn't handle non-finite values.
Results may differ from a plain program's by a relative error of at most 0.0003.
Values may be sent and summed in bfloat16 or wider, within the bound.
No kernel may reach another device: no remote copies, remote signals or barrier semaphores. Data moves between devices by JAX's collectives and lax.ppermute only.
A program may use at most 192 MiB of HBM per device.

v0:
```python
import jax
import jax.numpy as jnp
import numpy as np
from jax import lax
from jax.sharding import PartitionSpec as P

IMG = 64
FILTERS = 1024
D = 4096
TS = 256
NB = 16
NTILES = 136
MAXT = 20
CLASSES = 1000


def featurize(block, filters, bias):
    count = block.shape[0]
    pictures = block.reshape(count, IMG, IMG, 3)
    conv = lax.conv_general_dilated(
        pictures,
        filters,
        (2, 2),
        "VALID",
        dimension_numbers=("NHWC", "HWIO", "NHWC"),
        preferred_element_type=jnp.float32,
    )
    active = jnp.maximum(conv + bias, 0.0)
    side = conv.shape[1] // 2
    pooled = jnp.mean(active.reshape(count, 2, side, 2, side, FILTERS), axis=(2, 4))
    return pooled.reshape(count, 4 * FILTERS).astype(jnp.bfloat16)


def tile_product(grouped, row_block, col_block):
    left = lax.dynamic_slice_in_dim(grouped, row_block * TS, TS, 1)
    right = lax.dynamic_slice_in_dim(grouped, col_block * TS, TS, 1)
    return lax.dot_general(
        left, right, (((0,), (0,)), ((), ())), preferred_element_type=jnp.float32
    )


def one_hot_signs(label):
    return jnp.where(
        label[:, None] == jnp.arange(CLASSES, dtype=jnp.int32)[None, :], 1.0, -1.0
    ).astype(jnp.bfloat16)


def body(images, row_list, labels, filters, bias, tile_owner):
    local = images.shape[0]
    n_feat = lax.axis_size("feat")
    n_tile = lax.axis_size("tile")
    total = local * n_feat * n_tile
    chosen = jnp.take(images, row_list, axis=0)
    label = jnp.take(labels, row_list, axis=0)
    group = 8
    blocks = chosen.reshape(local // group, group, chosen.shape[1])
    feats = lax.map(lambda part: featurize(part, filters, bias), blocks).reshape(local, D)
    columns_all = lax.all_to_all(feats, ("feat", "tile"), split_axis=1, concat_axis=0, tiled=True)
    label_all = lax.all_gather(label, ("feat", "tile"), axis=0, tiled=True)
    targets_all = one_hot_signs(label_all)
    cross = (
        lax.dot_general(
            columns_all, targets_all, (((0,), (0,)), ((), ())), preferred_element_type=jnp.float32
        )
        / total
    )
    grouped = lax.all_gather(feats, "tile", axis=0, tiled=True)
    rows_np, cols_np = np.triu_indices(NB)
    tile_rows_of = jnp.asarray(rows_np, dtype=jnp.int32)
    tile_cols_of = jnp.asarray(cols_np, dtype=jnp.int32)
    order = jnp.arange(NTILES, dtype=jnp.int32)
    same = tile_owner[:, None] == tile_owner[None, :]
    before = order[:, None] > order[None, :]
    slot = jnp.sum((same & before).astype(jnp.int32), axis=1)
    me_tile = lax.axis_index("tile")
    mine = tile_owner == me_tile
    owned = jnp.sum(mine.astype(jnp.int32))
    slots = jnp.arange(MAXT, dtype=jnp.int32)
    match = mine[None, :] & (slot[None, :] == slots[:, None])
    tile_of_slot = jnp.sum(jnp.where(match, order[None, :], 0), axis=1)

    def one_slot(index, buffer):
        which = tile_of_slot[index]
        product = tile_product(grouped, tile_rows_of[which], tile_cols_of[which])
        return lax.dynamic_update_index_in_dim(buffer, product, index, 0)

    buffer = lax.fori_loop(0, owned, one_slot, jnp.zeros((MAXT, TS, TS), jnp.float32))
    gram_tiles = lax.psum_scatter(buffer, "feat", scatter_dimension=1, tiled=True) / total
    return (gram_tiles, cross)


def solution(mesh):
    return jax.shard_map(
        body,
        mesh=mesh,
        in_specs=(
            P(("feat", "tile"), None),
            P(("feat", "tile")),
            P(("feat", "tile")),
            P(),
            P(),
            P(),
        ),
        out_specs=(P("tile", "feat", None), P(("feat", "tile"), None)),
        check_vma=False,
    )
```

profile of v0, /device:TPU:0, one launch (start us, length us, event | category | flops | bytes accessed | tf_op | source)
XLA Modules:
  0.0 1181.6 jit_solution(8158605834467481643)
XLA Ops:
  12.3 24.2 %copy.16 = bf16[12,8,12288]{1,2,0:T(8,128)(2,1)} copy(bf16[12,8,12288]{2,1,0:T(8,128)(2,1)} %bitcast.36) | data formatting | bytes 4718592 | tf_op jit(solution)/shard_map/jit(_take)/gather | solution.py:53
  36.5 25.7 %broadcast_select_fusion = bf16[12,8,12288]{1,2,0:T(8,128)(2,1)} fusion(bf16[12,8,12288]{1,2,0:T(8,128)(2,1)} %copy.16, pred[12,8]{1,0:T(8,128)(4,1)S(1)} %broadcast_in_dim.67), kind=kLoop, calls=%fused_computation.13 | loop fusion | flops 1179648 | bytes 4718688 | tf_op jit(solution)/shard_map/jit(_take)/select_n | solution.py:53
  62.3 731.3 %while.21 = (s32[]{:T(128)}, bf16[12,8,4096]{2,1,0:T(8,128)(2,1)}, bf16[12,8,12288]{1,2,0:T(8,128)(2,1)}, bf16[6,6,3,1024]{3,2,1,0:T(4,128)(2,1)S(1)}, f32[1024]{0:T(1024)S(1)}, /*index=5*/s32[]{:T(128)}, f32[]{:T(128)}) while((s32[]{:T(128)}, bf16[12,8,4096]{2,1,0:T(8,128)(2,1)}, bf16[12,8,12288]{1,2,0:T(8,128)(2,1)}, ...), condition=%wide.region_5.6_spmd, body=%wide.region_3.5_spmd.sunk | while | flops 1614675968 | bytes 60650068 | solution.py:57
  74.6 36.7 %add_maximum_fusion.2 = f32[8,30,30,1024]{3,0,2,1:T(8,128)} fusion(f32[1024]{0:T(1024)S(1)} %get-tuple-element.193, bf16[8,64,64,3]{0,3,2,1:T(4,128)(2,1)} %reshape.80, bf16[6,6,3,1024]{3,2,1,0:T(4,128)(2,1)S(1)} %get-tuple-element.192), kind=kOutput, calls=%fused_computation.2.clone.1 | convolution fusion | flops 1607270400 | bytes 29913088 | tf_op jit(solution)/shard_map/while/body/eval_jaxpr/conv_general_dilated | solution.py:20
  111.3 11.3 reduce_sum.43
  135.6 36.7 %add_maximum_fusion.2 = f32[8,30,30,1024]{3,0,2,1:T(8,128)} fusion(f32[1024]{0:T(1024)S(1)} %get-tuple-element.193, bf16[8,64,64,3]{0,3,2,1:T(4,128)(2,1)} %reshape.80, bf16[6,6,3,1024]{3,2,1,0:T(4,128)(2,1)S(1)} %get-tuple-element.192), kind=kOutput, calls=%fused_computation.2.clone.1 | convolution fusion | flops 1607270400 | bytes 29913088 | tf_op jit(solution)/shard_map/while/body/eval_jaxpr/conv_general_dilated | solution.py:20
  172.2 11.3 reduce_sum.43
  196.5 36.7 %add_maximum_fusion.2 = f32[8,30,30,1024]{3,0,2,1:T(8,128)} fusion(f32[1024]{0:T(1024)S(1)} %get-tuple-element.193, bf16[8,64,64,3]{0,3,2,1:T(4,128)(2,1)} %reshape.80, bf16[6,6,3,1024]{3,2,1,0:T(4,128)(2,1)S(1)} %get-tuple-element.192), kind=kOutput, calls=%fused_computation.2.clone.1 | convolution fusion | flops 1607270400 | bytes 29913088 | tf_op jit(solution)/shard_map/while/body/eval_jaxpr/conv_general_dilated | solution.py:20
  233.2 11.3 reduce_sum.43
  257.4 36.7 %add_maximum_fusion.2 = f32[8,30,30,1024]{3,0,2,1:T(8,128)} fusion(f32[1024]{0:T(1024)S(1)} %get-tuple-element.193, bf16[8,64,64,3]{0,3,2,1:T(4,128)(2,1)} %reshape.80, bf16[6,6,3,1024]{3,2,1,0:T(4,128)(2,1)S(1)} %get-tuple-element.192), kind=kOutput, calls=%fused_computation.2.clone.1 | convolution fusion | flops 1607270400 | bytes 29913088 | tf_op jit(solution)/shard_map/while/body/eval_jaxpr/conv_general_dilated | solution.py:20
  294.1 11.3 reduce_sum.43
  318.3 36.7 %add_maximum_fusion.2 = f32[8,30,30,1024]{3,0,2,1:T(8,128)} fusion(f32[1024]{0:T(1024)S(1)} %get-tuple-element.193, bf16[8,64,64,3]{0,3,2,1:T(4,128)(2,1)} %reshape.80, bf16[6,6,3,1024]{3,2,1,0:T(4,128)(2,1)S(1)} %get-tuple-element.192), kind=kOutput, calls=%fused_computation.2.clone.1 | convolution fusion | flops 1607270400 | bytes 29913088 | tf_op jit(solution)/shard_map/while/body/eval_jaxpr/conv_general_dilated | solution.py:20
  379.3 36.7 %add_maximum_fusion.2 = f32[8,30,30,1024]{3,0,2,1:T(8,128)} fusion(f32[1024]{0:T(1024)S(1)} %get-tuple-element.193, bf16[8,64,64,3]{0,3,2,1:T(4,128)(2,1)} %reshape.80, bf16[6,6,3,1024]{3,2,1,0:T(4,128)(2,1)S(1)} %get-tuple-element.192), kind=kOutput, calls=%fused_computation.2.clone.1 | convolution fusion | flops 1607270400 | bytes 29913088 | tf_op jit(solution)/shard_map/while/body/eval_jaxpr/conv_general_dilated | solution.py:20
  440.2 36.7 %add_maximum_fusion.2 = f32[8,30,30,1024]{3,0,2,1:T(8,128)} fusion(f32[1024]{0:T(1024)S(1)} %get-tuple-element.193, bf16[8,64,64,3]{0,3,2,1:T(4,128)(2,1)} %reshape.80, bf16[6,6,3,1024]{3,2,1,0:T(4,128)(2,1)S(1)} %get-tuple-element.192), kind=kOutput, calls=%fused_computation.2.clone.1 | convolution fusion | flops 1607270400 | bytes 29913088 | tf_op jit(solution)/shard_map/while/body/eval_jaxpr/conv_general_dilated | solution.py:20
  501.2 36.7 %add_maximum_fusion.2 = f32[8,30,30,1024]{3,0,2,1:T(8,128)} fusion(f32[1024]{0:T(1024)S(1)} %get-tuple-element.193, bf16[8,64,64,3]{0,3,2,1:T(4,128)(2,1)} %reshape.80, bf16[6,6,3,1024]{3,2,1,0:T(4,128)(2,1)S(1)} %get-tuple-element.192), kind=kOutput, calls=%fused_computation.2.clone.1 | convolution fusion | flops 1607270400 | bytes 29913088 | tf_op jit(solution)/shard_map/while/body/eval_jaxpr/conv_general_dilated | solution.py:20
  562.1 36.7 %add_maximum_fusion.2 = f32[8,30,30,1024]{3,0,2,1:T(8,128)} fusion(f32[1024]{0:T(1024)S(1)} %get-tuple-element.193, bf16[8,64,64,3]{0,3,2,1:T(4,128)(2,1)} %reshape.80, bf16[6,6,3,1024]{3,2,1,0:T(4,128)(2,1)S(1)} %get-tuple-element.192), kind=kOutput, calls=%fused_computation.2.clone.1 | convolution fusion | flops 1607270400 | bytes 29913088 | tf_op jit(solution)/shard_map/while/body/eval_jaxpr/conv_general_dilated | solution.py:20
  598.8 11.3 reduce_sum.43
  623.0 36.7 %add_maximum_fusion.2 = f32[8,30,30,1024]{3,0,2,1:T(8,128)} fusion(f32[1024]{0:T(1024)S(1)} %get-tuple-element.193, bf16[8,64,64,3]{0,3,2,1:T(4,128)(2,1)} %reshape.80, bf16[6,6,3,1024]{3,2,1,0:T(4,128)(2,1)S(1)} %get-tuple-element.192), kind=kOutput, calls=%fused_computation.2.clone.1 | convolution fusion | flops 1607270400 | bytes 29913088 | tf_op jit(solution)/shard_map/while/body/eval_jaxpr/conv_general_dilated | solution.py:20
  684.0 36.7 %add_maximum_fusion.2 = f32[8,30,30,1024]{3,0,2,1:T(8,128)} fusion(f32[1024]{0:T(1024)S(1)} %get-tuple-element.193, bf16[8,64,64,3]{0,3,2,1:T(4,128)(2,1)} %reshape.80, bf16[6,6,3,1024]{3,2,1,0:T(4,128)(2,1)S(1)} %get-tuple-element.192), kind=kOutput, calls=%fused_computation.2.clone.1 | convolution fusion | flops 1607270400 | bytes 29913088 | tf_op jit(solution)/shard_map/while/body/eval_jaxpr/conv_general_dilated | solution.py:20
  744.9 36.7 %add_maximum_fusion.2 = f32[8,30,30,1024]{3,0,2,1:T(8,128)} fusion(f32[1024]{0:T(1024)S(1)} %get-tuple-element.193, bf16[8,64,64,3]{0,3,2,1:T(4,128)(2,1)} %reshape.80, bf16[6,6,3,1024]{3,2,1,0:T(4,128)(2,1)S(1)} %get-tuple-element.192), kind=kOutput, calls=%fused_computation.2.clone.1 | convolution fusion | flops 1607270400 | bytes 29913088 | tf_op jit(solution)/shard_map/while/body/eval_jaxpr/conv_general_dilated | solution.py:20
  794.8 92.3 %all-gather.2.cloned.1.call-done = bf16[1536,4096]{1,0:T(8,128)(2,1)} async-done(((bf16[96,4096]{1,0:T(8,128)(2,1)}), bf16[1536,4096]{1,0:T(8,128)(2,1)}) %all-gather.2.cloned.1.call-update) | async-done | bytes 12582928 | tf_op jit(solution)/shard_map/all_gather | solution.py:67
  889.9 162.8 %while.22 = (s32[]{:T(128)}, f32[20,256,256]{2,1,0:T(8,128)}, s32[]{:T(128)}, s32[20]{0:T(128)S(1)}, bf16[1536,4096]{1,0:T(8,128)(2,1)}, /*index=5*/s32[]{:T(128...) while((s32[]{:T(128)}, f32[20,256,256]{2,1,0:T(8,128)}, ...), condition=%wide.region_7.8_spmd.clone, body=%wide.region_6.7_spmd.sunk.clone.sunk | while | flops 201326608 | bytes 1835341 | solution.py:87
  1068.1 73.7 %all-reduce = s32[12288]{0:T(1024)S(1)} all-reduce(s32[12288]{0:T(1024)S(1)} %select_dynamic-update-slice_fusion), channel_id=1, replica_groups=mesh['feat'=8,'tile'=16] {'feat','tile'}, use_global_device_ids=true, to_apply=%add | all-reduce | flops 12288 | bytes 98304
  1151.4 21.4 %reduce-scatter.2.cloned.1.call-done = f32[20,32,256]{2,1,0:T(8,128)} async-done(((f32[20,256,256]{2,1,0:T(8,128)}), f32[20,32,256]{2,1,0:T(8,128)}) %reduce-scatter.2.cloned.1.call-update) | async-done | bytes 655376 | tf_op jit(solution)/shard_map/reduce_scatter | solution.py:88
  (182 shorter events, 357.2 us)
Async XLA Ops:
  7.2 1.7 copy-start
  7.2 879.9 %all-gather.2.cloned.1.call-start = ((), (), s32[]{:S(2)}) async-start(), calls=%async_computation.2 | async-start | bytes 13369344 | tf_op jit(solution)/shard_map/all_gather | solution.py:67
  8.9 27.6 %copy-start.5 = (s32[1024]{0:T(1024)}, s32[1024]{0:T(1024)S(1)}, u32[]{:S(2)}) copy-start(s32[1024]{0:T(1024)S(1)} %pad_clamp_fusion) | copy-start | bytes 12292
  36.5 25.7 %copy-start.7 = (bf16[6,6,3,1024]{3,2,1,0:T(4,128)(2,1)S(1)}, bf16[6,6,3,1024]{3,2,1,0:T(4,128)(2,1)}, u32[]{:S(2)}) copy-start(bf16[6,6,3,1024]{3,2,1,0:T(4,128)(2,1)} %param.15) | copy-start | bytes 663556
  36.5 25.7 %copy-start.8 = (f32[1024]{0:T(1024)S(1)}, f32[1024]{0:T(1024)}, u32[]{:S(2)}) copy-start(f32[1024]{0:T(1024)} %param.16) | copy-start | bytes 12292
  62.3 731.6 %copy-start.4 = (s32[136]{0:T(256)S(1)}, s32[136]{0:T(256)}, u32[]{:S(2)}) copy-start(s32[136]{0:T(256)} %param.17) | copy-start | bytes 1636
  62.3 827.6 %copy-start.9 = (s32[136]{0:T(256)S(1)}, s32[136]{0:T(256)}, u32[]{:S(2)}) copy-start(s32[136]{0:T(256)} %constant.84.clone..sunk.2) | copy-start | bytes 1636
  62.3 827.6 %copy-start.10 = (s32[136]{0:T(256)S(1)}, s32[136]{0:T(256)}, u32[]{:S(2)}) copy-start(s32[136]{0:T(256)} %constant.85.clone..sunk.2) | copy-start | bytes 1636
  793.6 259.2 %copy-start.3 = (bf16[12,8,4096]{2,1,0:T(8,128)(2,1)S(1)}, bf16[12,8,4096]{2,1,0:T(8,128)(2,1)}, u32[]{:S(2)}) copy-start(bf16[12,8,4096]{2,1,0:T(8,128)(2,1)} %get-tuple-element.67) | copy-start | bytes 2359300
  793.6 379.2 %reduce-scatter.2.cloned.1.call-start = ((), (), s32[]{:S(2)}) async-start(), calls=%async_computation.3 | async-start | bytes 5898240 | tf_op jit(solution)/shard_map/reduce_scatter | solution.py:88
  889.9 176.6 %copy-start.2 = (s32[96]{0:T(128)S(1)}, s32[96]{0:T(128)}, u32[]{:S(2)}) copy-start(s32[96]{0:T(128)} %param.14) | copy-start | bytes 1156
  889.9 178.0 %copy-start.6 = (s32[96]{0:T(128)S(1)}, s32[96]{0:T(128)}, u32[]{:S(2)}) copy-start(s32[96]{0:T(128)} %param.13) | copy-start | bytes 1156
  1061.3 80.5 %all-to-all-start = ((bf16[96,128,32]{0,2,1:T(8,128)(2,1)}), bf16[96,128,32]{0,2,1:T(8,128)(2,1)S(1)}, u32[]{:S(2)}, u32[]{:S(2)}) async-start(bf16[96,128,32]{0,2,1:T(8,128)(2,1)} %copy.17), calls=%async_computation.1 | async-start | bytes 2097152 | tf_op jit(solution)/shard_map/all_to_all | solution.py:58
  1143.6 31.2 %copy-start.1 = (bf16[96,12288]{1,0:T(8,128)(2,1)S(1)}, bf16[96,12288]{1,0:T(8,128)(2,1)}, u32[]{:S(2)}) copy-start(bf16[96,12288]{1,0:T(8,128)(2,1)} %param.12) | copy-start | bytes 7077892
Sparse Core Ops, SparseCore 0:
  793.7 93.3 all-gather.1
  1052.9 119.8 reduce-scatter.1
where the time goes:
time: 1190 us; the launch traced here: 1180 us
  matrix products  498 us (42%)
  local copies, waits for them, and re-layouts  234 us (20%)
  other arithmetic  166 us (14%)
  waiting for transfers between devices  114 us (10%)
  loops' own time  76.2 us (6%)
  blocking collectives  73.7 us (6%)
  between operations  14.2 us (1%)
    conv_general_dilated x12, matrix products, featurize(): lax.conv_general_dilated(pictures, filters, (2, 2), 'VALID', dimension_nu...  440 us
    reduce_sum x12, other arithmetic, featurize(): jnp.mean(active.reshape(count, 2, side, 2, side, FILTERS), axis=(2, 4))  136 us
    reshape x12, local copies, waits for them, and re-layouts, featurize(): pictures = block.reshape(count, IMG, IMG, 3)  110 us
    all_gather x1, waiting for transfers between devices, body(): grouped = lax.all_gather(feats, 'tile', axis=0, tiled=True)  92.3 us
    another operation x1, loops' own time, body(): lax.fori_loop(0, owned, one_slot, jnp.zeros((MAXT, TS, TS), jnp.float32))  76.1 us
    unnamed x1, blocking collectives  73.7 us
    dot_general x20, matrix products, tile_product(): lax.dot_general(left, right, (((0,), (0,)), ((), ())), preferred_element_...  50.2 us
    dynamic_slice x12, local copies, waits for them, and re-layouts, body(): lax.map(lambda part: featurize(part, filters, bias), blocks)  37.7 us
  transfers between devices with their start and end apart: 3, of which 2 were waited for; matrix products, arithmetic and copies ran while one was open for 1% of the time, Pallas kernels for 0%

commit v1 on v0

v1 whole, which is shorter than its diff:
```python
import jax
import jax.numpy as jnp
from jax import lax
from jax.experimental import pallas as pl
from jax.experimental.pallas import tpu as pltpu
from jax.sharding import PartitionSpec as P

ROWS = 96
BLK = 16
NBLK = 6
BF = jnp.bfloat16
F32 = jnp.float32
LAG = 3


def dot(a, b, dims=(((1,), (0,)), ((), ()))):
    return lax.dot_general(a, b, dims, preferred_element_type=F32)


def prep_kernel(rows_ref, labels_ref, img_ref, filt_ref, win_ref, w_ref, sel_ref, lab_ref, nblk_ref, x_ref, pick_ref):
    lanes = lax.broadcasted_iota(jnp.int32, (ROWS, 128), 1)
    subs = lax.broadcasted_iota(jnp.int32, (ROWS, 128), 0)
    hit = rows_ref[...] == lanes
    used = jnp.max(jnp.where(hit, 1.0, 0.0), axis=0, keepdims=True)
    low = lax.broadcasted_iota(jnp.int32, (128, 128), 0)
    high = lax.broadcasted_iota(jnp.int32, (128, 128), 1)
    upto = jnp.where(low <= high, 1.0, 0.0).astype(BF)
    rank = dot(jnp.broadcast_to(used, (16, 128)).astype(BF), upto)[0:1] - 1.0
    rank = rank.astype(jnp.int32)
    compact = jnp.where((subs == rank) & (used > 0.0), 1.0, 0.0).astype(BF)
    sel_ref[:, :ROWS] = dot(jnp.where(hit, 1.0, 0.0).astype(BF), compact, (((1,), (1,)), ((), ()))).astype(BF)
    sel_ref[:, ROWS:] = jnp.zeros((ROWS, 256 - ROWS), BF)
    total = jnp.sum(used).astype(jnp.int32)
    nblk_ref[0, 0] = (total + BLK - 1) // BLK
    label = jnp.sum(jnp.where(hit, labels_ref[...], 0), axis=1, keepdims=True)
    coarse = label // 8
    fine = label - coarse * 8
    lab_ref[...] = jnp.where(lanes == 0, coarse, jnp.where(lanes == 1, fine, 0)).astype(BF)
    take = compact[:, :ROWS]
    rows_i = lax.broadcasted_iota(jnp.int32, (1536, 128), 0)
    cols_i = lax.broadcasted_iota(jnp.int32, (1536, 128), 1)
    d = rows_i // 256
    di = d // 3
    dj = d - 3 * di
    r = rows_i % 256 // 32 - 2 * di
    c = rows_i % 32 - 6 * dj
    ok = (r >= 0) & (r < 6) & (c >= 0) & (c < 18)
    spread = jnp.where(ok & (cols_i == r * 18 + c), 1.0, 0.0).astype(BF)
    for nc in range(4):
        w_ref[nc] = dot(spread, filt_ref[:, nc * 256:(nc + 1) * 256]).astype(BF)
    for part in range(16):
        x_ref[part] = dot(take, img_ref[:, part * 768:(part + 1) * 768]).astype(BF)
    col = lax.broadcasted_iota(jnp.int32, (1, 1280), 1)
    within = col % 32
    source = (col % 128) // 32 * 192 + 18 * (col // 128) + within
    source = jnp.where(within < 30, source, -1)
    place = lax.broadcasted_iota(jnp.int32, (768, 1280), 0)
    pick_ref[...] = jnp.where(place == source, 1.0, 0.0).astype(BF)

    @pl.loop(0, 16)
    def _(part):
        for n in range(5):
            tile = dot(x_ref[part], pick_ref[:, n * 256:(n + 1) * 256]).astype(BF)
            for h in range(2):
                g = 2 * n + h
                for b in range(NBLK):
                    win_ref[part, b, g * 16:(g + 1) * 16, :] = tile[b * 16:(b + 1) * 16, h * 128:(h + 1) * 128]


def prep(images, row_list, labels, flat):
    return pl.pallas_call(
        prep_kernel,
        out_shape=(
            jax.ShapeDtypeStruct((16, NBLK, 160, 128), BF),
            jax.ShapeDtypeStruct((4, 1536, 256), BF),
            jax.ShapeDtypeStruct((ROWS, 256), BF),
            jax.ShapeDtypeStruct((ROWS, 128), BF),
            jax.ShapeDtypeStruct((1, 1), jnp.int32),
        ),
        out_specs=(
            pl.BlockSpec(memory_space=pltpu.VMEM),
            pl.BlockSpec(memory_space=pltpu.VMEM),
            pl.BlockSpec(memory_space=pltpu.VMEM),
            pl.BlockSpec(memory_space=pltpu.VMEM),
            pl.BlockSpec(memory_space=pltpu.SMEM),
        ),
        scratch_shapes=[pltpu.VMEM((16, ROWS, 768), BF), pltpu.VMEM((768, 1280), BF)],
        compiler_params=pltpu.CompilerParams(vmem_limit_bytes=40 * 2**20),
        name="prep",
    )(row_list.reshape(ROWS, 1), jnp.pad(labels, (0, 32)).reshape(1, 128), images, flat)


def conv_kernel(nblk_ref, win_ref, w_ref, sel_ref, bias_ref, out_ref, uniq_ref):
    bias = bias_ref[...]
    floor = jnp.broadcast_to(-bias, (16, 256))
    uniq_ref[...] = jnp.zeros_like(uniq_ref)

    steps = []
    for dd in range(6):
        for w in range(15):
            top = w <= (7 if dd < 3 else 6)
            steps.append((dd, w, 0 if top else 1))

    def block(b, acc):
        total = [[jnp.zeros((16, 256), F32) for _ in range(2)] for _ in range(2)]

        def take(k):
            dd, w, qr = steps[k]
            for m in range(2):
                got = pltpu.matmul_pop(acc[m][k % 8]).reshape(5, 16, 256)
                total[qr][m] = total[qr][m] + jnp.sum(jnp.maximum(got, floor[None]), axis=0)

        for k, (dd, w, qr) in enumerate(steps):
            if w == 0:
                for m in range(2):
                    pltpu.matmul_push_rhs(w_ref[dd * 256:(dd + 1) * 256, :], dd % 2, m)
            for m in range(2):
                lhs = jnp.concatenate(
                    [win_ref[w, b, m * 80:(m + 1) * 80, :], win_ref[w + 1, b, m * 80:(m + 1) * 80, :]], axis=1)
                pltpu.matmul_acc_lhs(acc[m][k % 8], lhs, load_staged_rhs=dd % 2 if w == 0 else None)
            if k >= LAG:
                take(k - LAG)
        for k in range(len(steps) - LAG, len(steps)):
            take(k)
        at = pl.multiple_of(b * 16, 16)
        for qr in range(2):
            for m in range(2):
                q = 2 * qr + m
                mean = (total[qr][m] + 225.0 * bias) * (1.0 / 225.0)
                uniq_ref[pl.ds(at, 16), q * 256:(q + 1) * 256] = mean.astype(BF)

    def scoped(*accs):
        @pl.loop(0, nblk_ref[0, 0])
        def _(b):
            block(b, (accs[:8], accs[8:16]))

        for m in range(2):
            for qr in range(2):
                q = 2 * qr + m
                pltpu.matmul_push_rhs(uniq_ref[:, q * 256:(q + 1) * 256], qr, m)
                pltpu.matmul_acc_lhs(accs[16 + q], sel_ref[...], load_staged_rhs=qr)
        for q in range(4):
            out_ref[:, q * 256:(q + 1) * 256] = pltpu.matmul_pop(accs[16 + q]).astype(BF)

    pl.run_scoped(
        scoped,
        *[pltpu.ACC(m)((80, 256), F32) for m in range(2) for _ in range(8)],
        *[pltpu.ACC(q % 2)((ROWS, 256), F32) for q in range(4)],
    )


def conv(nblk, win, w, sel, bias):
    return pl.pallas_call(
        conv_kernel,
        out_shape=jax.ShapeDtypeStruct((ROWS, 1024), BF),
        in_specs=[pl.BlockSpec(memory_space=pltpu.SMEM)] + [pl.BlockSpec(memory_space=pltpu.VMEM)] * 4,
        out_specs=pl.BlockSpec(memory_space=pltpu.VMEM),
        scratch_shapes=[pltpu.VMEM((256, 1024), BF)],
        compiler_params=pltpu.CompilerParams(vmem_limit_bytes=40 * 2**20),
        cost_estimate=pl.CostEstimate(flops=2 * 86400 * 256 * 256, bytes_accessed=8 * 2**20, transcendentals=0),
        name="conv",
    )(nblk, win, w, sel, bias)


TILES = 16
OWNED = 20
SLOTS = 24
NTILES = 136
GROUP = 1536
CLASSES = 1000
FEAT = 8


def gram_kernel(me_ref, owner_ref, *refs):
    chunks, lab, outs = refs[:4], refs[4], refs[5:5 + FEAT]
    f_ref, ft_ref, target_ref, left_ref, prod_ref, list_i, list_j, sem = refs[5 + FEAT:]
    me_tile = me_ref[0]
    me_feat = me_ref[1]
    copies = []
    for nc in range(4):
        for q in range(4):
            copy = pltpu.make_async_copy(chunks[nc].at[:, q * 256:(q + 1) * 256], f_ref.at[q * 4 + nc], sem.at[q * 4 + nc])
            copy.start()
            copies.append((q * 4 + nc, copy))

    def scan(k, carry):
        i, j, n = carry
        mine = owner_ref[k] == me_tile

        @pl.when(mine)
        def _():
            list_i[n] = i
            list_j[n] = j

        wrap = j == TILES - 1
        i2 = jnp.where(wrap, i + 1, i)
        return i2, jnp.where(wrap, i2, j + 1), n + mine.astype(jnp.int32)

    _, _, owned = lax.fori_loop(0, NTILES, scan, (jnp.int32(0), jnp.int32(0), jnp.int32(0)))

    labels = lab[...].astype(F32)
    label = (labels[:, 0:1] * 8.0 + labels[:, 1:2]).astype(jnp.int32)
    for s in range(4):
        classes = lax.broadcasted_iota(jnp.int32, (GROUP, 256), 1) + 256 * s
        target_ref[:, s * 256:(s + 1) * 256] = jnp.where(label == classes, 1.0, -1.0).astype(BF)
    for t, copy in copies:
        copy.wait()
        ft_ref[t] = f_ref[t].T

    def put(slot, product):
        prod_ref[...] = product
        for k in range(FEAT):
            dz, dy = k // 2, k % 2
            peer = (me_feat // 2 + dz) % 4 * 2 + (me_feat % 2 + dy) % 2
            outs[k][slot] = prod_ref[pl.ds(pl.multiple_of(peer * 32, 32), 32), :]

    @pl.loop(0, owned)
    def _(slot):
        put(slot, dot(ft_ref[list_i[slot]], f_ref[list_j[slot]]))

    @pl.loop(owned, OWNED)
    def _(slot):
        for k in range(FEAT):
            outs[k][slot] = jnp.zeros((32, 256), F32)

    start = pl.multiple_of(me_tile % 8 * 32, 32)
    for f in range(FEAT):
        t = f // 2 * 4 + f % 2 * 2 + me_tile // 8
        left_ref[f * 32:(f + 1) * 32, :] = ft_ref[t, pl.ds(start, 32), :]
    for s in range(4):
        put(OWNED + s, dot(left_ref[...], target_ref[:, s * 256:(s + 1) * 256]))


def gram(me, tile_owner, chunks, lab):
    smem = pl.BlockSpec(memory_space=pltpu.SMEM)
    vmem = pl.BlockSpec(memory_space=pltpu.VMEM)
    return pl.pallas_call(
        gram_kernel,
        out_shape=tuple(jax.ShapeDtypeStruct((SLOTS, 32, 256), F32) for _ in range(FEAT)),
        in_specs=[smem, smem] + [pl.BlockSpec(memory_space=pl.ANY)] * 4 + [vmem],
        out_specs=tuple(vmem for _ in range(FEAT)),
        scratch_shapes=[
            pltpu.VMEM((TILES, GROUP, 256), BF),
            pltpu.VMEM((TILES, 256, GROUP), BF),
            pltpu.VMEM((GROUP, 1024), BF),
            pltpu.VMEM((256, GROUP), BF),
            pltpu.VMEM((256, 256), F32),
            pltpu.SMEM((OWNED,), jnp.int32),
            pltpu.SMEM((OWNED,), jnp.int32),
            pltpu.SemaphoreType.DMA((TILES,)),
        ],
        compiler_params=pltpu.CompilerParams(vmem_limit_bytes=50 * 2**20),
        cost_estimate=pl.CostEstimate(flops=5 * 10**9, bytes_accessed=20 * 2**20, transcendentals=0),
        name="gram",
    )(me, tile_owner, *chunks, lab)


def finish_kernel(*refs):
    parts, gram_ref, cross_ref = refs[:FEAT], refs[FEAT], refs[FEAT + 1]
    scale = 1.0 / 12288.0
    for s in range(SLOTS):
        total = parts[0][s]
        for k in range(1, FEAT):
            total = total + parts[k][s]
        total = total * scale
        if s < OWNED:
            gram_ref[s] = total
        else:
            width = min(256, CLASSES - (s - OWNED) * 256)
            cross_ref[:, (s - OWNED) * 256:(s - OWNED) * 256 + width] = total[:, :width]


def finish(parts):
    return pl.pallas_call(
        finish_kernel,
        out_shape=(jax.ShapeDtypeStruct((OWNED, 32, 256), F32), jax.ShapeDtypeStruct((32, CLASSES), F32)),
        in_specs=[pl.BlockSpec(memory_space=pltpu.VMEM)] * FEAT,
        out_specs=(pl.BlockSpec(memory_space=pltpu.VMEM),) * 2,
        compiler_params=pltpu.CompilerParams(vmem_limit_bytes=40 * 2**20),
        name="finish",
    )(*parts)


def feat_shift(dz, dy):
    return [(z * 2 + y, (z + dz) % 4 * 2 + (y + dy) % 2) for z in range(4) for y in range(2)]


def body(images, row_list, labels, filters, bias, tile_owner):
    flat = jnp.pad(filters.reshape(108, 1024), ((0, 20), (0, 0)))
    win, w, sel, lab, nblk = prep(images, row_list, labels, flat)
    labs = lax.all_gather(lab, "tile", axis=0, tiled=True)
    chunks = []
    for nc in range(4):
        own = conv(nblk, win, w[nc], sel, bias[nc * 256:(nc + 1) * 256].reshape(1, 256))
        chunks.append(lax.all_gather(own, "tile", axis=0, tiled=True))
    me = jnp.stack([lax.axis_index("tile"), lax.axis_index("feat")]).astype(jnp.int32)
    partial = gram(me, tile_owner, chunks, labs)
    parts = [partial[0]]
    for k in range(1, FEAT):
        parts.append(lax.ppermute(partial[k], "feat", feat_shift(k // 2, k % 2)))
    return finish(parts)


def solution(mesh):
    def run(*args):
        return jax.shard_map(
            body,
            mesh=mesh,
            in_specs=(P(("feat", "tile"), None), P(("feat", "tile")), P(("feat", "tile")), P(), P(), P()),
            out_specs=(P("tile", "feat", None), P(("feat", "tile"), None)),
            check_vma=False,
        )(*args)

    return run
```

time: 1190 us -> 356 us (0.30)
  the two profiles are of different devices: /device:TPU:0 before, /device:TPU:64 now
where the time goes in v1:
time: 356 us; the launch traced here: 354 us
  waiting for transfers between devices  227 us (64%)
  Pallas kernels  72.4 us (20%)
  blocking collectives  20.3 us (6%)
  between operations  13.9 us (4%)
  local copies, waits for them, and re-layouts  13.3 us (4%)
  starting transfers between devices  7.28 us (2%)
    all_gather x4, waiting for transfers between devices, body(): chunks.append(lax.all_gather(own, 'tile', axis=0, tiled=True))  150 us
    ppermute x7, waiting for transfers between devices, body(): parts.append(lax.ppermute(partial[k], 'feat', feat_shift(k // 2, k % 2)))  76.6 us
    pallas_call x4, Pallas kernels, conv(): pl.pallas_call(conv_kernel, out_shape=jax.ShapeDtypeStruct((ROWS, 1024),...  48.3 us
    all_gather x1, blocking collectives, body(): labs = lax.all_gather(lab, 'tile', axis=0, tiled=True)  20.3 us
    pallas_call x1, Pallas kernels, gram(): pl.pallas_call(gram_kernel, out_shape=tuple((jax.ShapeDtypeStruct((SLOTS,...  13.1 us
    pallas_call x1, Pallas kernels, prep(): pl.pallas_call(prep_kernel, out_shape=(jax.ShapeDtypeStruct((16, NBLK, 16...  9.93 us
    unnamed x12, local copies, waits for them, and re-layouts  9.65 us
  transfers between devices with their start and end apart: 11, of which 6 were waited for; matrix products, arithmetic and copies ran while one was open for 0% of the time, Pallas kernels for 10%

profile of v1, /device:TPU:64, one launch (start us, length us, event | category | flops | bytes accessed | tf_op | source)
XLA Modules:
  0.0 353.8 jit_solution(6516310371301433465)
XLA Ops:
  9.5 1.1 reshape.27
  10.6 1.7 copy-done
  12.3 9.9 %prep.1 = (bf16[16,6,160,128]{3,2,1,0:T(8,128)(2,1)S(1)}, bf16[4,1536,256]{2,1,0:T(8,128)(2,1)S(1)}, bf16[96,256]{1,0:T(8,128)(2,1)S(1)}, bf16[96,128]{1,0:T(8,128)(2,1)S(1)}, s32[1,1]{1,0:T(1,128)}) custom-call(s32[96,1]{1,0:T(8,128)S(1)} %copy.8.rows_ref, s32[1,128]{1,0:T(1,128)S(1)} %pad_bitcast_fusion.labels_ref, bf16[96,12288]{1,0:T(8,128)(2,1)S(1)} %copy-done, ...), custom_call_target="tpu_custom_call" | custom-call | tf_op jit(solution)/shard_map/prep/pallas_call | solution.py:71
  22.5 1.6 copy-done.1
  24.1 12.0 %conv.7 = bf16[96,1024]{1,0:T(8,128)(2,1)} custom-call(s32[1,1]{1,0:T(1,128)} %get-tuple-element.15.nblk_ref, bf16[16,6,160,128]{3,2,1,0:T(8,128)(2,1)S(1)} %get-tuple-element.16.win_ref, bf16[1536,256]{1,0:T(8,128)(2,1)S(1)} %get-tuple-element.28.w_ref, bf16[96,256]{1,0:T(8,128)(2,1)S(1)} %get-tuple-element.18.sel_ref, f32[1,256]{1,0:T(1,128)S(1)} %bitcast.20), custom_call_target="tpu_custom_call" | custom-call | flops 11324620800 | bytes 8388608 | tf_op jit(solution)/shard_map/conv/pallas_call | solution.py:153
  36.2 2.1 copy-done.2
  38.3 12.0 %conv.6 = bf16[96,1024]{1,0:T(8,128)(2,1)} custom-call(s32[1,1]{1,0:T(1,128)} %get-tuple-element.15.nblk_ref, bf16[16,6,160,128]{3,2,1,0:T(8,128)(2,1)S(1)} %copy-done.2, bf16[1536,256]{1,0:T(8,128)(2,1)S(1)} %get-tuple-element.29.w_ref, bf16[96,256]{1,0:T(8,128)(2,1)S(1)} %get-tuple-element.18.sel_ref, f32[1,256]{1,0:T(1,128)S(1)} %bitcast.19), custom_call_target="tpu_custom_call" | custom-call | flops 11324620800 | bytes 8388608 | tf_op jit(solution)/shard_map/conv/pallas_call | solution.py:153
  50.4 2.1 copy-done.3
  52.6 12.0 %conv.4 = bf16[96,1024]{1,0:T(8,128)(2,1)} custom-call(s32[1,1]{1,0:T(1,128)} %get-tuple-element.15.nblk_ref, bf16[16,6,160,128]{3,2,1,0:T(8,128)(2,1)S(1)} %copy-done.3, bf16[1536,256]{1,0:T(8,128)(2,1)S(1)} %get-tuple-element.31.w_ref, bf16[96,256]{1,0:T(8,128)(2,1)S(1)} %get-tuple-element.18.sel_ref, f32[1,256]{1,0:T(1,128)S(1)} %bitcast.18), custom_call_target="tpu_custom_call" | custom-call | flops 11324620800 | bytes 8388608 | tf_op jit(solution)/shard_map/conv/pallas_call | solution.py:153
  64.7 2.1 copy-done.4
  66.8 12.2 %conv.5 = bf16[96,1024]{1,0:T(8,128)(2,1)} custom-call(s32[1,1]{1,0:T(1,128)} %get-tuple-element.15.nblk_ref, bf16[16,6,160,128]{3,2,1,0:T(8,128)(2,1)S(1)} %copy-done.4, bf16[1536,256]{1,0:T(8,128)(2,1)S(1)} %get-tuple-element.30.w_ref, bf16[96,256]{1,0:T(8,128)(2,1)S(1)} %get-tuple-element.18.sel_ref, f32[1,256]{1,0:T(1,128)S(1)} %bitcast.17), custom_call_target="tpu_custom_call" | custom-call | flops 11324620800 | bytes 8388608 | tf_op jit(solution)/shard_map/conv/pallas_call | solution.py:153
  79.1 20.3 %all_gather.19.refs_4_ = bf16[1536,128]{1,0:T(8,128)(2,1)S(1)} all-gather(bf16[96,128]{1,0:T(8,128)(2,1)S(1)} %get-tuple-element.19), channel_id=1, replica_groups=mesh['feat'=8,'tile'=16] {'tile'}, dimensions={0}, use_global_device_ids=true | all-gather | bytes 417792 | tf_op jit(solution)/shard_map/all_gather | solution.py:291
  99.4 42.4 %all-gather.9.cloned.1.call-done.refs_2_ = bf16[1536,1024]{1,0:T(8,128)(2,1)} async-done(((bf16[96,1024]{1,0:T(8,128)(2,1)}), bf16[1536,1024]{1,0:T(8,128)(2,1)}) %all-gather.9.cloned.1.call-update) | async-done | bytes 3145744 | tf_op jit(solution)/shard_map/all_gather | solution.py:295
  141.8 54.1 %all-gather.5.cloned.1.call-done.refs_0_ = bf16[1536,1024]{1,0:T(8,128)(2,1)} async-done(((bf16[96,1024]{1,0:T(8,128)(2,1)}), bf16[1536,1024]{1,0:T(8,128)(2,1)}) %all-gather.5.cloned.1.call-update) | async-done | bytes 3145744 | tf_op jit(solution)/shard_map/all_gather | solution.py:295
  195.9 53.4 %all-gather.7.cloned.1.call-done.refs_1_ = bf16[1536,1024]{1,0:T(8,128)(2,1)} async-done(((bf16[96,1024]{1,0:T(8,128)(2,1)}), bf16[1536,1024]{1,0:T(8,128)(2,1)}) %all-gather.7.cloned.1.call-update) | async-done | bytes 3145744 | tf_op jit(solution)/shard_map/all_gather | solution.py:295
  249.3 13.1 %gram.1 = (f32[24,32,256]{2,1,0:T(8,128)S(1)}, f32[24,32,256]{2,1,0:T(8,128)S(1)}, f32[24,32,256]{2,1,0:T(8,128)S(1)}, f32[24,32,256]{2,1,0:T(8,128)S(1)}, f32[2...) custom-call(s32[2]{0:T(128)S(1)} %pad_add_fusion.me_ref, ...), custom_call_target="tpu_custom_call" | custom-call | flops 5000000000 | bytes 20971520 | tf_op jit(solution)/shard_map/gram/pallas_call | solution.py:237
  263.1 1.3 collective-permute-start.1
  264.4 1.1 collective-permute-start.2
  265.5 1.9 collective-permute-start.3
  267.4 1.6 collective-permute-start.4
  269.1 13.8 %collective-permute-done.refs_1_ = f32[24,32,256]{2,1,0:T(8,128)S(1)} collective-permute-done((f32[24,32,256]{2,1,0:T(8,128)S(1)}, f32[24,32,256]{2,1,0:T(8,128)S(1)}, u32[]{:S(2)}, u32[]{:S(2)}) %collective-permute-start) | collective-permute-done | bytes 786464 | tf_op jit(solution)/shard_map/ppermute | solution.py:300
  283.3 49.7 %collective-permute-done.1.refs_2_ = f32[24,32,256]{2,1,0:T(8,128)S(1)} collective-permute-done((f32[24,32,256]{2,1,0:T(8,128)S(1)}, f32[24,32,256]{2,1,0:T(8,128)S(1)}, u32[]{:S(2)}, u32[]{:S(2)}) %collective-permute-start.1) | collective-permute-done | bytes 786464 | tf_op jit(solution)/shard_map/ppermute | solution.py:300
  333.1 13.1 %collective-permute-done.6.refs_7_ = f32[24,32,256]{2,1,0:T(8,128)S(1)} collective-permute-done((f32[24,32,256]{2,1,0:T(8,128)}, f32[24,32,256]{2,1,0:T(8,128)S(1)}, u32[]{:S(2)}, u32[]{:S(2)}) %collective-permute-start.6) | collective-permute-done | bytes 786464 | tf_op jit(solution)/shard_map/ppermute | solution.py:300
  346.2 1.1 finish.1
  (29 shorter events, 4.0 us)
Async XLA Ops:
  7.2 92.2 %all-gather.11.cloned.1.call-start = ((), (), s32[]{:S(2)}) async-start(), calls=%async_computation.3 | async-start | bytes 3342336 | tf_op jit(solution)/shard_map/all_gather | solution.py:295
  10.6 1.7 copy-start
  22.2 1.9 copy-start.1
  36.2 105.6 %all-gather.9.cloned.1.call-start = ((), (), s32[]{:S(2)}) async-start(), calls=%async_computation.2 | async-start | bytes 3342336 | tf_op jit(solution)/shard_map/all_gather | solution.py:295
  36.2 2.1 copy-start.2
  50.4 145.5 %all-gather.5.cloned.1.call-start = ((), (), s32[]{:S(2)}) async-start(), calls=%async_computation | async-start | bytes 3342336 | tf_op jit(solution)/shard_map/all_gather | solution.py:295
  50.4 2.1 copy-start.3
  64.6 184.7 %all-gather.7.cloned.1.call-start = ((), (), s32[]{:S(2)}) async-start(), calls=%async_computation.1 | async-start | bytes 3342336 | tf_op jit(solution)/shard_map/all_gather | solution.py:295
  64.7 2.1 copy-start.4
  66.8 182.5 %copy-start.5 = (s32[136]{0:T(256)S(1)}, s32[136]{0:T(256)}, u32[]{:S(2)}) copy-start(s32[136]{0:T(256)} %owner_ref.1) | copy-start | bytes 1636
  262.4 20.4 %collective-permute-start = (f32[24,32,256]{2,1,0:T(8,128)S(1)}, f32[24,32,256]{2,1,0:T(8,128)S(1)}, u32[]{:S(2)}, u32[]{:S(2)}) collective-permute-start(f32[24,32,256]{2,1,0:T(8,128)S(1)} %get-tuple-element.21), channel_id=1, source_target_pairs={{0,16},{16,0},{32,48},{48,32},{64,80},{80,64},{96,112},{112,96},{1... | collective-permute-start | bytes 2359304 | tf_op jit(solution)/shard_map/ppermute | solution.py:300
  263.1 70.0 %collective-permute-start.1 = (f32[24,32,256]{2,1,0:T(8,128)S(1)}, f32[24,32,256]{2,1,0:T(8,128)S(1)}, u32[]{:S(2)}, u32[]{:S(2)}) collective-permute-start(f32[24,32,256]{2,1,0:T(8,128)S(1)} %get-tuple-element.22), channel_id=1, source_target_pairs={{0,32},{16,48},{32,64},{48,80},{64,96},{80,112},{96,0},{112,16},{1... | collective-permute-start | bytes 2359304 | tf_op jit(solution)/shard_map/ppermute | solution.py:300
  264.4 68.7 %collective-permute-start.2 = (f32[24,32,256]{2,1,0:T(8,128)S(1)}, f32[24,32,256]{2,1,0:T(8,128)S(1)}, u32[]{:S(2)}, u32[]{:S(2)}) collective-permute-start(f32[24,32,256]{2,1,0:T(8,128)S(1)} %get-tuple-element.23), channel_id=1, source_target_pairs={{0,48},{16,32},{32,80},{48,64},{64,112},{80,96},{96,16},{112,0},{1... | collective-permute-start | bytes 2359304 | tf_op jit(solution)/shard_map/ppermute | solution.py:300
  265.5 67.6 %collective-permute-start.3 = (f32[24,32,256]{2,1,0:T(8,128)}, f32[24,32,256]{2,1,0:T(8,128)S(1)}, u32[]{:S(2)}, u32[]{:S(2)}) collective-permute-start(f32[24,32,256]{2,1,0:T(8,128)} %get-tuple-element.24), channel_id=1, source_target_pairs={{0,64},{16,80},{32,96},{48,112},{64,0},{80,16},{96,32},{112,48},{1... | collective-permute-start | bytes 2359304 | tf_op jit(solution)/shard_map/ppermute | solution.py:300
  267.4 65.6 %collective-permute-start.4 = (f32[24,32,256]{2,1,0:T(8,128)}, f32[24,32,256]{2,1,0:T(8,128)S(1)}, u32[]{:S(2)}, u32[]{:S(2)}) collective-permute-start(f32[24,32,256]{2,1,0:T(8,128)} %get-tuple-element.25), channel_id=1, source_target_pairs={{0,80},{16,64},{32,112},{48,96},{64,16},{80,0},{96,48},{112,32},{1... | collective-permute-start | bytes 2359304 | tf_op jit(solution)/shard_map/ppermute | solution.py:300
  282.9 50.2 %collective-permute-start.5 = (f32[24,32,256]{2,1,0:T(8,128)}, f32[24,32,256]{2,1,0:T(8,128)S(1)}, u32[]{:S(2)}, u32[]{:S(2)}) collective-permute-start(f32[24,32,256]{2,1,0:T(8,128)} %get-tuple-element.26), channel_id=1, source_target_pairs={{0,96},{16,112},{32,0},{48,16},{64,32},{80,48},{96,64},{112,80},{1... | collective-permute-start | bytes 2359304 | tf_op jit(solution)/shard_map/ppermute | solution.py:300
  333.1 13.1 %collective-permute-start.6 = (f32[24,32,256]{2,1,0:T(8,128)}, f32[24,32,256]{2,1,0:T(8,128)S(1)}, u32[]{:S(2)}, u32[]{:S(2)}) collective-permute-start(f32[24,32,256]{2,1,0:T(8,128)} %get-tuple-element.27), channel_id=1, source_target_pairs={{0,112},{16,96},{32,16},{48,0},{64,48},{80,32},{96,80},{112,64},{1... | collective-permute-start | bytes 2359304 | tf_op jit(solution)/shard_map/ppermute | solution.py:300
Sparse Core Ops, SparseCore 0:
  36.3 51.8 all-gather.10
  90.6 51.1 all-gather.8
  144.8 51.0 all-gather.4
  198.2 51.0 all-gather.6

commit v2 on v1

--- a/solution.py
+++ b/solution.py
@@ -90,34 +90,34 @@
     )(row_list.reshape(ROWS, 1), jnp.pad(labels, (0, 32)).reshape(1, 128), images, flat)
 
 
-def conv_kernel(nblk_ref, win_ref, w_ref, sel_ref, bias_ref, out_ref, uniq_ref):
-    bias = bias_ref[...]
-    floor = jnp.broadcast_to(-bias, (16, 256))
+def conv_kernel(nblk_ref, win_ref, w_ref, sel_ref, bias_ref, lab_ref, *refs):
+    out_ref, uniq_ref = refs[-2:]
+    count = w_ref.shape[0]
     uniq_ref[...] = jnp.zeros_like(uniq_ref)
-
+    if out_ref.shape[1] > count * 1024:
+        out_ref[:, count * 1024:] = lab_ref[...]
     steps = []
-    for dd in range(6):
+    for d in range(6):
         for w in range(15):
-            top = w <= (7 if dd < 3 else 6)
-            steps.append((dd, w, 0 if top else 1))
-
-    def block(b, acc):
+            steps.append((d, w, 0 if w <= (7 if d < 3 else 6) else 1))
+
+    def block(nc, b, bias, floor, acc):
         total = [[jnp.zeros((16, 256), F32) for _ in range(2)] for _ in range(2)]
 
         def take(k):
-            dd, w, qr = steps[k]
+            qr = steps[k][2]
             for m in range(2):
                 got = pltpu.matmul_pop(acc[m][k % 8]).reshape(5, 16, 256)
                 total[qr][m] = total[qr][m] + jnp.sum(jnp.maximum(got, floor[None]), axis=0)
 
-        for k, (dd, w, qr) in enumerate(steps):
+        for k, (d, w, _) in enumerate(steps):
             if w == 0:
                 for m in range(2):
-                    pltpu.matmul_push_rhs(w_ref[dd * 256:(dd + 1) * 256, :], dd % 2, m)
+                    pltpu.matmul_push_rhs(w_ref[nc, d * 256:(d + 1) * 256, :], d % 2, m)
             for m in range(2):
-                lhs = jnp.concatenate(
-                    [win_ref[w, b, m * 80:(m + 1) * 80, :], win_ref[w + 1, b, m * 80:(m + 1) * 80, :]], axis=1)
-                pltpu.matmul_acc_lhs(acc[m][k % 8], lhs, load_staged_rhs=dd % 2 if w == 0 else None)
+                rows = slice(m * 80, (m + 1) * 80)
+                lhs = jnp.concatenate([win_ref[w, b, rows, :], win_ref[w + 1, b, rows, :]], axis=1)
+                pltpu.matmul_acc_lhs(acc[m][k % 8], lhs, load_staged_rhs=d % 2 if w == 0 else None)
             if k >= LAG:
                 take(k - LAG)
         for k in range(len(steps) - LAG, len(steps)):
@@ -130,17 +130,23 @@
                 uniq_ref[pl.ds(at, 16), q * 256:(q + 1) * 256] = mean.astype(BF)
 
     def scoped(*accs):
-        @pl.loop(0, nblk_ref[0, 0])
-        def _(b):
-            block(b, (accs[:8], accs[8:16]))
-
-        for m in range(2):
-            for qr in range(2):
-                q = 2 * qr + m
-                pltpu.matmul_push_rhs(uniq_ref[:, q * 256:(q + 1) * 256], qr, m)
-                pltpu.matmul_acc_lhs(accs[16 + q], sel_ref[...], load_staged_rhs=qr)
-        for q in range(4):
-            out_ref[:, q * 256:(q + 1) * 256] = pltpu.matmul_pop(accs[16 + q]).astype(BF)
+        @pl.loop(0, count)
+        def _(nc):
+            bias = bias_ref[nc]
+            floor = jnp.broadcast_to(-bias, (16, 256))
+
+            @pl.loop(0, nblk_ref[0, 0])
+            def _(b):
+                block(nc, b, bias, floor, (accs[:8], accs[8:16]))
+
+            for m in range(2):
+                for qr in range(2):
+                    q = 2 * qr + m
+                    pltpu.matmul_push_rhs(uniq_ref[:, q * 256:(q + 1) * 256], qr, m)
+                    pltpu.matmul_acc_lhs(accs[16 + q], sel_ref[...], load_staged_rhs=qr)
+            for q in range(4):
+                at = pl.multiple_of(nc * 1024 + q * 256, 256)
+                out_ref[:, pl.ds(at, 256)] = pltpu.matmul_pop(accs[16 + q]).astype(BF)
 
     pl.run_scoped(
         scoped,
@@ -149,17 +155,19 @@
     )
 
 
-def conv(nblk, win, w, sel, bias):
+def conv(nblk, win, w, sel, bias, lab, extra, after=()):
+    count = w.shape[0]
     return pl.pallas_call(
         conv_kernel,
-        out_shape=jax.ShapeDtypeStruct((ROWS, 1024), BF),
-        in_specs=[pl.BlockSpec(memory_space=pltpu.SMEM)] + [pl.BlockSpec(memory_space=pltpu.VMEM)] * 4,
+        out_shape=jax.ShapeDtypeStruct((ROWS, count * 1024 + extra), BF),
+        in_specs=[pl.BlockSpec(memory_space=pltpu.SMEM)] + [pl.BlockSpec(memory_space=pltpu.VMEM)] * 5
+        + [pl.BlockSpec(memory_space=pl.ANY)] * len(after),
         out_specs=pl.BlockSpec(memory_space=pltpu.VMEM),
         scratch_shapes=[pltpu.VMEM((256, 1024), BF)],
         compiler_params=pltpu.CompilerParams(vmem_limit_bytes=40 * 2**20),
-        cost_estimate=pl.CostEstimate(flops=2 * 86400 * 256 * 256, bytes_accessed=8 * 2**20, transcendentals=0),
+        cost_estimate=pl.CostEstimate(flops=count * 2 * 86400 * 256 * 256, bytes_accessed=8 * 2**20, transcendentals=0),
         name="conv",
-    )(nblk, win, w, sel, bias)
+    )(nblk, win, w, sel, bias, lab, *after)
 
 
 TILES = 16
@@ -171,17 +179,32 @@
 FEAT = 8
 
 
+BLOCKS = ((0, 96), (96, 96), (192, 96), (288, 96), (384, 96), (480, 96), (576, 96), (672, 96), (768, 384), (1152, 288), (1440, 96))
+
+
 def gram_kernel(me_ref, owner_ref, *refs):
-    chunks, lab, outs = refs[:4], refs[4], refs[5:5 + FEAT]
-    f_ref, ft_ref, target_ref, left_ref, prod_ref, list_i, list_j, sem = refs[5 + FEAT:]
+    n = len(BLOCKS)
+    parts, (out_ref, peak_ref) = (refs[:n], refs[n:2 * n]), refs[2 * n:2 * n + 2]
+    f_ref, ft_ref, lab, target_ref, left_ref, list_i, list_j, sem = refs[2 * n + 2:]
     me_tile = me_ref[0]
-    me_feat = me_ref[1]
-    copies = []
-    for nc in range(4):
-        for q in range(4):
-            copy = pltpu.make_async_copy(chunks[nc].at[:, q * 256:(q + 1) * 256], f_ref.at[q * 4 + nc], sem.at[q * 4 + nc])
+    peak_ref[...] = jnp.zeros_like(peak_ref)
+    copies = {}
+    for part in range(2):
+        for local in range(2):
+            for q in range(4):
+                tile = q * 4 + part * 2 + local
+                cols = slice(local * 1024 + q * 256, local * 1024 + (q + 1) * 256)
+                copies[tile] = [
+                    pltpu.make_async_copy(ref.at[:, cols], f_ref.at[tile, start:start + size], sem.at[tile])
+                    for ref, (start, size) in zip(parts[part], BLOCKS)
+                ]
+    copies[TILES] = [
+        pltpu.make_async_copy(ref.at[:, 2048:], lab.at[start:start + size], sem.at[TILES])
+        for ref, (start, size) in zip(parts[0], BLOCKS)
+    ]
+    for group in copies.values():
+        for copy in group:
             copy.start()
-            copies.append((q * 4 + nc, copy))
 
     def scan(k, carry):
         i, j, n = carry
@@ -198,21 +221,22 @@
 
     _, _, owned = lax.fori_loop(0, NTILES, scan, (jnp.int32(0), jnp.int32(0), jnp.int32(0)))
 
+    for copy in copies[TILES]:
+        copy.wait()
     labels = lab[...].astype(F32)
     label = (labels[:, 0:1] * 8.0 + labels[:, 1:2]).astype(jnp.int32)
     for s in range(4):
         classes = lax.broadcasted_iota(jnp.int32, (GROUP, 256), 1) + 256 * s
         target_ref[:, s * 256:(s + 1) * 256] = jnp.where(label == classes, 1.0, -1.0).astype(BF)
-    for t, copy in copies:
-        copy.wait()
+    for t in range(TILES):
+        for copy in copies[t]:
+            copy.wait()
         ft_ref[t] = f_ref[t].T
 
     def put(slot, product):
-        prod_ref[...] = product
+        peak_ref[...] = jnp.maximum(peak_ref[...], jnp.max(jnp.abs(product).reshape(32, 8, 256), axis=0))
         for k in range(FEAT):
-            dz, dy = k // 2, k % 2
-            peer = (me_feat // 2 + dz) % 4 * 2 + (me_feat % 2 + dy) % 2
-            outs[k][slot] = prod_ref[pl.ds(pl.multiple_of(peer * 32, 32), 32), :]
+            out_ref[k, slot] = product[k * 32:(k + 1) * 32, :]
 
     @pl.loop(0, owned)
     def _(slot):
@@ -221,7 +245,7 @@
     @pl.loop(owned, OWNED)
     def _(slot):
         for k in range(FEAT):
-            outs[k][slot] = jnp.zeros((32, 256), F32)
+            out_ref[k, slot] = jnp.zeros((32, 256), F32)
 
     start = pl.multiple_of(me_tile % 8 * 32, 32)
     for f in range(FEAT):
@@ -231,74 +255,109 @@
         put(OWNED + s, dot(left_ref[...], target_ref[:, s * 256:(s + 1) * 256]))
 
 
-def gram(me, tile_owner, chunks, lab):
+def gram(me, tile_owner, parts):
     smem = pl.BlockSpec(memory_space=pltpu.SMEM)
     vmem = pl.BlockSpec(memory_space=pltpu.VMEM)
     return pl.pallas_call(
         gram_kernel,
-        out_shape=tuple(jax.ShapeDtypeStruct((SLOTS, 32, 256), F32) for _ in range(FEAT)),
-        in_specs=[smem, smem] + [pl.BlockSpec(memory_space=pl.ANY)] * 4 + [vmem],
-        out_specs=tuple(vmem for _ in range(FEAT)),
+        out_shape=(jax.ShapeDtypeStruct((FEAT, SLOTS, 32, 256), F32), jax.ShapeDtypeStruct((8, 256), F32)),
+        in_specs=[smem, smem] + [pl.BlockSpec(memory_space=pl.ANY)] * (2 * len(BLOCKS)),
+        out_specs=(vmem, vmem),
         scratch_shapes=[
             pltpu.VMEM((TILES, GROUP, 256), BF),
             pltpu.VMEM((TILES, 256, GROUP), BF),
+            pltpu.VMEM((GROUP, 128), BF),
             pltpu.VMEM((GROUP, 1024), BF),
             pltpu.VMEM((256, GROUP), BF),
-            pltpu.VMEM((256, 256), F32),
             pltpu.SMEM((OWNED,), jnp.int32),
             pltpu.SMEM((OWNED,), jnp.int32),
-            pltpu.SemaphoreType.DMA((TILES,)),
+            pltpu.SemaphoreType.DMA((TILES + 1,)),
         ],
         compiler_params=pltpu.CompilerParams(vmem_limit_bytes=50 * 2**20),
         cost_estimate=pl.CostEstimate(flops=5 * 10**9, bytes_accessed=20 * 2**20, transcendentals=0),
         name="gram",
-    )(me, tile_owner, *chunks, lab)
-
-
-def finish_kernel(*refs):
-    parts, gram_ref, cross_ref = refs[:FEAT], refs[FEAT], refs[FEAT + 1]
-    scale = 1.0 / 12288.0
-    for s in range(SLOTS):
-        total = parts[0][s]
-        for k in range(1, FEAT):
-            total = total + parts[k][s]
-        total = total * scale
-        if s < OWNED:
-            gram_ref[s] = total
-        else:
-            width = min(256, CLASSES - (s - OWNED) * 256)
-            cross_ref[:, (s - OWNED) * 256:(s - OWNED) * 256 + width] = total[:, :width]
-
-
-def finish(parts):
-    return pl.pallas_call(
-        finish_kernel,
-        out_shape=(jax.ShapeDtypeStruct((OWNED, 32, 256), F32), jax.ShapeDtypeStruct((32, CLASSES), F32)),
-        in_specs=[pl.BlockSpec(memory_space=pltpu.VMEM)] * FEAT,
-        out_specs=(pl.BlockSpec(memory_space=pltpu.VMEM),) * 2,
-        compiler_params=pltpu.CompilerParams(vmem_limit_bytes=40 * 2**20),
-        name="finish",
-    )(*parts)
-
-
-def feat_shift(dz, dy):
-    return [(z * 2 + y, (z + dz) % 4 * 2 + (y + dy) % 2) for z in range(4) for y in range(2)]
+    )(me, tile_owner, *parts[0], *parts[1])
+
+
+HALF = jnp.float16
+
+
+def exchange(partial, peak):
+    exponent = jnp.floor(jnp.log2(jnp.maximum(jnp.max(peak), 1e-30)))
+    coded = (partial * jnp.exp2(13.0 - exponent)).astype(HALF)
+    note = jnp.broadcast_to(exponent.astype(HALF), (FEAT, 1, 32, 256))
+    got = lax.all_to_all(jnp.concatenate([coded, note], axis=1), "feat", split_axis=0, concat_axis=0, tiled=True)
+    back = jnp.exp2(got[:, SLOTS:, :1, :1].astype(F32) - 13.0) * (1.0 / 12288.0)
+    total = jnp.sum(got[:, :SLOTS].astype(F32) * back, axis=0)
+    return total
+
+
+def finish(total):
+    cross = total[OWNED:].transpose(1, 0, 2).reshape(32, 1024)[:, :CLASSES]
+    return total[:OWNED], cross
+
+
+def hop(dy=0, dx=0, core=0):
+    def index(y, x, c):
+        return (y % 2 * 4 + x % 4) * 2 + c % 2
+
+    return [(index(y, x, c), index(y + dy, x + dx, c + core)) for y in range(2) for x in range(4) for c in range(2)]
+
+
+def onward():
+    return [(s, d) if s % 2 == 0 else (s, e) for (s, d), (_, e) in zip(hop(dx=1), hop(dx=-1))]
+
+
+def send(block, perm):
+    return lax.ppermute(block, "tile", perm)
+
+
+def spread_first(own):
+    left = send(own, hop(dx=1))
+    right = send(own, hop(dx=-1))
+    over = send(own, hop(dy=1))
+    return own, over, left, right
+
+
+def spread_second(first):
+    own, over, left, right = first
+    even = lax.axis_index("tile") % 2 == 0
+    far = send(jnp.where(even, left, right), onward())
+    over_left = send(over, hop(dx=1))
+    over_right = send(over, hop(dx=-1))
+    swap_a = send(jnp.concatenate([own, over, left, right], axis=0), hop(core=1))
+    return far, over_left, over_right, swap_a
+
+
+def spread_third(first, second):
+    own, over, left, right = first
+    far, over_left, over_right, swap_a = second
+    even = lax.axis_index("tile") % 2 == 0
+    over_far = send(jnp.where(even, over_left, over_right), onward())
+    swap_b = send(jnp.concatenate([over_left, over_right, far], axis=0), hop(core=1))
+    swap_c = send(over_far, hop(core=1))
+    return [own, over, left, right, over_left, over_right, far, over_far, swap_a, swap_b, swap_c]
 
 
 def body(images, row_list, labels, filters, bias, tile_owner):
     flat = jnp.pad(filters.reshape(108, 1024), ((0, 20), (0, 0)))
     win, w, sel, lab, nblk = prep(images, row_list, labels, flat)
-    labs = lax.all_gather(lab, "tile", axis=0, tiled=True)
-    chunks = []
-    for nc in range(4):
-        own = conv(nblk, win, w[nc], sel, bias[nc * 256:(nc + 1) * 256].reshape(1, 256))
-        chunks.append(lax.all_gather(own, "tile", axis=0, tiled=True))
+    bias4 = bias.reshape(4, 1, 256)
+    own_a = conv(nblk, win, w[0:2], sel, bias4[0:2], lab, 128)
+    first_a = spread_first(own_a)
+    own_b2 = conv(nblk, win, w[2:3], sel, bias4[2:3], lab, 0, (own_a,))
+    second_a = spread_second(first_a)
+    own_b3 = conv(nblk, win, w[3:4], sel, bias4[3:4], lab, 0, first_a[1:])
+    own_b = jnp.concatenate([own_b2, own_b3], axis=1)
+    own_b, far, over_left, over_right = lax.optimization_barrier((own_b,) + second_a[:3])
+    second_a = (far, over_left, over_right, second_a[3])
+    first_b = spread_first(own_b)
+    part_a = spread_third(first_a, second_a)
+    second_b = spread_second(first_b)
+    part_b = spread_third(first_b, second_b)
     me = jnp.stack([lax.axis_index("tile"), lax.axis_index("feat")]).astype(jnp.int32)
-    partial = gram(me, tile_owner, chunks, labs)
-    parts = [partial[0]]
-    for k in range(1, FEAT):
-        parts.append(lax.ppermute(partial[k], "feat", feat_shift(k // 2, k % 2)))
-    return finish(parts)
+    partial, peak = gram(me, tile_owner, (part_a, part_b))
+    return finish(exchange(partial, peak))
 
 
 def solution(mesh):

time: 356 us -> 186 us (0.52)
  the two profiles are of different devices: /device:TPU:64 before, /device:TPU:0 now
where the time goes in v2:
time: 186 us; the launch traced here: 183 us
  Pallas kernels  63.1 us (34%)
  blocking collectives  44.6 us (24%)
  waiting for transfers between devices  33.3 us (18%)
  starting transfers between devices  22.3 us (12%)
  other arithmetic  10.6 us (6%)
  local copies, waits for them, and re-layouts  7.81 us (4%)
    all_to_all x1, blocking collectives, exchange(): lax.all_to_all(jnp.concatenate([coded, note], axis=1), 'feat', split_axis...  44.6 us
    pallas_call x3, Pallas kernels, conv(): pl.pallas_call(conv_kernel, out_shape=jax.ShapeDtypeStruct((ROWS, count *...  36.6 us
    ppermute x20, waiting for transfers between devices, send(): return lax.ppermute(block, 'tile', perm)  33.3 us
    ppermute x20, starting transfers between devices, send(): return lax.ppermute(block, 'tile', perm)  22.3 us
    pallas_call x1, Pallas kernels, gram(): pl.pallas_call(gram_kernel, out_shape=(jax.ShapeDtypeStruct((FEAT, SLOTS,...  16.5 us
    pallas_call x1, Pallas kernels, prep(): pl.pallas_call(prep_kernel, out_shape=(jax.ShapeDtypeStruct((16, NBLK, 16...  9.93 us
    convert_element_type x1, other arithmetic, exchange(): coded = (partial * jnp.exp2(13.0 - exponent)).astype(HALF)  3.76 us
  transfers between devices with their start and end apart: 20, of which 10 were waited for; matrix products, arithmetic and copies ran while one was open for 3% of the time, Pallas kernels for 10%

profile of v2, /device:TPU:0, one launch (start us, length us, event | category | flops | bytes accessed | tf_op | source)
XLA Modules:
  0.0 183.5 jit_solution(4673169276328268959)
XLA Ops:
  3.9 1.7 copy-done
  5.6 9.9 %prep.1 = (bf16[16,6,160,128]{3,2,1,0:T(8,128)(2,1)S(1)}, bf16[4,1536,256]{2,1,0:T(8,128)(2,1)S(1)}, bf16[96,256]{1,0:T(8,128)(2,1)S(1)}, bf16[96,128]{1,0:T(8,128)(2,1)S(1)}, s32[1,1]{1,0:T(1,128)}) custom-call(s32[96,1]{1,0:T(8,128)S(1)} %copy.12.rows_ref, s32[1,128]{1,0:T(1,128)S(1)} %pad_bitcast_fusion.labels_ref, bf16[96,12288]{1,0:T(8,128)(2,1)S(1)} %copy-done, ...), custom_call_target="tpu_custom_call" | custom-call | tf_op jit(solution)/shard_map/prep/pallas_call | solution.py:71
  15.6 18.0 %conv.3.refs_0_ = bf16[96,2176]{1,0:T(8,128)(2,1)S(1)} custom-call(s32[1,1]{1,0:T(1,128)} %get-tuple-element.13.nblk_ref, bf16[16,6,160,128]{3,2,1,0:T(8,128)(2,1)S(1)} %get-tuple-element.14.win_ref, bf16[2,1536,256]{2,1,0:T(8,128)(2,1)S(1)} %slice.50.w_ref, bf16[96,256]{1,0:T(8,128)(2,1)S(1)} %get-tuple-element.16.sel_ref, f32[2,1,256]{2,1,0:T(1,128)S(1)} %bitcast.13, ...), custom_call_target="tpu_custom_call" | custom-call | flops 22649241600 | bytes 8388608 | tf_op jit(solution)/shard_map/conv/pallas_call | solution.py:160
  33.6 2.9 %collective-permute-start.2 = (bf16[96,2176]{1,0:T(8,128)(2,1)S(1)}, bf16[96,2176]{1,0:T(8,128)(2,1)S(1)}, u32[]{:S(2)}, u32[]{:S(2)}) collective-permute-start(bf16[96,2176]{1,0:T(8,128)(2,1)S(1)} %conv.3.refs_0_), channel_id=1, source_target_pairs={{0,6},{1,7},{2,0},{3,1},{4,2},{5,3},{6,4},{7,5},{8,14},{9,15},{10,... | collective-permute-start | bytes 1253384 | tf_op jit(solution)/shard_map/ppermute | solution.py:312
  36.5 7.4 %collective-permute-start = (bf16[96,2176]{1,0:T(8,128)(2,1)S(1)}, bf16[96,2176]{1,0:T(8,128)(2,1)S(1)}, u32[]{:S(2)}, u32[]{:S(2)}) collective-permute-start(bf16[96,2176]{1,0:T(8,128)(2,1)S(1)} %conv.3.refs_0_), channel_id=1, source_target_pairs={{0,8},{1,9},{2,10},{3,11},{4,12},{5,13},{6,14},{7,15},{8,0},{9,1},... | collective-permute-start | bytes 1253384 | tf_op jit(solution)/shard_map/ppermute | solution.py:312
  44.0 9.3 %conv.4 = bf16[96,1024]{1,0:T(8,128)(2,1)S(1)} custom-call(s32[1,1]{1,0:T(1,128)} %get-tuple-element.13.nblk_ref, bf16[16,6,160,128]{3,2,1,0:T(8,128)(2,1)S(1)} %get-tuple-element.14.win_ref, bf16[1,1536,256]{2,1,0:T(8,128)(2,1)S(1)} %get-tuple-element.24.w_ref, bf16[96,256]{1,0:T(8,128)(2,1)S(1)} %get-tuple-element.16.sel_ref, f32[1,1,256]{2,1,0:T(1,128)S(1)} %bitcast.15, ...), custom_call_target="tpu_custom_call" | custom-call | flops 11324620800 | bytes 8388608 | tf_op jit(solution)/shard_map/conv/pallas_call | solution.py:160
  53.5 1.3 pad_maximum_fusion
  54.8 3.2 %collective-permute-start.5 = (bf16[96,2176]{1,0:T(8,128)(2,1)S(1)}, bf16[96,2176]{1,0:T(8,128)(2,1)S(1)}, u32[]{:S(2)}, u32[]{:S(2)}) collective-permute-start(bf16[96,2176]{1,0:T(8,128)(2,1)S(1)} %collective-permute-done.refs_0_.refs_1_), channel_id=1, source_target_pairs={{0,6},{1,7},{2,0},{3,1},{4,2},{5,3},{6,4},{7,5},{8,14},{9,15},{10,... | collective-permute-start | bytes 1253384 | tf_op jit(solution)/shard_map/ppermute | solution.py:312
  58.1 9.4 %conv.5 = bf16[96,1024]{1,0:T(8,128)(2,1)S(1)} custom-call(s32[1,1]{1,0:T(1,128)} %get-tuple-element.13.nblk_ref, bf16[16,6,160,128]{3,2,1,0:T(8,128)(2,1)S(1)} %copy-done.5, bf16[1,1536,256]{2,1,0:T(8,128)(2,1)S(1)} %get-tuple-element.25.w_ref, bf16[96,256]{1,0:T(8,128)(2,1)S(1)} %get-tuple-element.16.sel_ref, f32[1,1,256]{2,1,0:T(1,128)S(1)} %bitcast.14, ...), custom_call_target="tpu_custom_call" | custom-call | flops 11324620800 | bytes 8388608 | tf_op jit(solution)/shard_map/conv/pallas_call | solution.py:160
  67.6 4.1 %collective-permute-done.4.refs_4_ = bf16[96,2176]{1,0:T(8,128)(2,1)S(1)} collective-permute-done((bf16[96,2176]{1,0:T(8,128)(2,1)S(1)}, bf16[96,2176]{1,0:T(8,128)(2,1)S(1)}, u32[]{:S(2)}, u32[]{:S(2)}) %collective-permute-start.4) | collective-permute-done | bytes 417824 | tf_op jit(solution)/shard_map/ppermute | solution.py:312
  71.7 2.0 %collective-permute-start.12 = (bf16[96,2048]{1,0:T(8,128)(2,1)S(1)}, bf16[96,2048]{1,0:T(8,128)(2,1)S(1)}, u32[]{:S(2)}, u32[]{:S(2)}) collective-permute-start(bf16[96,2048]{1,0:T(8,128)(2,1)S(1)} %pad_maximum_fusion.4.refs_11_), channel_id=1, source_target_pairs={{0,6},{1,7},{2,0},{3,1},{4,2},{5,3},{6,4},{7,5},{8,14},{9,15},{10,... | collective-permute-start | bytes 1179656 | tf_op jit(solution)/shard_map/ppermute | solution.py:312
  73.7 2.1 %collective-permute-start.10 = (bf16[96,2048]{1,0:T(8,128)(2,1)S(1)}, bf16[96,2048]{1,0:T(8,128)(2,1)S(1)}, u32[]{:S(2)}, u32[]{:S(2)}) collective-permute-start(bf16[96,2048]{1,0:T(8,128)(2,1)S(1)} %pad_maximum_fusion.4.refs_11_), channel_id=1, source_target_pairs={{0,8},{1,9},{2,10},{3,11},{4,12},{5,13},{6,14},{7,15},{8,0},{9,1},... | collective-permute-start | bytes 1179656 | tf_op jit(solution)/shard_map/ppermute | solution.py:312
  76.0 7.8 %collective-permute-done.12.refs_14_ = bf16[96,2048]{1,0:T(8,128)(2,1)S(1)} collective-permute-done((bf16[96,2048]{1,0:T(8,128)(2,1)S(1)}, bf16[96,2048]{1,0:T(8,128)(2,1)S(1)}, u32[]{:S(2)}, u32[]{:S(2)}) %collective-permute-start.12) | collective-permute-done | bytes 393248 | tf_op jit(solution)/shard_map/ppermute | solution.py:312
  85.2 2.1 %collective-permute-start.14 = (bf16[96,2048]{1,0:T(8,128)(2,1)S(1)}, bf16[96,2048]{1,0:T(8,128)(2,1)S(1)}, u32[]{:S(2)}, u32[]{:S(2)}) collective-permute-start(bf16[96,2048]{1,0:T(8,128)(2,1)S(1)} %collective-permute-done.10.refs_12_), channel_id=1, source_target_pairs={{0,6},{1,7},{2,0},{3,1},{4,2},{5,3},{6,4},{7,5},{8,14},{9,15},{10,... | collective-permute-start | bytes 1179656 | tf_op jit(solution)/shard_map/ppermute | solution.py:312
  87.3 1.3 pad_maximum_fusion.1
  89.3 1.2 pad_maximum_fusion.2
  90.4 6.4 %collective-permute-done.15.refs_17_ = bf16[96,2048]{1,0:T(8,128)(2,1)S(1)} collective-permute-done((bf16[96,2048]{1,0:T(8,128)(2,1)S(1)}, bf16[96,2048]{1,0:T(8,128)(2,1)S(1)}, u32[]{:S(2)}, u32[]{:S(2)}) %collective-permute-start.15) | collective-permute-done | bytes 393248 | tf_op jit(solution)/shard_map/ppermute | solution.py:312
  97.3 2.2 %collective-permute-start.9 = (bf16[96,2176]{1,0:T(8,128)(2,1)S(1)}, bf16[96,2176]{1,0:T(8,128)(2,1)S(1)}, u32[]{:S(2)}, u32[]{:S(2)}) collective-permute-start(bf16[96,2176]{1,0:T(8,128)(2,1)S(1)} %collective-permute-done.6.refs_7_), channel_id=1, source_target_pairs={{0,1},{1,0},{2,3},{3,2},{4,5},{5,4},{6,7},{7,6},{8,9},{9,8},{10,11... | collective-permute-start | bytes 1253384 | tf_op jit(solution)/shard_map/ppermute | solution.py:312
  99.5 1.6 collective-permute-done.13.refs_15_
  102.4 9.1 %collective-permute-done.16.refs_18_ = bf16[96,2048]{1,0:T(8,128)(2,1)} collective-permute-done((bf16[96,2048]{1,0:T(8,128)(2,1)S(1)}, bf16[96,2048]{1,0:T(8,128)(2,1)}, u32[]{:S(2)}, u32[]{:S(2)}) %collective-permute-start.16) | collective-permute-done | bytes 393248 | tf_op jit(solution)/shard_map/ppermute | solution.py:312
  111.5 2.0 %collective-permute-done.19.refs_21_ = bf16[96,2048]{1,0:T(8,128)(2,1)} collective-permute-done((bf16[96,2048]{1,0:T(8,128)(2,1)}, bf16[96,2048]{1,0:T(8,128)(2,1)}, u32[]{:S(2)}, u32[]{:S(2)}) %collective-permute-start.19) | collective-permute-done | bytes 393248 | tf_op jit(solution)/shard_map/ppermute | solution.py:312
  113.5 16.5 %gram.1 = (f32[8,24,32,256]{3,2,1,0:T(8,128)}, f32[8,256]{1,0:T(8,128)S(1)}) custom-call(s32[2]{0:T(128)S(1)} %pad_add_fusion.me_ref, s32[136]{0:T(256)S(1)} %copy-done.6, bf16[96,2176]{1,0:T(8,128)(2,1)S(1)} %conv.3.refs_0_, bf16[96,2176]{1,0:T(8,128)(2,1)} %copy-done.3, bf16[96,2176]{1,0:T(8,128)(2,1)} %copy-done.2, bf16[96,2176]{1,0:T(8,128)(2,1)} %copy-done.1, ...), custom_call_target="tpu_custom_call" | custom-call | flops 5000000000 | bytes 20971520 | tf_op jit(solution)/shard_map/gram/pallas_call | solution.py:261
  131.4 3.8 %multiply_convert_fusion = f16[8,24,32,256]{3,2,1,0:T(8,128)(2,1)S(1)} fusion(f32[8,24,32,256]{3,2,1,0:T(8,128)} %get-tuple-element.22, f32[]{:T(128)S(6)} %exp2.13), kind=kLoop, calls=%fused_computation.1 | loop fusion | flops 3145728 | bytes 9437188 | tf_op jit(solution)/shard_map/convert_element_type | solution.py:287
  136.2 44.6 %all_to_all.5 = f16[8,25,32,256]{3,2,1,0:T(8,128)(2,1)S(1)} all-to-all(f16[8,25,32,256]{3,2,1,0:T(8,128)(2,1)S(1)} %concatenate.23), channel_id=1, replica_groups=mesh['feat'=8,'tile'=16] {'feat'}, dimensions={0} | all-to-all | bytes 6553600 | tf_op jit(solution)/shard_map/all_to_all | solution.py:289
  (74 shorter events, 12.0 us)
Async XLA Ops:
  15.5 28.5 %copy-start.4 = (bf16[16,6,160,128]{3,2,1,0:T(8,128)(2,1)}, bf16[16,6,160,128]{3,2,1,0:T(8,128)(2,1)S(1)}, u32[]{:S(2)}) copy-start(bf16[16,6,160,128]{3,2,1,0:T(8,128)(2,1)S(1)} %get-tuple-element.14.win_ref) | copy-start | bytes 11796484
  15.6 28.3 %copy-start.10 = (f32[1024]{0:T(1024)S(1)}, f32[1024]{0:T(1024)}, u32[]{:S(2)}) copy-start(f32[1024]{0:T(1024)} %param.10) | copy-start | bytes 12292
  33.6 19.7 %collective-permute-start.2 = (bf16[96,2176]{1,0:T(8,128)(2,1)S(1)}, bf16[96,2176]{1,0:T(8,128)(2,1)S(1)}, u32[]{:S(2)}, u32[]{:S(2)}) collective-permute-start(bf16[96,2176]{1,0:T(8,128)(2,1)S(1)} %conv.3.refs_0_), channel_id=1, source_target_pairs={{0,6},{1,7},{2,0},{3,1},{4,2},{5,3},{6,4},{7,5},{8,14},{9,15},{10,... | collective-permute-start | bytes 1253384 | tf_op jit(solution)/shard_map/ppermute | solution.py:312
  36.5 16.8 %collective-permute-start.1 = (bf16[96,2176]{1,0:T(8,128)(2,1)S(1)}, bf16[96,2176]{1,0:T(8,128)(2,1)S(1)}, u32[]{:S(2)}, u32[]{:S(2)}) collective-permute-start(bf16[96,2176]{1,0:T(8,128)(2,1)S(1)} %conv.3.refs_0_), channel_id=1, source_target_pairs={{0,2},{1,3},{2,4},{3,5},{4,6},{5,7},{6,0},{7,1},{8,10},{9,11},{10,... | collective-permute-start | bytes 1253384 | tf_op jit(solution)/shard_map/ppermute | solution.py:312
  36.5 17.0 %collective-permute-start = (bf16[96,2176]{1,0:T(8,128)(2,1)S(1)}, bf16[96,2176]{1,0:T(8,128)(2,1)S(1)}, u32[]{:S(2)}, u32[]{:S(2)}) collective-permute-start(bf16[96,2176]{1,0:T(8,128)(2,1)S(1)} %conv.3.refs_0_), channel_id=1, source_target_pairs={{0,8},{1,9},{2,10},{3,11},{4,12},{5,13},{6,14},{7,15},{8,0},{9,1},... | collective-permute-start | bytes 1253384 | tf_op jit(solution)/shard_map/ppermute | solution.py:312
  53.4 14.1 %collective-permute-start.3 = (bf16[96,2176]{1,0:T(8,128)(2,1)S(1)}, bf16[96,2176]{1,0:T(8,128)(2,1)S(1)}, u32[]{:S(2)}, u32[]{:S(2)}) collective-permute-start(bf16[96,2176]{1,0:T(8,128)(2,1)S(1)} %broadcast_select_fusion.1), channel_id=1, source_target_pairs={{0,2},{1,7},{2,4},{3,1},{4,6},{5,3},{6,0},{7,5},{8,10},{9,15},{10,... | collective-permute-start | bytes 1253384 | tf_op jit(solution)/shard_map/ppermute | solution.py:312
  54.8 56.7 %collective-permute-start.7 = (bf16[384,2176]{1,0:T(8,128)(2,1)}, bf16[384,2176]{1,0:T(8,128)(2,1)}, u32[]{:S(2)}, u32[]{:S(2)}) collective-permute-start(bf16[384,2176]{1,0:T(8,128)(2,1)} %pad_maximum_fusion), channel_id=1, source_target_pairs={{0,1},{1,0},{2,3},{3,2},{4,5},{5,4},{6,7},{7,6},{8,9},{9,8},{10,11... | collective-permute-start | bytes 5013512 | tf_op jit(solution)/shard_map/ppermute | solution.py:312
  54.8 12.8 %collective-permute-start.5 = (bf16[96,2176]{1,0:T(8,128)(2,1)S(1)}, bf16[96,2176]{1,0:T(8,128)(2,1)S(1)}, u32[]{:S(2)}, u32[]{:S(2)}) collective-permute-start(bf16[96,2176]{1,0:T(8,128)(2,1)S(1)} %collective-permute-done.refs_0_.refs_1_), channel_id=1, source_target_pairs={{0,6},{1,7},{2,0},{3,1},{4,2},{5,3},{6,4},{7,5},{8,14},{9,15},{10,... | collective-permute-start | bytes 1253384 | tf_op jit(solution)/shard_map/ppermute | solution.py:312
  58.0 13.6 %collective-permute-start.4 = (bf16[96,2176]{1,0:T(8,128)(2,1)S(1)}, bf16[96,2176]{1,0:T(8,128)(2,1)S(1)}, u32[]{:S(2)}, u32[]{:S(2)}) collective-permute-start(bf16[96,2176]{1,0:T(8,128)(2,1)S(1)} %collective-permute-done.refs_0_.refs_1_), channel_id=1, source_target_pairs={{0,2},{1,3},{2,4},{3,5},{4,6},{5,7},{6,0},{7,1},{8,10},{9,11},{10,... | collective-permute-start | bytes 1253384 | tf_op jit(solution)/shard_map/ppermute | solution.py:312
  67.6 21.7 %copy-start.9 = (bf16[96,2176]{1,0:T(8,128)(2,1)}, bf16[96,2176]{1,0:T(8,128)(2,1)S(1)}, u32[]{:S(2)}) copy-start(bf16[96,2176]{1,0:T(8,128)(2,1)S(1)} %collective-permute-done.3.refs_6_) | copy-start | bytes 1253380
  71.7 12.0 %collective-permute-start.12 = (bf16[96,2048]{1,0:T(8,128)(2,1)S(1)}, bf16[96,2048]{1,0:T(8,128)(2,1)S(1)}, u32[]{:S(2)}, u32[]{:S(2)}) collective-permute-start(bf16[96,2048]{1,0:T(8,128)(2,1)S(1)} %pad_maximum_fusion.4.refs_11_), channel_id=1, source_target_pairs={{0,6},{1,7},{2,0},{3,1},{4,2},{5,3},{6,4},{7,5},{8,14},{9,15},{10,... | collective-permute-start | bytes 1179656 | tf_op jit(solution)/shard_map/ppermute | solution.py:312
  73.7 10.2 %collective-permute-start.11 = (bf16[96,2048]{1,0:T(8,128)(2,1)S(1)}, bf16[96,2048]{1,0:T(8,128)(2,1)S(1)}, u32[]{:S(2)}, u32[]{:S(2)}) collective-permute-start(bf16[96,2048]{1,0:T(8,128)(2,1)S(1)} %pad_maximum_fusion.4.refs_11_), channel_id=1, source_target_pairs={{0,2},{1,3},{2,4},{3,5},{4,6},{5,7},{6,0},{7,1},{8,10},{9,11},{10,... | collective-permute-start | bytes 1179656 | tf_op jit(solution)/shard_map/ppermute | solution.py:312
  73.7 11.5 %collective-permute-start.10 = (bf16[96,2048]{1,0:T(8,128)(2,1)S(1)}, bf16[96,2048]{1,0:T(8,128)(2,1)S(1)}, u32[]{:S(2)}, u32[]{:S(2)}) collective-permute-start(bf16[96,2048]{1,0:T(8,128)(2,1)S(1)} %pad_maximum_fusion.4.refs_11_), channel_id=1, source_target_pairs={{0,8},{1,9},{2,10},{3,11},{4,12},{5,13},{6,14},{7,15},{8,0},{9,1},... | collective-permute-start | bytes 1179656 | tf_op jit(solution)/shard_map/ppermute | solution.py:312
  75.9 13.4 %collective-permute-start.6 = (bf16[96,2176]{1,0:T(8,128)(2,1)S(1)}, bf16[96,2176]{1,0:T(8,128)(2,1)S(1)}, u32[]{:S(2)}, u32[]{:S(2)}) collective-permute-start(bf16[96,2176]{1,0:T(8,128)(2,1)S(1)} %broadcast_select_fusion), channel_id=1, source_target_pairs={{0,2},{1,7},{2,4},{3,1},{4,6},{5,3},{6,0},{7,5},{8,10},{9,15},{10,... | collective-permute-start | bytes 1253384 | tf_op jit(solution)/shard_map/ppermute | solution.py:312
  84.0 12.9 %collective-permute-start.15 = (bf16[96,2048]{1,0:T(8,128)(2,1)S(1)}, bf16[96,2048]{1,0:T(8,128)(2,1)S(1)}, u32[]{:S(2)}, u32[]{:S(2)}) collective-permute-start(bf16[96,2048]{1,0:T(8,128)(2,1)S(1)} %broadcast_select_fusion.3), channel_id=1, source_target_pairs={{0,2},{1,7},{2,4},{3,1},{4,6},{5,3},{6,0},{7,5},{8,10},{9,15},{10,... | collective-permute-start | bytes 1179656 | tf_op jit(solution)/shard_map/ppermute | solution.py:312
  85.2 12.1 %collective-permute-start.14 = (bf16[96,2048]{1,0:T(8,128)(2,1)S(1)}, bf16[96,2048]{1,0:T(8,128)(2,1)S(1)}, u32[]{:S(2)}, u32[]{:S(2)}) collective-permute-start(bf16[96,2048]{1,0:T(8,128)(2,1)S(1)} %collective-permute-done.10.refs_12_), channel_id=1, source_target_pairs={{0,6},{1,7},{2,0},{3,1},{4,2},{5,3},{6,4},{7,5},{8,14},{9,15},{10,... | collective-permute-start | bytes 1179656 | tf_op jit(solution)/shard_map/ppermute | solution.py:312
  87.3 13.8 %collective-permute-start.13 = (bf16[96,2048]{1,0:T(8,128)(2,1)S(1)}, bf16[96,2048]{1,0:T(8,128)(2,1)S(1)}, u32[]{:S(2)}, u32[]{:S(2)}) collective-permute-start(bf16[96,2048]{1,0:T(8,128)(2,1)S(1)} %collective-permute-done.10.refs_12_), channel_id=1, source_target_pairs={{0,2},{1,3},{2,4},{3,5},{4,6},{5,7},{6,0},{7,1},{8,10},{9,11},{10,... | collective-permute-start | bytes 1179656 | tf_op jit(solution)/shard_map/ppermute | solution.py:312
  88.6 24.9 %copy-start.6 = (s32[136]{0:T(256)S(1)}, s32[136]{0:T(256)}, u32[]{:S(2)}) copy-start(s32[136]{0:T(256)} %owner_ref.1) | copy-start | bytes 1636
  89.3 24.3 %collective-permute-start.17 = (bf16[384,2048]{1,0:T(8,128)(2,1)}, bf16[384,2048]{1,0:T(8,128)(2,1)}, u32[]{:S(2)}, u32[]{:S(2)}) collective-permute-start(bf16[384,2048]{1,0:T(8,128)(2,1)} %pad_maximum_fusion.1), channel_id=1, source_target_pairs={{0,1},{1,0},{2,3},{3,2},{4,5},{5,4},{6,7},{7,6},{8,9},{9,8},{10,11... | collective-permute-start | bytes 4718600 | tf_op jit(solution)/shard_map/ppermute | solution.py:312
  96.9 14.7 %collective-permute-start.8 = (bf16[288,2176]{1,0:T(8,128)(2,1)}, bf16[288,2176]{1,0:T(8,128)(2,1)}, u32[]{:S(2)}, u32[]{:S(2)}) collective-permute-start(bf16[288,2176]{1,0:T(8,128)(2,1)} %pad_maximum_fusion.2), channel_id=1, source_target_pairs={{0,1},{1,0},{2,3},{3,2},{4,5},{5,4},{6,7},{7,6},{8,9},{9,8},{10,11... | collective-permute-start | bytes 3760136 | tf_op jit(solution)/shard_map/ppermute | solution.py:312
  97.3 5.0 %collective-permute-start.9 = (bf16[96,2176]{1,0:T(8,128)(2,1)S(1)}, bf16[96,2176]{1,0:T(8,128)(2,1)S(1)}, u32[]{:S(2)}, u32[]{:S(2)}) collective-permute-start(bf16[96,2176]{1,0:T(8,128)(2,1)S(1)} %collective-permute-done.6.refs_7_), channel_id=1, source_target_pairs={{0,1},{1,0},{2,3},{3,2},{4,5},{5,4},{6,7},{7,6},{8,9},{9,8},{10,11... | collective-permute-start | bytes 1253384 | tf_op jit(solution)/shard_map/ppermute | solution.py:312
  102.2 11.3 %collective-permute-start.18 = (bf16[288,2048]{1,0:T(8,128)(2,1)}, bf16[288,2048]{1,0:T(8,128)(2,1)}, u32[]{:S(2)}, u32[]{:S(2)}) collective-permute-start(bf16[288,2048]{1,0:T(8,128)(2,1)} %pad_maximum_fusion.3), channel_id=1, source_target_pairs={{0,1},{1,0},{2,3},{3,2},{4,5},{5,4},{6,7},{7,6},{8,9},{9,8},{10,11... | collective-permute-start | bytes 3538952 | tf_op jit(solution)/shard_map/ppermute | solution.py:312
  102.3 9.2 %collective-permute-start.16 = (bf16[96,2048]{1,0:T(8,128)(2,1)S(1)}, bf16[96,2048]{1,0:T(8,128)(2,1)}, u32[]{:S(2)}, u32[]{:S(2)}) collective-permute-start(bf16[96,2048]{1,0:T(8,128)(2,1)S(1)} %broadcast_select_fusion.2), channel_id=1, source_target_pairs={{0,2},{1,7},{2,4},{3,1},{4,6},{5,3},{6,0},{7,5},{8,10},{9,15},{10,... | collective-permute-start | bytes 1179656 | tf_op jit(solution)/shard_map/ppermute | solution.py:312
  111.4 2.1 %collective-permute-start.19 = (bf16[96,2048]{1,0:T(8,128)(2,1)}, bf16[96,2048]{1,0:T(8,128)(2,1)}, u32[]{:S(2)}, u32[]{:S(2)}) collective-permute-start(bf16[96,2048]{1,0:T(8,128)(2,1)} %collective-permute-done.16.refs_18_), channel_id=1, source_target_pairs={{0,1},{1,0},{2,3},{3,2},{4,5},{5,4},{6,7},{7,6},{8,9},{9,8},{10,11... | collective-permute-start | bytes 1179656 | tf_op jit(solution)/shard_map/ppermute | solution.py:312
  (9 other events, 110.2 us)

commit v3 on v2

--- a/solution.py
+++ b/solution.py
@@ -1,3 +1,5 @@
+import functools
+
 import jax
 import jax.numpy as jnp
 from jax import lax
@@ -17,10 +19,30 @@
     return lax.dot_general(a, b, dims, preferred_element_type=F32)
 
 
-def prep_kernel(rows_ref, labels_ref, img_ref, filt_ref, win_ref, w_ref, sel_ref, lab_ref, nblk_ref, x_ref, pick_ref):
+def prep_kernel(rows_ref, labels_ref, filt_ref, img_hbm, win_ref, w_ref, sel_ref, lab_ref, nblk_ref, img_ref, x_ref, pick_ref, flat_ref, sem):
+    fetch = pltpu.make_async_copy(img_hbm, img_ref, sem)
+    fetch.start()
+    flat_ref[...] = jnp.zeros_like(flat_ref)
+    for i in range(6):
+        for j in range(6):
+            p = 6 * i + j
+            flat_ref[3 * p:3 * p + 3, :] = filt_ref[i, j].astype(F32)
+    rows_i = lax.broadcasted_iota(jnp.int32, (1536, 128), 0)
+    cols_i = lax.broadcasted_iota(jnp.int32, (1536, 128), 1)
+    d = rows_i // 256
+    di = d // 3
+    dj = d - 3 * di
+    r = rows_i % 256 // 32 - 2 * di
+    c = rows_i % 32 - 6 * dj
+    ok = (r >= 0) & (r < 6) & (c >= 0) & (c < 18)
+    spread = jnp.where(ok & (cols_i == r * 18 + c), 1.0, 0.0).astype(BF)
+    for nc in range(4):
+        w_ref[nc] = dot(spread, flat_ref[:, nc * 256:(nc + 1) * 256].astype(BF)).astype(BF)
+
     lanes = lax.broadcasted_iota(jnp.int32, (ROWS, 128), 1)
     subs = lax.broadcasted_iota(jnp.int32, (ROWS, 128), 0)
-    hit = rows_ref[...] == lanes
+    rows = jnp.broadcast_to(rows_ref[...], (128, 128)).astype(F32).T[:ROWS]
+    hit = rows.astype(jnp.int32) == lanes
     used = jnp.max(jnp.where(hit, 1.0, 0.0), axis=0, keepdims=True)
     low = lax.broadcasted_iota(jnp.int32, (128, 128), 0)
     high = lax.broadcasted_iota(jnp.int32, (128, 128), 1)
@@ -37,37 +59,29 @@
     fine = label - coarse * 8
     lab_ref[...] = jnp.where(lanes == 0, coarse, jnp.where(lanes == 1, fine, 0)).astype(BF)
     take = compact[:, :ROWS]
-    rows_i = lax.broadcasted_iota(jnp.int32, (1536, 128), 0)
-    cols_i = lax.broadcasted_iota(jnp.int32, (1536, 128), 1)
-    d = rows_i // 256
-    di = d // 3
-    dj = d - 3 * di
-    r = rows_i % 256 // 32 - 2 * di
-    c = rows_i % 32 - 6 * dj
-    ok = (r >= 0) & (r < 6) & (c >= 0) & (c < 18)
-    spread = jnp.where(ok & (cols_i == r * 18 + c), 1.0, 0.0).astype(BF)
-    for nc in range(4):
-        w_ref[nc] = dot(spread, filt_ref[:, nc * 256:(nc + 1) * 256]).astype(BF)
-    for part in range(16):
-        x_ref[part] = dot(take, img_ref[:, part * 768:(part + 1) * 768]).astype(BF)
     col = lax.broadcasted_iota(jnp.int32, (1, 1280), 1)
     within = col % 32
     source = (col % 128) // 32 * 192 + 18 * (col // 128) + within
     source = jnp.where(within < 30, source, -1)
     place = lax.broadcasted_iota(jnp.int32, (768, 1280), 0)
     pick_ref[...] = jnp.where(place == source, 1.0, 0.0).astype(BF)
-
-    @pl.loop(0, 16)
-    def _(part):
-        for n in range(5):
-            tile = dot(x_ref[part], pick_ref[:, n * 256:(n + 1) * 256]).astype(BF)
-            for h in range(2):
-                g = 2 * n + h
+    fetch.wait()
+    for part in range(16):
+        x_ref[part * ROWS:(part + 1) * ROWS, :] = dot(take, img_ref[:, part * 768:(part + 1) * 768]).astype(BF)
+
+    @pl.loop(0, 5)
+    def _(n):
+        tile = dot(x_ref[...], pick_ref[:, pl.ds(pl.multiple_of(n * 256, 256), 256)]).astype(BF)
+        for h in range(2):
+            at = pl.multiple_of((2 * n + h) * 16, 16)
+            for part in range(16):
                 for b in range(NBLK):
-                    win_ref[part, b, g * 16:(g + 1) * 16, :] = tile[b * 16:(b + 1) * 16, h * 128:(h + 1) * 128]
-
-
-def prep(images, row_list, labels, flat):
+                    row = part * ROWS + b * 16
+                    win_ref[part, b, pl.ds(at, 16), :] = tile[row:row + 16, h * 128:(h + 1) * 128]
+
+
+def prep(images, row_list, labels, filters):
+    vmem = pl.BlockSpec(memory_space=pltpu.VMEM)
     return pl.pallas_call(
         prep_kernel,
         out_shape=(
@@ -77,22 +91,22 @@
             jax.ShapeDtypeStruct((ROWS, 128), BF),
             jax.ShapeDtypeStruct((1, 1), jnp.int32),
         ),
-        out_specs=(
-            pl.BlockSpec(memory_space=pltpu.VMEM),
-            pl.BlockSpec(memory_space=pltpu.VMEM),
-            pl.BlockSpec(memory_space=pltpu.VMEM),
-            pl.BlockSpec(memory_space=pltpu.VMEM),
-            pl.BlockSpec(memory_space=pltpu.SMEM),
-        ),
-        scratch_shapes=[pltpu.VMEM((16, ROWS, 768), BF), pltpu.VMEM((768, 1280), BF)],
+        in_specs=[vmem, vmem, vmem, pl.BlockSpec(memory_space=pl.ANY)],
+        out_specs=(vmem, vmem, vmem, vmem, pl.BlockSpec(memory_space=pltpu.SMEM)),
+        scratch_shapes=[
+            pltpu.VMEM((ROWS, 12288), BF),
+            pltpu.VMEM((16 * ROWS, 768), BF),
+            pltpu.VMEM((768, 1280), BF),
+            pltpu.VMEM((128, 1024), F32),
+            pltpu.SemaphoreType.DMA,
+        ],
         compiler_params=pltpu.CompilerParams(vmem_limit_bytes=40 * 2**20),
         name="prep",
-    )(row_list.reshape(ROWS, 1), jnp.pad(labels, (0, 32)).reshape(1, 128), images, flat)
-
-
-def conv_kernel(nblk_ref, win_ref, w_ref, sel_ref, bias_ref, lab_ref, *refs):
+    )(jnp.pad(row_list, (0, 32)).reshape(1, 128), jnp.pad(labels, (0, 32)).reshape(1, 128), filters, images)
+
+
+def conv_kernel(first, count, nblk_ref, win_ref, w_ref, sel_ref, bias_ref, lab_ref, *refs):
     out_ref, uniq_ref = refs[-2:]
-    count = w_ref.shape[0]
     uniq_ref[...] = jnp.zeros_like(uniq_ref)
     if out_ref.shape[1] > count * 1024:
         out_ref[:, count * 1024:] = lab_ref[...]
@@ -113,7 +127,7 @@
         for k, (d, w, _) in enumerate(steps):
             if w == 0:
                 for m in range(2):
-                    pltpu.matmul_push_rhs(w_ref[nc, d * 256:(d + 1) * 256, :], d % 2, m)
+                    pltpu.matmul_push_rhs(w_ref[first + nc, d * 256:(d + 1) * 256, :], d % 2, m)
             for m in range(2):
                 rows = slice(m * 80, (m + 1) * 80)
                 lhs = jnp.concatenate([win_ref[w, b, rows, :], win_ref[w + 1, b, rows, :]], axis=1)
@@ -132,7 +146,7 @@
     def scoped(*accs):
         @pl.loop(0, count)
         def _(nc):
-            bias = bias_ref[nc]
+            bias = bias_ref[first + nc]
             floor = jnp.broadcast_to(-bias, (16, 256))
 
             @pl.loop(0, nblk_ref[0, 0])
@@ -155,10 +169,9 @@
     )
 
 
-def conv(nblk, win, w, sel, bias, lab, extra, after=()):
-    count = w.shape[0]
+def conv(first, count, nblk, win, w, sel, bias, lab, extra, after=()):
     return pl.pallas_call(
-        conv_kernel,
+        functools.partial(conv_kernel, first, count),
         out_shape=jax.ShapeDtypeStruct((ROWS, count * 1024 + extra), BF),
         in_specs=[pl.BlockSpec(memory_space=pltpu.SMEM)] + [pl.BlockSpec(memory_space=pltpu.VMEM)] * 5
         + [pl.BlockSpec(memory_space=pl.ANY)] * len(after),
@@ -172,7 +185,9 @@
 
 TILES = 16
 OWNED = 20
-SLOTS = 24
+SLOTS = 25
+NOTE = 4
+FIRST = 5
 NTILES = 136
 GROUP = 1536
 CLASSES = 1000
@@ -185,24 +200,17 @@
 def gram_kernel(me_ref, owner_ref, *refs):
     n = len(BLOCKS)
     parts, (out_ref, peak_ref) = (refs[:n], refs[n:2 * n]), refs[2 * n:2 * n + 2]
-    f_ref, ft_ref, lab, target_ref, left_ref, list_i, list_j, sem = refs[2 * n + 2:]
+    fa_ref, fb_ref, ft_ref, target_ref, left_ref, list_i, list_j, sem = refs[2 * n + 2:]
+    held = (fa_ref, fb_ref)
     me_tile = me_ref[0]
-    peak_ref[...] = jnp.zeros_like(peak_ref)
-    copies = {}
-    for part in range(2):
-        for local in range(2):
-            for q in range(4):
-                tile = q * 4 + part * 2 + local
-                cols = slice(local * 1024 + q * 256, local * 1024 + (q + 1) * 256)
-                copies[tile] = [
-                    pltpu.make_async_copy(ref.at[:, cols], f_ref.at[tile, start:start + size], sem.at[tile])
-                    for ref, (start, size) in zip(parts[part], BLOCKS)
-                ]
-    copies[TILES] = [
-        pltpu.make_async_copy(ref.at[:, 2048:], lab.at[start:start + size], sem.at[TILES])
-        for ref, (start, size) in zip(parts[0], BLOCKS)
+    copies = [
+        [
+            pltpu.make_async_copy(ref, held[part].at[start:start + size], sem.at[part * n + k])
+            for k, (ref, (start, size)) in enumerate(zip(parts[part], BLOCKS))
+        ]
+        for part in range(2)
     ]
-    for group in copies.values():
+    for group in copies:
         for copy in group:
             copy.start()
 
@@ -220,39 +228,54 @@
         return i2, jnp.where(wrap, i2, j + 1), n + mine.astype(jnp.int32)
 
     _, _, owned = lax.fori_loop(0, NTILES, scan, (jnp.int32(0), jnp.int32(0), jnp.int32(0)))
-
-    for copy in copies[TILES]:
-        copy.wait()
-    labels = lab[...].astype(F32)
-    label = (labels[:, 0:1] * 8.0 + labels[:, 1:2]).astype(jnp.int32)
+    peak_ref[...] = jnp.zeros_like(peak_ref)
+
+    @pl.loop(owned, OWNED)
+    def _(slot):
+        for k in range(FEAT):
+            out_ref[k, slot + FIRST] = jnp.zeros((32, 256), F32)
+
+    for part in range(2):
+        for copy in copies[part]:
+            copy.wait()
+        for local in range(2):
+            for q in range(4):
+                cols = slice(local * 1024 + q * 256, local * 1024 + (q + 1) * 256)
+                ft_ref[q * 4 + part * 2 + local] = held[part][:, cols].T
+    digit = lax.broadcasted_iota(jnp.int32, (128, 256), 0)
+    weight = jnp.where(digit == 0, 8.0, jnp.where(digit == 1, 1.0, 0.0)).astype(BF)
+    label = dot(fa_ref[:, 2048:], weight)
+    classes = lax.broadcasted_iota(jnp.int32, (GROUP, 256), 1).astype(F32)
     for s in range(4):
-        classes = lax.broadcasted_iota(jnp.int32, (GROUP, 256), 1) + 256 * s
-        target_ref[:, s * 256:(s + 1) * 256] = jnp.where(label == classes, 1.0, -1.0).astype(BF)
-    for t in range(TILES):
-        for copy in copies[t]:
-            copy.wait()
-        ft_ref[t] = f_ref[t].T
+        target_ref[:, s * 256:(s + 1) * 256] = jnp.where(label == classes + 256.0 * s, 1.0, -1.0).astype(BF)
 
     def put(slot, product):
         peak_ref[...] = jnp.maximum(peak_ref[...], jnp.max(jnp.abs(product).reshape(32, 8, 256), axis=0))
         for k in range(FEAT):
             out_ref[k, slot] = product[k * 32:(k + 1) * 32, :]
-
-    @pl.loop(0, owned)
-    def _(slot):
-        put(slot, dot(ft_ref[list_i[slot]], f_ref[list_j[slot]]))
-
-    @pl.loop(owned, OWNED)
-    def _(slot):
-        for k in range(FEAT):
-            out_ref[k, slot] = jnp.zeros((32, 256), F32)
 
     start = pl.multiple_of(me_tile % 8 * 32, 32)
     for f in range(FEAT):
         t = f // 2 * 4 + f % 2 * 2 + me_tile // 8
         left_ref[f * 32:(f + 1) * 32, :] = ft_ref[t, pl.ds(start, 32), :]
     for s in range(4):
-        put(OWNED + s, dot(left_ref[...], target_ref[:, s * 256:(s + 1) * 256]))
+        put(s, dot(left_ref[...], target_ref[:, s * 256:(s + 1) * 256]))
+    for s in range(0, FEAT, 2):
+        out_ref[s:s + 2, NOTE] = jnp.zeros((2, 32, 256), F32)
+
+    @pl.loop(0, owned)
+    def _(slot):
+        j = list_j[slot]
+        at = pl.multiple_of(j % 2 * 1024 + j // 4 * 256, 256)
+        second = j % 4 >= 2
+
+        @pl.when(second)
+        def _():
+            put(slot + FIRST, dot(ft_ref[list_i[slot]], fb_ref[:, pl.ds(at, 256)]))
+
+        @pl.when(jnp.logical_not(second))
+        def _():
+            put(slot + FIRST, dot(ft_ref[list_i[slot]], fa_ref[:, pl.ds(at, 256)]))
 
 
 def gram(me, tile_owner, parts):
@@ -261,19 +284,19 @@
     return pl.pallas_call(
         gram_kernel,
         out_shape=(jax.ShapeDtypeStruct((FEAT, SLOTS, 32, 256), F32), jax.ShapeDtypeStruct((8, 256), F32)),
-        in_specs=[smem, smem] + [pl.BlockSpec(memory_space=pl.ANY)] * (2 * len(BLOCKS)),
+        in_specs=[smem, smem] + [pl.BlockSpec(memory_space=pltpu.HBM)] * (2 * len(BLOCKS)),
         out_specs=(vmem, vmem),
         scratch_shapes=[
-            pltpu.VMEM((TILES, GROUP, 256), BF),
+            pltpu.VMEM((GROUP, 2176), BF),
+            pltpu.VMEM((GROUP, 2048), BF),
             pltpu.VMEM((TILES, 256, GROUP), BF),
-            pltpu.VMEM((GROUP, 128), BF),
             pltpu.VMEM((GROUP, 1024), BF),
             pltpu.VMEM((256, GROUP), BF),
             pltpu.SMEM((OWNED,), jnp.int32),
             pltpu.SMEM((OWNED,), jnp.int32),
-            pltpu.SemaphoreType.DMA((TILES + 1,)),
+            pltpu.SemaphoreType.DMA((2 * len(BLOCKS),)),
         ],
-        compiler_params=pltpu.CompilerParams(vmem_limit_bytes=50 * 2**20),
+        compiler_params=pltpu.CompilerParams(vmem_limit_bytes=56 * 2**20),
         cost_estimate=pl.CostEstimate(flops=5 * 10**9, bytes_accessed=20 * 2**20, transcendentals=0),
         name="gram",
     )(me, tile_owner, *parts[0], *parts[1])
@@ -282,19 +305,25 @@
 HALF = jnp.float16
 
 
-def exchange(partial, peak):
+STEPS = (8, 12, 20)
+
+
+def exchange(partial, peak, owned):
     exponent = jnp.floor(jnp.log2(jnp.maximum(jnp.max(peak), 1e-30)))
-    coded = (partial * jnp.exp2(13.0 - exponent)).astype(HALF)
-    note = jnp.broadcast_to(exponent.astype(HALF), (FEAT, 1, 32, 256))
-    got = lax.all_to_all(jnp.concatenate([coded, note], axis=1), "feat", split_axis=0, concat_axis=0, tiled=True)
-    back = jnp.exp2(got[:, SLOTS:, :1, :1].astype(F32) - 13.0) * (1.0 / 12288.0)
-    total = jnp.sum(got[:, :SLOTS].astype(F32) * back, axis=0)
-    return total
-
-
-def finish(total):
-    cross = total[OWNED:].transpose(1, 0, 2).reshape(32, 1024)[:, :CLASSES]
-    return total[:OWNED], cross
+    scale = jnp.exp2(13.0 - exponent)
+
+    def some(count, partial):
+        used = partial[:, :FIRST + count]
+        note = lax.broadcasted_iota(jnp.int32, used.shape, 1) == NOTE
+        coded = jnp.where(note, exponent, used * scale).astype(HALF)
+        got = lax.all_to_all(coded, "feat", split_axis=0, concat_axis=0, tiled=True)
+        back = jnp.exp2(got[:, NOTE:FIRST, :1, :1].astype(F32) - 13.0) * (1.0 / 12288.0)
+        total = jnp.sum(got.astype(F32) * back, axis=0)
+        cross = total[:NOTE].transpose(1, 0, 2).reshape(32, 1024)[:, :CLASSES]
+        return jnp.pad(total[FIRST:], ((0, OWNED - count), (0, 0), (0, 0))), cross
+
+    level = sum((owned > step).astype(jnp.int32) for step in STEPS[:-1])
+    return lax.switch(level, [functools.partial(some, step) for step in STEPS], partial)
 
 
 def hop(dy=0, dx=0, core=0):
@@ -340,14 +369,13 @@
 
 
 def body(images, row_list, labels, filters, bias, tile_owner):
-    flat = jnp.pad(filters.reshape(108, 1024), ((0, 20), (0, 0)))
-    win, w, sel, lab, nblk = prep(images, row_list, labels, flat)
+    win, w, sel, lab, nblk = prep(images, row_list, labels, filters)
     bias4 = bias.reshape(4, 1, 256)
-    own_a = conv(nblk, win, w[0:2], sel, bias4[0:2], lab, 128)
+    own_a = conv(0, 2, nblk, win, w, sel, bias4, lab, 128)
     first_a = spread_first(own_a)
-    own_b2 = conv(nblk, win, w[2:3], sel, bias4[2:3], lab, 0, (own_a,))
+    own_b2 = conv(2, 1, nblk, win, w, sel, bias4, lab, 0, (own_a,))
     second_a = spread_second(first_a)
-    own_b3 = conv(nblk, win, w[3:4], sel, bias4[3:4], lab, 0, first_a[1:])
+    own_b3 = conv(3, 1, nblk, win, w, sel, bias4, lab, 0, first_a[1:])
     own_b = jnp.concatenate([own_b2, own_b3], axis=1)
     own_b, far, over_left, over_right = lax.optimization_barrier((own_b,) + second_a[:3])
     second_a = (far, over_left, over_right, second_a[3])
@@ -357,7 +385,8 @@
     part_b = spread_third(first_b, second_b)
     me = jnp.stack([lax.axis_index("tile"), lax.axis_index("feat")]).astype(jnp.int32)
     partial, peak = gram(me, tile_owner, (part_a, part_b))
-    return finish(exchange(partial, peak))
+    owned = jnp.sum((tile_owner == me[0]).astype(jnp.int32))
+    return exchange(partial, peak, owned)
 
 
 def solution(mesh):

time: 186 us -> 166 us (0.89)
  the two profiles are of different devices: /device:TPU:0 before, /device:TPU:4 now
where the time goes in v3:
time: 166 us; the launch traced here: 165 us
  Pallas kernels  63 us (38%)
  blocking collectives  33.1 us (20%)
  starting transfers between devices  25.2 us (15%)
  waiting for transfers between devices  20.3 us (12%)
  other arithmetic  11.7 us (7%)
  local copies, waits for them, and re-layouts  8.38 us (5%)
  between operations  2.93 us (2%)
    pallas_call x3, Pallas kernels, conv(): pl.pallas_call(functools.partial(conv_kernel, first, count), out_shape=ja...  36.3 us
    all_to_all x1, blocking collectives, some(): got = lax.all_to_all(coded, 'feat', split_axis=0, concat_axis=0, tiled=True)  33.1 us
    ppermute x20, starting transfers between devices, send(): return lax.ppermute(block, 'tile', perm)  25.2 us
    ppermute x20, waiting for transfers between devices, send(): return lax.ppermute(block, 'tile', perm)  20.3 us
    pallas_call x1, Pallas kernels, gram(): pl.pallas_call(gram_kernel, out_shape=(jax.ShapeDtypeStruct((FEAT, SLOTS,...  19.6 us
    pallas_call x1, Pallas kernels, prep(): pl.pallas_call(prep_kernel, out_shape=(jax.ShapeDtypeStruct((16, NBLK, 16...  7.17 us
    unnamed x54, local copies, waits for them, and re-layouts  6.03 us
    convert_element_type x1, other arithmetic, some(): coded = jnp.where(note, exponent, used * scale).astype(HALF)  4.08 us
  transfers between devices with their start and end apart: 20, of which 6 were waited for; matrix products, arithmetic and copies ran while one was open for 3% of the time, Pallas kernels for 11%

profile of v3, /device:TPU:4, one launch (start us, length us, event | category | flops | bytes accessed | tf_op | source)
XLA Modules:
  0.0 164.7 jit_solution(17015871372152627231)
XLA Ops:
  1.3 1.7 %copy-done = bf16[96,12288]{1,0:T(8,128)(2,1)S(1)} copy-done((bf16[96,12288]{1,0:T(8,128)(2,1)S(1)}, bf16[96,12288]{1,0:T(8,128)(2,1)}, u32[]{:S(2)}) %copy-start) | copy-done | bytes 2359320
  3.9 7.2 %prep.1 = (bf16[16,6,160,128]{3,2,1,0:T(8,128)(2,1)S(1)}, bf16[4,1536,256]{2,1,0:T(8,128)(2,1)S(1)}, bf16[96,256]{1,0:T(8,128)(2,1)S(1)}, bf16[96,128]{1,0:T(8,128)(2,1)S(1)}, s32[1,1]{1,0:T(1,128)}) custom-call(s32[1,128]{1,0:T(1,128)S(1)} %get-tuple-element.63.rows_ref, s32[1,128]{1,0:T(1,128)S(1)} %get-tuple-element.62.labels_ref, ...), custom_call_target="tpu_custom_call" | custom-call | tf_op jit(solution)/shard_map/prep/pallas_call | solution.py:85
  11.9 17.8 %conv.3.refs_0_ = bf16[96,2176]{1,0:T(8,128)(2,1)S(1)} custom-call(s32[1,1]{1,0:T(1,128)} %get-tuple-element.40.nblk_ref, bf16[16,6,160,128]{3,2,1,0:T(8,128)(2,1)S(1)} %get-tuple-element.41.win_ref, bf16[4,1536,256]{2,1,0:T(8,128)(2,1)S(1)} %get-tuple-element.42.w_ref, bf16[96,256]{1,0:T(8,128)(2,1)S(1)} %get-tuple-element.43.sel_ref, ...), custom_call_target="tpu_custom_call" | custom-call | flops 22649241600 | bytes 8388608 | tf_op jit(solution)/shard_map/conv/pallas_call | solution.py:173
  30.3 1.5 collective-permute-start.1
  31.8 3.2 %collective-permute-start = (bf16[96,2176]{1,0:T(8,128)(2,1)S(1)}, bf16[96,2176]{1,0:T(8,128)(2,1)S(1)}, u32[]{:S(2)}, u32[]{:S(2)}) collective-permute-start(bf16[96,2176]{1,0:T(8,128)(2,1)S(1)} %conv.3.refs_0_), channel_id=1, source_target_pairs={{0,8},{1,9},{2,10},{3,11},{4,12},{5,13},{6,14},{7,15},{8,0},{9,1},... | collective-permute-start | bytes 1253384 | tf_op jit(solution)/shard_map/ppermute | solution.py:341
  35.0 9.2 %conv.4 = bf16[96,1024]{1,0:T(8,128)(2,1)S(1)} custom-call(s32[1,1]{1,0:T(1,128)} %get-tuple-element.40.nblk_ref, bf16[16,6,160,128]{3,2,1,0:T(8,128)(2,1)S(1)} %get-tuple-element.41.win_ref, bf16[4,1536,256]{2,1,0:T(8,128)(2,1)S(1)} %get-tuple-element.42.w_ref, bf16[96,256]{1,0:T(8,128)(2,1)S(1)} %get-tuple-element.43.sel_ref, f32[4,1,256]{2,1,0:T(1,128)S(1)} %bitcast.29, ...), custom_call_target="tpu_custom_call" | custom-call | flops 11324620800 | bytes 8388608 | tf_op jit(solution)/shard_map/conv/pallas_call | solution.py:173
  44.3 2.5 %collective-permute-start.3 = (bf16[96,2176]{1,0:T(8,128)(2,1)S(1)}, bf16[96,2176]{1,0:T(8,128)(2,1)S(1)}, u32[]{:S(2)}, u32[]{:S(2)}) collective-permute-start(bf16[96,2176]{1,0:T(8,128)(2,1)S(1)} %broadcast_select_fusion.1), channel_id=1, source_target_pairs={{0,2},{1,7},{2,4},{3,1},{4,6},{5,3},{6,0},{7,5},{8,10},{9,15},{10,... | collective-permute-start | bytes 1253384 | tf_op jit(solution)/shard_map/ppermute | solution.py:341
  49.5 1.7 %collective-permute-start.4 = (bf16[96,2176]{1,0:T(8,128)(2,1)S(1)}, bf16[96,2176]{1,0:T(8,128)(2,1)S(1)}, u32[]{:S(2)}, u32[]{:S(2)}) collective-permute-start(bf16[96,2176]{1,0:T(8,128)(2,1)S(1)} %collective-permute-done.refs_0_.refs_1_), channel_id=1, source_target_pairs={{0,2},{1,3},{2,4},{3,5},{4,6},{5,7},{6,0},{7,1},{8,10},{9,11},{10,... | collective-permute-start | bytes 1253384 | tf_op jit(solution)/shard_map/ppermute | solution.py:341
  51.2 1.9 %copy-done.9 = bf16[4,1536,256]{2,1,0:T(8,128)(2,1)S(1)} copy-done((bf16[4,1536,256]{2,1,0:T(8,128)(2,1)S(1)}, bf16[4,1536,256]{2,1,0:T(8,128)(2,1)}, u32[]{:S(2)}) %copy-start.9) | copy-done | bytes 3145752
  53.1 9.3 %conv.5 = bf16[96,1024]{1,0:T(8,128)(2,1)S(1)} custom-call(s32[1,1]{1,0:T(1,128)} %get-tuple-element.40.nblk_ref, bf16[16,6,160,128]{3,2,1,0:T(8,128)(2,1)S(1)} %copy-done.7, bf16[4,1536,256]{2,1,0:T(8,128)(2,1)S(1)} %copy-done.9, bf16[96,256]{1,0:T(8,128)(2,1)S(1)} %get-tuple-element.43.sel_ref, f32[4,1,256]{2,1,0:T(1,128)S(1)} %bitcast.30, ...), custom_call_target="tpu_custom_call" | custom-call | flops 11324620800 | bytes 8388608 | tf_op jit(solution)/shard_map/conv/pallas_call | solution.py:173
  63.0 1.7 %collective-permute-start.11 = (bf16[96,2048]{1,0:T(8,128)(2,1)S(1)}, bf16[96,2048]{1,0:T(8,128)(2,1)S(1)}, u32[]{:S(2)}, u32[]{:S(2)}) collective-permute-start(bf16[96,2048]{1,0:T(8,128)(2,1)S(1)} %pad_maximum_fusion.4.refs_11_), channel_id=1, source_target_pairs={{0,2},{1,3},{2,4},{3,5},{4,6},{5,7},{6,0},{7,1},{8,10},{9,11},{10,... | collective-permute-start | bytes 1179656 | tf_op jit(solution)/shard_map/ppermute | solution.py:341
  64.7 2.4 %collective-permute-start.10 = (bf16[96,2048]{1,0:T(8,128)(2,1)S(1)}, bf16[96,2048]{1,0:T(8,128)(2,1)S(1)}, u32[]{:S(2)}, u32[]{:S(2)}) collective-permute-start(bf16[96,2048]{1,0:T(8,128)(2,1)S(1)} %pad_maximum_fusion.4.refs_11_), channel_id=1, source_target_pairs={{0,8},{1,9},{2,10},{3,11},{4,12},{5,13},{6,14},{7,15},{8,0},{9,1},... | collective-permute-start | bytes 1179656 | tf_op jit(solution)/shard_map/ppermute | solution.py:341
  67.1 2.2 %collective-permute-start.6 = (bf16[96,2176]{1,0:T(8,128)(2,1)S(1)}, bf16[96,2176]{1,0:T(8,128)(2,1)S(1)}, u32[]{:S(2)}, u32[]{:S(2)}) collective-permute-start(bf16[96,2176]{1,0:T(8,128)(2,1)S(1)} %broadcast_select_fusion), channel_id=1, source_target_pairs={{0,2},{1,7},{2,4},{3,1},{4,6},{5,3},{6,0},{7,5},{8,10},{9,15},{10,... | collective-permute-start | bytes 1253384 | tf_op jit(solution)/shard_map/ppermute | solution.py:341
  69.3 5.4 %collective-permute-done.12.refs_14_ = bf16[96,2048]{1,0:T(8,128)(2,1)S(1)} collective-permute-done((bf16[96,2048]{1,0:T(8,128)(2,1)S(1)}, bf16[96,2048]{1,0:T(8,128)(2,1)S(1)}, u32[]{:S(2)}, u32[]{:S(2)}) %collective-permute-start.12) | collective-permute-done | bytes 393248 | tf_op jit(solution)/shard_map/ppermute | solution.py:341
  74.8 2.7 %collective-permute-start.15 = (bf16[96,2048]{1,0:T(8,128)(2,1)S(1)}, bf16[96,2048]{1,0:T(8,128)(2,1)S(1)}, u32[]{:S(2)}, u32[]{:S(2)}) collective-permute-start(bf16[96,2048]{1,0:T(8,128)(2,1)S(1)} %broadcast_select_fusion.3), channel_id=1, source_target_pairs={{0,2},{1,7},{2,4},{3,1},{4,6},{5,3},{6,0},{7,5},{8,10},{9,15},{10,... | collective-permute-start | bytes 1179656 | tf_op jit(solution)/shard_map/ppermute | solution.py:341
  78.0 1.5 collective-permute-start.13
  82.0 4.8 %collective-permute-done.15.refs_17_ = bf16[96,2048]{1,0:T(8,128)(2,1)S(1)} collective-permute-done((bf16[96,2048]{1,0:T(8,128)(2,1)S(1)}, bf16[96,2048]{1,0:T(8,128)(2,1)S(1)}, u32[]{:S(2)}, u32[]{:S(2)}) %collective-permute-start.15) | collective-permute-done | bytes 393248 | tf_op jit(solution)/shard_map/ppermute | solution.py:341
  86.8 2.7 %collective-permute-done.14.refs_16_ = bf16[96,2048]{1,0:T(8,128)(2,1)S(1)} collective-permute-done((bf16[96,2048]{1,0:T(8,128)(2,1)S(1)}, bf16[96,2048]{1,0:T(8,128)(2,1)S(1)}, u32[]{:S(2)}, u32[]{:S(2)}) %collective-permute-start.14) | collective-permute-done | bytes 393248 | tf_op jit(solution)/shard_map/ppermute | solution.py:341
  92.2 2.0 %collective-permute-start.16 = (bf16[96,2048]{1,0:T(8,128)(2,1)S(1)}, bf16[96,2048]{1,0:T(8,128)(2,1)S(1)}, u32[]{:S(2)}, u32[]{:S(2)}) collective-permute-start(bf16[96,2048]{1,0:T(8,128)(2,1)S(1)} %broadcast_select_fusion.2), channel_id=1, source_target_pairs={{0,2},{1,7},{2,4},{3,1},{4,6},{5,3},{6,0},{7,5},{8,10},{9,15},{10,... | collective-permute-start | bytes 1179656 | tf_op jit(solution)/shard_map/ppermute | solution.py:341
  94.1 5.9 %collective-permute-done.16.refs_18_ = bf16[96,2048]{1,0:T(8,128)(2,1)S(1)} collective-permute-done((bf16[96,2048]{1,0:T(8,128)(2,1)S(1)}, bf16[96,2048]{1,0:T(8,128)(2,1)S(1)}, u32[]{:S(2)}, u32[]{:S(2)}) %collective-permute-start.16) | collective-permute-done | bytes 393248 | tf_op jit(solution)/shard_map/ppermute | solution.py:341
  103.2 19.6 %gram.1 = (f32[8,25,32,256]{3,2,1,0:T(8,128)}, f32[8,256]{1,0:T(8,128)}) custom-call(s32[2]{0:T(128)} %pad_add_fusion.me_ref, s32[136]{0:T(256)} %owner_ref.1, bf16[96,2176]{1,0:T(8,128)(2,1)} %copy-done.3, bf16[96,2176]{1,0:T(8,128)(2,1)} %copy-done.4, bf16[96,2176]{1,0:T(8,128)(2,1)} %copy-done.2, bf16[96,2176]{1,0:T(8,128)(2,1)} %copy-done.1, ...), custom_call_target="tpu_custom_call" | custom-call | flops 5000000000 | bytes 20971520 | tf_op jit(solution)/shard_map/gram/pallas_call | solution.py:284
  124.9 39.9 %conditional.1 = (f32[20,32,256]{2,1,0:T(8,128)}, f32[32,1000]{1,0:T(8,128)}) conditional(s32[]{:T(128)} %clamp.3, (f32[]{:T(128)}, f32[8,25,32,256]{3,2,1,0:T(8,128)}, f32[]{:T(128)}) %tuple.21, (f32[]{:T(128)}, f32[8,25,32,256]{3,2,1,0:T(8,128)}, f32[]{:T(128)}) %tuple.21, (f32[]{:T(128)}, f32[]{:T(128)}, ...), branch_computations={%region_2.4_spmd, %region_4.6_spmd, %region_6.8_spmd} | conditional | flops 9625657 | bytes 22315226 | solution.py:326
  124.9 4.1 %select_convert_fusion.2 = f16[8,25,32,256]{3,2,1,0:T(8,128)(2,1)S(1)} fusion(f32[8,25,32,256]{3,2,1,0:T(8,128)} %get-tuple-element.25, f32[]{:T(128)} %get-tuple-element.26, f32[]{:T(128)} %get-tuple-element.24, pred[25]{0:T(512)(128)(4,1)S(1)} %iota_compare_fusion.2), kind=kLoop, calls=%fused_computation.11 | loop fusion | flops 4915200 | bytes 9830433 | tf_op jit(solution)/shard_map/cond/branch_2_fun/convert_element_type | solution.py:318
  129.0 33.1 %all_to_all.14 = f16[8,25,32,256]{3,2,1,0:T(8,128)(2,1)S(1)} all-to-all(f16[8,25,32,256]{3,2,1,0:T(8,128)(2,1)S(1)} %select_convert_fusion.2), channel_id=1, replica_groups=mesh['feat'=8,'tile'=16] {'feat'}, dimensions={0} | all-to-all | bytes 6553600 | tf_op jit(solution)/shard_map/cond/branch_2_fun/all_to_all | solution.py:319
  (99 shorter events, 17.8 us)
Async XLA Ops:
  11.1 23.9 %copy-start.6 = (bf16[16,6,160,128]{3,2,1,0:T(8,128)(2,1)}, bf16[16,6,160,128]{3,2,1,0:T(8,128)(2,1)S(1)}, u32[]{:S(2)}) copy-start(bf16[16,6,160,128]{3,2,1,0:T(8,128)(2,1)S(1)} %get-tuple-element.41.win_ref) | copy-start | bytes 11796484
  11.1 23.9 %copy-start.8 = (bf16[4,1536,256]{2,1,0:T(8,128)(2,1)}, bf16[4,1536,256]{2,1,0:T(8,128)(2,1)S(1)}, u32[]{:S(2)}) copy-start(bf16[4,1536,256]{2,1,0:T(8,128)(2,1)S(1)} %get-tuple-element.42.w_ref) | copy-start | bytes 9437188
  11.9 23.1 %copy-start.11 = (f32[1024]{0:T(1024)S(1)}, f32[1024]{0:T(1024)}, u32[]{:S(2)}) copy-start(f32[1024]{0:T(1024)} %param.13) | copy-start | bytes 12292
  29.7 14.5 %collective-permute-start.2 = (bf16[96,2176]{1,0:T(8,128)(2,1)S(1)}, bf16[96,2176]{1,0:T(8,128)(2,1)S(1)}, u32[]{:S(2)}, u32[]{:S(2)}) collective-permute-start(bf16[96,2176]{1,0:T(8,128)(2,1)S(1)} %conv.3.refs_0_), channel_id=1, source_target_pairs={{0,6},{1,7},{2,0},{3,1},{4,2},{5,3},{6,4},{7,5},{8,14},{9,15},{10,... | collective-permute-start | bytes 1253384 | tf_op jit(solution)/shard_map/ppermute | solution.py:341
  30.3 13.9 %collective-permute-start.1 = (bf16[96,2176]{1,0:T(8,128)(2,1)S(1)}, bf16[96,2176]{1,0:T(8,128)(2,1)S(1)}, u32[]{:S(2)}, u32[]{:S(2)}) collective-permute-start(bf16[96,2176]{1,0:T(8,128)(2,1)S(1)} %conv.3.refs_0_), channel_id=1, source_target_pairs={{0,2},{1,3},{2,4},{3,5},{4,6},{5,7},{6,0},{7,1},{8,10},{9,11},{10,... | collective-permute-start | bytes 1253384 | tf_op jit(solution)/shard_map/ppermute | solution.py:341
  31.8 15.0 %collective-permute-start = (bf16[96,2176]{1,0:T(8,128)(2,1)S(1)}, bf16[96,2176]{1,0:T(8,128)(2,1)S(1)}, u32[]{:S(2)}, u32[]{:S(2)}) collective-permute-start(bf16[96,2176]{1,0:T(8,128)(2,1)S(1)} %conv.3.refs_0_), channel_id=1, source_target_pairs={{0,8},{1,9},{2,10},{3,11},{4,12},{5,13},{6,14},{7,15},{8,0},{9,1},... | collective-permute-start | bytes 1253384 | tf_op jit(solution)/shard_map/ppermute | solution.py:341
  44.3 18.2 %collective-permute-start.3 = (bf16[96,2176]{1,0:T(8,128)(2,1)S(1)}, bf16[96,2176]{1,0:T(8,128)(2,1)S(1)}, u32[]{:S(2)}, u32[]{:S(2)}) collective-permute-start(bf16[96,2176]{1,0:T(8,128)(2,1)S(1)} %broadcast_select_fusion.1), channel_id=1, source_target_pairs={{0,2},{1,7},{2,4},{3,1},{4,6},{5,3},{6,0},{7,5},{8,10},{9,15},{10,... | collective-permute-start | bytes 1253384 | tf_op jit(solution)/shard_map/ppermute | solution.py:341
  48.1 54.3 %collective-permute-start.7 = (bf16[384,2176]{1,0:T(8,128)(2,1)}, bf16[384,2176]{1,0:T(8,128)(2,1)}, u32[]{:S(2)}, u32[]{:S(2)}) collective-permute-start(bf16[384,2176]{1,0:T(8,128)(2,1)} %pad_maximum_fusion), channel_id=1, source_target_pairs={{0,1},{1,0},{2,3},{3,2},{4,5},{5,4},{6,7},{7,6},{8,9},{9,8},{10,11... | collective-permute-start | bytes 5013512 | tf_op jit(solution)/shard_map/ppermute | solution.py:341
  49.2 13.4 %collective-permute-start.5 = (bf16[96,2176]{1,0:T(8,128)(2,1)S(1)}, bf16[96,2176]{1,0:T(8,128)(2,1)S(1)}, u32[]{:S(2)}, u32[]{:S(2)}) collective-permute-start(bf16[96,2176]{1,0:T(8,128)(2,1)S(1)} %collective-permute-done.refs_0_.refs_1_), channel_id=1, source_target_pairs={{0,6},{1,7},{2,0},{3,1},{4,2},{5,3},{6,4},{7,5},{8,14},{9,15},{10,... | collective-permute-start | bytes 1253384 | tf_op jit(solution)/shard_map/ppermute | solution.py:341
  49.5 13.0 %collective-permute-start.4 = (bf16[96,2176]{1,0:T(8,128)(2,1)S(1)}, bf16[96,2176]{1,0:T(8,128)(2,1)S(1)}, u32[]{:S(2)}, u32[]{:S(2)}) collective-permute-start(bf16[96,2176]{1,0:T(8,128)(2,1)S(1)} %collective-permute-done.refs_0_.refs_1_), channel_id=1, source_target_pairs={{0,2},{1,3},{2,4},{3,5},{4,6},{5,7},{6,0},{7,1},{8,10},{9,11},{10,... | collective-permute-start | bytes 1253384 | tf_op jit(solution)/shard_map/ppermute | solution.py:341
  62.5 19.5 %copy-start.14 = (bf16[96,2048]{1,0:T(8,128)(2,1)}, bf16[96,2048]{1,0:T(8,128)(2,1)S(1)}, u32[]{:S(2)}) copy-start(bf16[96,2048]{1,0:T(8,128)(2,1)S(1)} %pad_maximum_fusion.4.refs_11_) | copy-start | bytes 1179652
  62.6 12.1 %collective-permute-start.12 = (bf16[96,2048]{1,0:T(8,128)(2,1)S(1)}, bf16[96,2048]{1,0:T(8,128)(2,1)S(1)}, u32[]{:S(2)}, u32[]{:S(2)}) collective-permute-start(bf16[96,2048]{1,0:T(8,128)(2,1)S(1)} %pad_maximum_fusion.4.refs_11_), channel_id=1, source_target_pairs={{0,6},{1,7},{2,0},{3,1},{4,2},{5,3},{6,4},{7,5},{8,14},{9,15},{10,... | collective-permute-start | bytes 1179656 | tf_op jit(solution)/shard_map/ppermute | solution.py:341
  63.0 11.8 %collective-permute-start.11 = (bf16[96,2048]{1,0:T(8,128)(2,1)S(1)}, bf16[96,2048]{1,0:T(8,128)(2,1)S(1)}, u32[]{:S(2)}, u32[]{:S(2)}) collective-permute-start(bf16[96,2048]{1,0:T(8,128)(2,1)S(1)} %pad_maximum_fusion.4.refs_11_), channel_id=1, source_target_pairs={{0,2},{1,3},{2,4},{3,5},{4,6},{5,7},{6,0},{7,1},{8,10},{9,11},{10,... | collective-permute-start | bytes 1179656 | tf_op jit(solution)/shard_map/ppermute | solution.py:341
  64.7 12.8 %collective-permute-start.10 = (bf16[96,2048]{1,0:T(8,128)(2,1)S(1)}, bf16[96,2048]{1,0:T(8,128)(2,1)S(1)}, u32[]{:S(2)}, u32[]{:S(2)}) collective-permute-start(bf16[96,2048]{1,0:T(8,128)(2,1)S(1)} %pad_maximum_fusion.4.refs_11_), channel_id=1, source_target_pairs={{0,8},{1,9},{2,10},{3,11},{4,12},{5,13},{6,14},{7,15},{8,0},{9,1},... | collective-permute-start | bytes 1179656 | tf_op jit(solution)/shard_map/ppermute | solution.py:341
  67.1 13.7 %collective-permute-start.6 = (bf16[96,2176]{1,0:T(8,128)(2,1)S(1)}, bf16[96,2176]{1,0:T(8,128)(2,1)S(1)}, u32[]{:S(2)}, u32[]{:S(2)}) collective-permute-start(bf16[96,2176]{1,0:T(8,128)(2,1)S(1)} %broadcast_select_fusion), channel_id=1, source_target_pairs={{0,2},{1,7},{2,4},{3,1},{4,6},{5,3},{6,0},{7,5},{8,10},{9,15},{10,... | collective-permute-start | bytes 1253384 | tf_op jit(solution)/shard_map/ppermute | solution.py:341
  74.8 12.0 %collective-permute-start.15 = (bf16[96,2048]{1,0:T(8,128)(2,1)S(1)}, bf16[96,2048]{1,0:T(8,128)(2,1)S(1)}, u32[]{:S(2)}, u32[]{:S(2)}) collective-permute-start(bf16[96,2048]{1,0:T(8,128)(2,1)S(1)} %broadcast_select_fusion.3), channel_id=1, source_target_pairs={{0,2},{1,7},{2,4},{3,1},{4,6},{5,3},{6,0},{7,5},{8,10},{9,15},{10,... | collective-permute-start | bytes 1179656 | tf_op jit(solution)/shard_map/ppermute | solution.py:341
  77.5 12.1 %collective-permute-start.14 = (bf16[96,2048]{1,0:T(8,128)(2,1)S(1)}, bf16[96,2048]{1,0:T(8,128)(2,1)S(1)}, u32[]{:S(2)}, u32[]{:S(2)}) collective-permute-start(bf16[96,2048]{1,0:T(8,128)(2,1)S(1)} %collective-permute-done.10.refs_12_), channel_id=1, source_target_pairs={{0,6},{1,7},{2,0},{3,1},{4,2},{5,3},{6,4},{7,5},{8,14},{9,15},{10,... | collective-permute-start | bytes 1179656 | tf_op jit(solution)/shard_map/ppermute | solution.py:341
  78.0 13.9 %collective-permute-start.13 = (bf16[96,2048]{1,0:T(8,128)(2,1)S(1)}, bf16[96,2048]{1,0:T(8,128)(2,1)S(1)}, u32[]{:S(2)}, u32[]{:S(2)}) collective-permute-start(bf16[96,2048]{1,0:T(8,128)(2,1)S(1)} %collective-permute-done.10.refs_12_), channel_id=1, source_target_pairs={{0,2},{1,3},{2,4},{3,5},{4,6},{5,7},{6,0},{7,1},{8,10},{9,11},{10,... | collective-permute-start | bytes 1179656 | tf_op jit(solution)/shard_map/ppermute | solution.py:341
  80.8 21.7 %collective-permute-start.17 = (bf16[384,2048]{1,0:T(8,128)(2,1)}, bf16[384,2048]{1,0:T(8,128)(2,1)}, u32[]{:S(2)}, u32[]{:S(2)}) collective-permute-start(bf16[384,2048]{1,0:T(8,128)(2,1)} %pad_maximum_fusion.1), channel_id=1, source_target_pairs={{0,1},{1,0},{2,3},{3,2},{4,5},{5,4},{6,7},{7,6},{8,9},{9,8},{10,11... | collective-permute-start | bytes 4718600 | tf_op jit(solution)/shard_map/ppermute | solution.py:341
  86.8 15.6 %collective-permute-start.8 = (bf16[288,2176]{1,0:T(8,128)(2,1)}, bf16[288,2176]{1,0:T(8,128)(2,1)}, u32[]{:S(2)}, u32[]{:S(2)}) collective-permute-start(bf16[288,2176]{1,0:T(8,128)(2,1)} %pad_maximum_fusion.2), channel_id=1, source_target_pairs={{0,1},{1,0},{2,3},{3,2},{4,5},{5,4},{6,7},{7,6},{8,9},{9,8},{10,11... | collective-permute-start | bytes 3760136 | tf_op jit(solution)/shard_map/ppermute | solution.py:341
  89.6 2.6 %collective-permute-start.9 = (bf16[96,2176]{1,0:T(8,128)(2,1)S(1)}, bf16[96,2176]{1,0:T(8,128)(2,1)S(1)}, u32[]{:S(2)}, u32[]{:S(2)}) collective-permute-start(bf16[96,2176]{1,0:T(8,128)(2,1)S(1)} %collective-permute-done.6.refs_7_), channel_id=1, source_target_pairs={{0,1},{1,0},{2,3},{3,2},{4,5},{5,4},{6,7},{7,6},{8,9},{9,8},{10,11... | collective-permute-start | bytes 1253384 | tf_op jit(solution)/shard_map/ppermute | solution.py:341
  92.0 10.5 %collective-permute-start.18 = (bf16[288,2048]{1,0:T(8,128)(2,1)S(1)}, bf16[288,2048]{1,0:T(8,128)(2,1)}, u32[]{:S(2)}, u32[]{:S(2)}) collective-permute-start(bf16[288,2048]{1,0:T(8,128)(2,1)S(1)} %pad_maximum_fusion.3), channel_id=1, source_target_pairs={{0,1},{1,0},{2,3},{3,2},{4,5},{5,4},{6,7},{7,6},{8,9},{9,8},{10,11... | collective-permute-start | bytes 3538952 | tf_op jit(solution)/shard_map/ppermute | solution.py:341
  92.2 7.8 %collective-permute-start.16 = (bf16[96,2048]{1,0:T(8,128)(2,1)S(1)}, bf16[96,2048]{1,0:T(8,128)(2,1)S(1)}, u32[]{:S(2)}, u32[]{:S(2)}) collective-permute-start(bf16[96,2048]{1,0:T(8,128)(2,1)S(1)} %broadcast_select_fusion.2), channel_id=1, source_target_pairs={{0,2},{1,7},{2,4},{3,1},{4,6},{5,3},{6,0},{7,5},{8,10},{9,15},{10,... | collective-permute-start | bytes 1179656 | tf_op jit(solution)/shard_map/ppermute | solution.py:341
  100.0 2.4 %collective-permute-start.19 = (bf16[96,2048]{1,0:T(8,128)(2,1)S(1)}, bf16[96,2048]{1,0:T(8,128)(2,1)S(1)}, u32[]{:S(2)}, u32[]{:S(2)}) collective-permute-start(bf16[96,2048]{1,0:T(8,128)(2,1)S(1)} %collective-permute-done.16.refs_18_), channel_id=1, source_target_pairs={{0,1},{1,0},{2,3},{3,2},{4,5},{5,4},{6,7},{7,6},{8,9},{9,8},{10,11... | collective-permute-start | bytes 1179656 | tf_op jit(solution)/shard_map/ppermute | solution.py:341
  (23 other events, 249.8 us)

commit v4 on v3

--- a/solution.py
+++ b/solution.py
@@ -194,19 +194,21 @@
 FEAT = 8
 
 
-BLOCKS = ((0, 96), (96, 96), (192, 96), (288, 96), (384, 96), (480, 96), (576, 96), (672, 96), (768, 384), (1152, 288), (1440, 96))
+COMMON = tuple((96 * k, 96) for k in range(8)) + ((768, 384),)
+BLOCKS = (COMMON + ((1152, 288), (1440, 96)), COMMON + tuple((1152 + 96 * k, 96) for k in range(4)))
+COUNT = len(BLOCKS[0]) + len(BLOCKS[1])
 
 
 def gram_kernel(me_ref, owner_ref, *refs):
-    n = len(BLOCKS)
-    parts, (out_ref, peak_ref) = (refs[:n], refs[n:2 * n]), refs[2 * n:2 * n + 2]
-    fa_ref, fb_ref, ft_ref, target_ref, left_ref, list_i, list_j, sem = refs[2 * n + 2:]
+    n = len(BLOCKS[0])
+    parts, (out_ref, peak_ref) = (refs[:n], refs[n:COUNT]), refs[COUNT:COUNT + 2]
+    fa_ref, fb_ref, ft_ref, target_ref, left_ref, list_i, list_j, sem = refs[COUNT + 2:]
     held = (fa_ref, fb_ref)
     me_tile = me_ref[0]
     copies = [
         [
             pltpu.make_async_copy(ref, held[part].at[start:start + size], sem.at[part * n + k])
-            for k, (ref, (start, size)) in enumerate(zip(parts[part], BLOCKS))
+            for k, (ref, (start, size)) in enumerate(zip(parts[part], BLOCKS[part]))
         ]
         for part in range(2)
     ]
@@ -284,7 +286,7 @@
     return pl.pallas_call(
         gram_kernel,
         out_shape=(jax.ShapeDtypeStruct((FEAT, SLOTS, 32, 256), F32), jax.ShapeDtypeStruct((8, 256), F32)),
-        in_specs=[smem, smem] + [pl.BlockSpec(memory_space=pltpu.HBM)] * (2 * len(BLOCKS)),
+        in_specs=[smem, smem] + [pl.BlockSpec(memory_space=pltpu.HBM)] * COUNT,
         out_specs=(vmem, vmem),
         scratch_shapes=[
             pltpu.VMEM((GROUP, 2176), BF),
@@ -294,7 +296,7 @@
             pltpu.VMEM((256, GROUP), BF),
             pltpu.SMEM((OWNED,), jnp.int32),
             pltpu.SMEM((OWNED,), jnp.int32),
-            pltpu.SemaphoreType.DMA((2 * len(BLOCKS),)),
+            pltpu.SemaphoreType.DMA((COUNT,)),
         ],
         compiler_params=pltpu.CompilerParams(vmem_limit_bytes=56 * 2**20),
         cost_estimate=pl.CostEstimate(flops=5 * 10**9, bytes_accessed=20 * 2**20, transcendentals=0),
@@ -348,24 +350,30 @@
     return own, over, left, right
 
 
-def spread_second(first):
+def spread_second(first, earlier=None):
     own, over, left, right = first
     even = lax.axis_index("tile") % 2 == 0
     far = send(jnp.where(even, left, right), onward())
+    if earlier is not None:
+        over, far, *earlier[7:10] = lax.optimization_barrier((over, far, *earlier[7:10]))
     over_left = send(over, hop(dx=1))
     over_right = send(over, hop(dx=-1))
     swap_a = send(jnp.concatenate([own, over, left, right], axis=0), hop(core=1))
     return far, over_left, over_right, swap_a
 
 
-def spread_third(first, second):
+def spread_third(first, second, apart):
     own, over, left, right = first
     far, over_left, over_right, swap_a = second
-    even = lax.axis_index("tile") % 2 == 0
-    over_far = send(jnp.where(even, over_left, over_right), onward())
+    over_far = send(far, hop(dy=1))
+    held = [own, over, left, right, over_left, over_right, far, over_far, swap_a]
+    if apart:
+        far_swap = send(far, hop(core=1))
+        rest = lax.optimization_barrier((over_left, over_right, over_far))
+        swaps = [send(block, hop(core=1)) for block in rest]
+        return held + [swaps[0], swaps[1], far_swap, swaps[2]]
     swap_b = send(jnp.concatenate([over_left, over_right, far], axis=0), hop(core=1))
-    swap_c = send(over_far, hop(core=1))
-    return [own, over, left, right, over_left, over_right, far, over_far, swap_a, swap_b, swap_c]
+    return held + [swap_b, send(over_far, hop(core=1))]
 
 
 def body(images, row_list, labels, filters, bias, tile_owner):
@@ -380,9 +388,9 @@
     own_b, far, over_left, over_right = lax.optimization_barrier((own_b,) + second_a[:3])
     second_a = (far, over_left, over_right, second_a[3])
     first_b = spread_first(own_b)
-    part_a = spread_third(first_a, second_a)
-    second_b = spread_second(first_b)
-    part_b = spread_third(first_b, second_b)
+    part_a = spread_third(first_a, second_a, False)
+    second_b = spread_second(first_b, part_a)
+    part_b = spread_third(first_b, second_b, True)
     me = jnp.stack([lax.axis_index("tile"), lax.axis_index("feat")]).astype(jnp.int32)
     partial, peak = gram(me, tile_owner, (part_a, part_b))
     owned = jnp.sum((tile_owner == me[0]).astype(jnp.int32))

time: 166 us -> 167 us (level)
  the two profiles are of different devices: /device:TPU:4 before, /device:TPU:19 now
where the time goes in v4:
time: 167 us
  Pallas kernels  63.1 us (38%)
  starting transfers between devices  30.1 us (18%)
  blocking collectives  30 us (18%)
  waiting for transfers between devices  24.9 us (15%)
  other arithmetic  8.13 us (5%)
  local copies, waits for them, and re-layouts  7.67 us (5%)
  between operations  2.89 us (2%)
    pallas_call x3, Pallas kernels, conv(): pl.pallas_call(functools.partial(conv_kernel, first, count), out_shape=ja...  36.3 us
    ppermute x22, starting transfers between devices, send(): return lax.ppermute(block, 'tile', perm)  30.1 us
    all_to_all x1, blocking collectives, some(): got = lax.all_to_all(coded, 'feat', split_axis=0, concat_axis=0, tiled=True)  30 us
    ppermute x22, waiting for transfers between devices, send(): return lax.ppermute(block, 'tile', perm)  24.9 us
    pallas_call x1, Pallas kernels, gram(): pl.pallas_call(gram_kernel, out_shape=(jax.ShapeDtypeStruct((FEAT, SLOTS,...  19.6 us
    pallas_call x1, Pallas kernels, prep(): pl.pallas_call(prep_kernel, out_shape=(jax.ShapeDtypeStruct((16, NBLK, 16...  7.17 us
    unnamed x50, local copies, waits for them, and re-layouts  5.33 us
    convert_element_type x1, other arithmetic, some(): coded = jnp.where(note, exponent, used * scale).astype(HALF)  4.08 us
  transfers between devices with their start and end apart: 22, of which 5 were waited for; matrix products, arithmetic and copies ran while one was open for 1% of the time, Pallas kernels for 11%

profile of v4, /device:TPU:19, one launch (start us, length us, event | category | flops | bytes accessed | tf_op | source)
XLA Modules:
  0.0 166.9 jit_solution(10978928877527888520)
XLA Ops:
  1.3 1.7 copy-done
  3.9 7.2 %prep.1 = (bf16[16,6,160,128]{3,2,1,0:T(8,128)(2,1)S(1)}, bf16[4,1536,256]{2,1,0:T(8,128)(2,1)S(1)}, bf16[96,256]{1,0:T(8,128)(2,1)S(1)}, bf16[96,128]{1,0:T(8,128)(2,1)S(1)}, s32[1,1]{1,0:T(1,128)}) custom-call(s32[1,128]{1,0:T(1,128)S(1)} %get-tuple-element.79.rows_ref, s32[1,128]{1,0:T(1,128)S(1)} %get-tuple-element.78.labels_ref, ...), custom_call_target="tpu_custom_call" | custom-call | tf_op jit(solution)/shard_map/prep/pallas_call | solution.py:85
  11.9 17.8 %conv.3.refs_0_ = bf16[96,2176]{1,0:T(8,128)(2,1)S(1)} custom-call(s32[1,1]{1,0:T(1,128)} %get-tuple-element.48.nblk_ref, bf16[16,6,160,128]{3,2,1,0:T(8,128)(2,1)S(1)} %get-tuple-element.49.win_ref, bf16[4,1536,256]{2,1,0:T(8,128)(2,1)S(1)} %get-tuple-element.50.w_ref, bf16[96,256]{1,0:T(8,128)(2,1)S(1)} %get-tuple-element.51.sel_ref, ...), custom_call_target="tpu_custom_call" | custom-call | flops 22649241600 | bytes 8388608 | tf_op jit(solution)/shard_map/conv/pallas_call | solution.py:173
  31.3 9.2 %conv.4 = bf16[96,1024]{1,0:T(8,128)(2,1)S(1)} custom-call(s32[1,1]{1,0:T(1,128)} %get-tuple-element.48.nblk_ref, bf16[16,6,160,128]{3,2,1,0:T(8,128)(2,1)S(1)} %get-tuple-element.49.win_ref, bf16[4,1536,256]{2,1,0:T(8,128)(2,1)S(1)} %get-tuple-element.50.w_ref, bf16[96,256]{1,0:T(8,128)(2,1)S(1)} %get-tuple-element.51.sel_ref, f32[4,1,256]{2,1,0:T(1,128)S(1)} %bitcast.29, ...), custom_call_target="tpu_custom_call" | custom-call | flops 11324620800 | bytes 8388608 | tf_op jit(solution)/shard_map/conv/pallas_call | solution.py:173
  40.6 5.5 %collective-permute-start.3 = (bf16[96,2176]{1,0:T(8,128)(2,1)S(1)}, bf16[96,2176]{1,0:T(8,128)(2,1)S(1)}, u32[]{:S(2)}, u32[]{:S(2)}) collective-permute-start(bf16[96,2176]{1,0:T(8,128)(2,1)S(1)} %broadcast_select_fusion), channel_id=1, source_target_pairs={{0,2},{1,7},{2,4},{3,1},{4,6},{5,3},{6,0},{7,5},{8,10},{9,15},{10,... | collective-permute-start | bytes 1253384 | tf_op jit(solution)/shard_map/ppermute | solution.py:343
  47.0 2.1 %collective-permute-start.5 = (bf16[96,2176]{1,0:T(8,128)(2,1)S(1)}, bf16[96,2176]{1,0:T(8,128)(2,1)S(1)}, u32[]{:S(2)}, u32[]{:S(2)}) collective-permute-start(bf16[96,2176]{1,0:T(8,128)(2,1)S(1)} %collective-permute-done.refs_0_.refs_1_), channel_id=1, source_target_pairs={{0,6},{1,7},{2,0},{3,1},{4,2},{5,3},{6,4},{7,5},{8,14},{9,15},{10,... | collective-permute-start | bytes 1253384 | tf_op jit(solution)/shard_map/ppermute | solution.py:343
  49.1 2.9 %collective-permute-start.4 = (bf16[96,2176]{1,0:T(8,128)(2,1)S(1)}, bf16[96,2176]{1,0:T(8,128)(2,1)S(1)}, u32[]{:S(2)}, u32[]{:S(2)}) collective-permute-start(bf16[96,2176]{1,0:T(8,128)(2,1)S(1)} %collective-permute-done.refs_0_.refs_1_), channel_id=1, source_target_pairs={{0,2},{1,3},{2,4},{3,5},{4,6},{5,7},{6,0},{7,1},{8,10},{9,11},{10,... | collective-permute-start | bytes 1253384 | tf_op jit(solution)/shard_map/ppermute | solution.py:343
  52.0 1.9 %copy-done.9 = bf16[4,1536,256]{2,1,0:T(8,128)(2,1)S(1)} copy-done((bf16[4,1536,256]{2,1,0:T(8,128)(2,1)S(1)}, bf16[4,1536,256]{2,1,0:T(8,128)(2,1)}, u32[]{:S(2)}) %copy-start.9) | copy-done | bytes 3145752
  53.9 9.4 %conv.5 = bf16[96,1024]{1,0:T(8,128)(2,1)S(1)} custom-call(s32[1,1]{1,0:T(1,128)} %get-tuple-element.48.nblk_ref, bf16[16,6,160,128]{3,2,1,0:T(8,128)(2,1)S(1)} %copy-done.7, bf16[4,1536,256]{2,1,0:T(8,128)(2,1)S(1)} %copy-done.9, bf16[96,256]{1,0:T(8,128)(2,1)S(1)} %get-tuple-element.51.sel_ref, f32[4,1,256]{2,1,0:T(1,128)S(1)} %bitcast.30, ...), custom_call_target="tpu_custom_call" | custom-call | flops 11324620800 | bytes 8388608 | tf_op jit(solution)/shard_map/conv/pallas_call | solution.py:173
  63.4 1.9 %collective-permute-start.8 = (bf16[96,2048]{1,0:T(8,128)(2,1)S(1)}, bf16[96,2048]{1,0:T(8,128)(2,1)S(1)}, u32[]{:S(2)}, u32[]{:S(2)}) collective-permute-start(bf16[96,2048]{1,0:T(8,128)(2,1)S(1)} %pad_maximum_fusion.3.refs_11_), channel_id=1, source_target_pairs={{0,6},{1,7},{2,0},{3,1},{4,2},{5,3},{6,4},{7,5},{8,14},{9,15},{10,... | collective-permute-start | bytes 1179656 | tf_op jit(solution)/shard_map/ppermute | solution.py:343
  65.4 2.4 %collective-permute-start.12 = (bf16[288,2176]{1,0:T(8,128)(2,1)S(1)}, bf16[288,2176]{1,0:T(8,128)(2,1)S(1)}, u32[]{:S(2)}, u32[]{:S(2)}) collective-permute-start(bf16[288,2176]{1,0:T(8,128)(2,1)S(1)} %pad_maximum_fusion.2), channel_id=1, source_target_pairs={{0,1},{1,0},{2,3},{3,2},{4,5},{5,4},{6,7},{7,6},{8,9},{9,8},{10,11... | collective-permute-start | bytes 3760136 | tf_op jit(solution)/shard_map/ppermute | solution.py:343
  69.0 4.1 %collective-permute-done.8.refs_14_ = bf16[96,2048]{1,0:T(8,128)(2,1)S(1)} collective-permute-done((bf16[96,2048]{1,0:T(8,128)(2,1)S(1)}, bf16[96,2048]{1,0:T(8,128)(2,1)S(1)}, u32[]{:S(2)}, u32[]{:S(2)}) %collective-permute-start.8) | collective-permute-done | bytes 393248 | tf_op jit(solution)/shard_map/ppermute | solution.py:343
  74.2 3.6 %collective-permute-start.9 = (bf16[96,2048]{1,0:T(8,128)(2,1)S(1)}, bf16[96,2048]{1,0:T(8,128)(2,1)}, u32[]{:S(2)}, u32[]{:S(2)}) collective-permute-start(bf16[96,2048]{1,0:T(8,128)(2,1)S(1)} %broadcast_select_fusion.1), channel_id=1, source_target_pairs={{0,2},{1,7},{2,4},{3,1},{4,6},{5,3},{6,0},{7,5},{8,10},{9,15},{10,... | collective-permute-start | bytes 1179656 | tf_op jit(solution)/shard_map/ppermute | solution.py:343
  77.9 2.1 %collective-permute-done.6.refs_12_ = bf16[96,2048]{1,0:T(8,128)(2,1)S(1)} collective-permute-done((bf16[96,2048]{1,0:T(8,128)(2,1)S(1)}, bf16[96,2048]{1,0:T(8,128)(2,1)S(1)}, u32[]{:S(2)}, u32[]{:S(2)}) %collective-permute-start.6) | collective-permute-done | bytes 393248 | tf_op jit(solution)/shard_map/ppermute | solution.py:343
  80.0 9.0 %collective-permute-done.10.refs_7_ = bf16[96,2176]{1,0:T(8,128)(2,1)S(1)} collective-permute-done((bf16[96,2176]{1,0:T(8,128)(2,1)S(1)}, bf16[96,2176]{1,0:T(8,128)(2,1)S(1)}, u32[]{:S(2)}, u32[]{:S(2)}) %collective-permute-start.10) | collective-permute-done | bytes 417824 | tf_op jit(solution)/shard_map/ppermute | solution.py:343
  90.2 1.9 %collective-permute-start.15 = (bf16[96,2048]{1,0:T(8,128)(2,1)S(1)}, bf16[96,2048]{1,0:T(8,128)(2,1)S(1)}, u32[]{:S(2)}, u32[]{:S(2)}) collective-permute-start(bf16[96,2048]{1,0:T(8,128)(2,1)S(1)} %collective-permute-done.6.refs_12_), channel_id=1, source_target_pairs={{0,6},{1,7},{2,0},{3,1},{4,2},{5,3},{6,4},{7,5},{8,14},{9,15},{10,... | collective-permute-start | bytes 1179656 | tf_op jit(solution)/shard_map/ppermute | solution.py:343
  93.1 7.5 %collective-permute-done.15.refs_16_ = bf16[96,2048]{1,0:T(8,128)(2,1)S(1)} collective-permute-done((bf16[96,2048]{1,0:T(8,128)(2,1)S(1)}, bf16[96,2048]{1,0:T(8,128)(2,1)S(1)}, u32[]{:S(2)}, u32[]{:S(2)}) %collective-permute-start.15) | collective-permute-done | bytes 393248 | tf_op jit(solution)/shard_map/ppermute | solution.py:343
  101.8 2.2 %collective-permute-done.14.refs_15_ = bf16[96,2048]{1,0:T(8,128)(2,1)} collective-permute-done((bf16[96,2048]{1,0:T(8,128)(2,1)S(1)}, bf16[96,2048]{1,0:T(8,128)(2,1)}, u32[]{:S(2)}, u32[]{:S(2)}) %collective-permute-start.14) | collective-permute-done | bytes 393248 | tf_op jit(solution)/shard_map/ppermute | solution.py:343
  104.0 1.5 collective-permute-start.18
  108.5 19.6 %gram.1 = (f32[8,25,32,256]{3,2,1,0:T(8,128)}, f32[8,256]{1,0:T(8,128)}) custom-call(s32[2]{0:T(128)} %pad_add_fusion.me_ref, s32[136]{0:T(256)} %owner_ref.1, bf16[96,2176]{1,0:T(8,128)(2,1)} %copy-done.3, bf16[96,2176]{1,0:T(8,128)(2,1)} %copy-done.4, bf16[96,2176]{1,0:T(8,128)(2,1)} %copy-done.2, bf16[96,2176]{1,0:T(8,128)(2,1)} %copy-done.1, ...), custom_call_target="tpu_custom_call" | custom-call | flops 5000000000 | bytes 20971520 | tf_op jit(solution)/shard_map/gram/pallas_call | solution.py:286
  128.1 1.3 reduce_max.9
  130.2 36.7 %conditional.1 = (f32[20,32,256]{2,1,0:T(8,128)}, f32[32,1000]{1,0:T(8,128)}) conditional(s32[]{:T(128)} %clamp.3, (f32[]{:T(128)}, f32[8,25,32,256]{3,2,1,0:T(8,128)}, f32[]{:T(128)}) %tuple.25, (f32[]{:T(128)}, f32[8,25,32,256]{3,2,1,0:T(8,128)}, f32[]{:T(128)}) %tuple.25, (f32[]{:T(128)}, f32[]{:T(128)}, ...), branch_computations={%region_2.4_spmd, %region_4.6_spmd, %region_6.8_spmd} | conditional | flops 9625657 | bytes 22315226 | solution.py:328
  130.2 4.1 %select_convert_fusion.2 = f16[8,25,32,256]{3,2,1,0:T(8,128)(2,1)S(1)} fusion(f32[8,25,32,256]{3,2,1,0:T(8,128)} %get-tuple-element.25, f32[]{:T(128)} %get-tuple-element.26, f32[]{:T(128)} %get-tuple-element.24, pred[25]{0:T(512)(128)(4,1)S(1)} %iota_compare_fusion.2), kind=kLoop, calls=%fused_computation.11 | loop fusion | flops 4915200 | bytes 9830433 | tf_op jit(solution)/shard_map/cond/branch_2_fun/convert_element_type | solution.py:320
  134.3 30.0 %all_to_all.14 = f16[8,25,32,256]{3,2,1,0:T(8,128)(2,1)S(1)} all-to-all(f16[8,25,32,256]{3,2,1,0:T(8,128)(2,1)S(1)} %select_convert_fusion.2), channel_id=1, replica_groups=mesh['feat'=8,'tile'=16] {'feat'}, dimensions={0} | all-to-all | bytes 6553600 | tf_op jit(solution)/shard_map/cond/branch_2_fun/all_to_all | solution.py:321
  (96 shorter events, 15.3 us)
Async XLA Ops:
  29.7 10.8 %collective-permute-start.2 = (bf16[96,2176]{1,0:T(8,128)(2,1)S(1)}, bf16[96,2176]{1,0:T(8,128)(2,1)S(1)}, u32[]{:S(2)}, u32[]{:S(2)}) collective-permute-start(bf16[96,2176]{1,0:T(8,128)(2,1)S(1)} %conv.3.refs_0_), channel_id=1, source_target_pairs={{0,6},{1,7},{2,0},{3,1},{4,2},{5,3},{6,4},{7,5},{8,14},{9,15},{10,... | collective-permute-start | bytes 1253384 | tf_op jit(solution)/shard_map/ppermute | solution.py:343
  30.0 10.5 %collective-permute-start.1 = (bf16[96,2176]{1,0:T(8,128)(2,1)S(1)}, bf16[96,2176]{1,0:T(8,128)(2,1)S(1)}, u32[]{:S(2)}, u32[]{:S(2)}) collective-permute-start(bf16[96,2176]{1,0:T(8,128)(2,1)S(1)} %conv.3.refs_0_), channel_id=1, source_target_pairs={{0,2},{1,3},{2,4},{3,5},{4,6},{5,7},{6,0},{7,1},{8,10},{9,11},{10,... | collective-permute-start | bytes 1253384 | tf_op jit(solution)/shard_map/ppermute | solution.py:343
  31.3 14.9 %collective-permute-start = (bf16[96,2176]{1,0:T(8,128)(2,1)S(1)}, bf16[96,2176]{1,0:T(8,128)(2,1)S(1)}, u32[]{:S(2)}, u32[]{:S(2)}) collective-permute-start(bf16[96,2176]{1,0:T(8,128)(2,1)S(1)} %conv.3.refs_0_), channel_id=1, source_target_pairs={{0,8},{1,9},{2,10},{3,11},{4,12},{5,13},{6,14},{7,15},{8,0},{9,1},... | collective-permute-start | bytes 1253384 | tf_op jit(solution)/shard_map/ppermute | solution.py:343
  40.6 22.7 %collective-permute-start.3 = (bf16[96,2176]{1,0:T(8,128)(2,1)S(1)}, bf16[96,2176]{1,0:T(8,128)(2,1)S(1)}, u32[]{:S(2)}, u32[]{:S(2)}) collective-permute-start(bf16[96,2176]{1,0:T(8,128)(2,1)S(1)} %broadcast_select_fusion), channel_id=1, source_target_pairs={{0,2},{1,7},{2,4},{3,1},{4,6},{5,3},{6,0},{7,5},{8,10},{9,15},{10,... | collective-permute-start | bytes 1253384 | tf_op jit(solution)/shard_map/ppermute | solution.py:343
  46.3 42.7 %collective-permute-start.11 = (bf16[384,2176]{1,0:T(8,128)(2,1)S(1)}, bf16[384,2176]{1,0:T(8,128)(2,1)S(1)}, u32[]{:S(2)}, u32[]{:S(2)}) collective-permute-start(bf16[384,2176]{1,0:T(8,128)(2,1)S(1)} %pad_maximum_fusion), channel_id=1, source_target_pairs={{0,1},{1,0},{2,3},{3,2},{4,5},{5,4},{6,7},{7,6},{8,9},{9,8},{10,11... | collective-permute-start | bytes 5013512 | tf_op jit(solution)/shard_map/ppermute | solution.py:343
  47.0 16.3 %collective-permute-start.5 = (bf16[96,2176]{1,0:T(8,128)(2,1)S(1)}, bf16[96,2176]{1,0:T(8,128)(2,1)S(1)}, u32[]{:S(2)}, u32[]{:S(2)}) collective-permute-start(bf16[96,2176]{1,0:T(8,128)(2,1)S(1)} %collective-permute-done.refs_0_.refs_1_), channel_id=1, source_target_pairs={{0,6},{1,7},{2,0},{3,1},{4,2},{5,3},{6,4},{7,5},{8,14},{9,15},{10,... | collective-permute-start | bytes 1253384 | tf_op jit(solution)/shard_map/ppermute | solution.py:343
  49.1 14.3 %collective-permute-start.4 = (bf16[96,2176]{1,0:T(8,128)(2,1)S(1)}, bf16[96,2176]{1,0:T(8,128)(2,1)S(1)}, u32[]{:S(2)}, u32[]{:S(2)}) collective-permute-start(bf16[96,2176]{1,0:T(8,128)(2,1)S(1)} %collective-permute-done.refs_0_.refs_1_), channel_id=1, source_target_pairs={{0,2},{1,3},{2,4},{3,5},{4,6},{5,7},{6,0},{7,1},{8,10},{9,11},{10,... | collective-permute-start | bytes 1253384 | tf_op jit(solution)/shard_map/ppermute | solution.py:343
  63.3 42.7 %copy-start.19 = (s32[136]{0:T(256)S(1)}, s32[136]{0:T(256)}, u32[]{:S(2)}) copy-start(s32[136]{0:T(256)} %owner_ref.1) | copy-start | bytes 1636
  63.4 9.6 %collective-permute-start.8 = (bf16[96,2048]{1,0:T(8,128)(2,1)S(1)}, bf16[96,2048]{1,0:T(8,128)(2,1)S(1)}, u32[]{:S(2)}, u32[]{:S(2)}) collective-permute-start(bf16[96,2048]{1,0:T(8,128)(2,1)S(1)} %pad_maximum_fusion.3.refs_11_), channel_id=1, source_target_pairs={{0,6},{1,7},{2,0},{3,1},{4,2},{5,3},{6,4},{7,5},{8,14},{9,15},{10,... | collective-permute-start | bytes 1179656 | tf_op jit(solution)/shard_map/ppermute | solution.py:343
  65.3 8.9 %collective-permute-start.7 = (bf16[96,2048]{1,0:T(8,128)(2,1)S(1)}, bf16[96,2048]{1,0:T(8,128)(2,1)S(1)}, u32[]{:S(2)}, u32[]{:S(2)}) collective-permute-start(bf16[96,2048]{1,0:T(8,128)(2,1)S(1)} %pad_maximum_fusion.3.refs_11_), channel_id=1, source_target_pairs={{0,2},{1,3},{2,4},{3,5},{4,6},{5,7},{6,0},{7,1},{8,10},{9,11},{10,... | collective-permute-start | bytes 1179656 | tf_op jit(solution)/shard_map/ppermute | solution.py:343
  65.4 23.6 %collective-permute-start.12 = (bf16[288,2176]{1,0:T(8,128)(2,1)S(1)}, bf16[288,2176]{1,0:T(8,128)(2,1)S(1)}, u32[]{:S(2)}, u32[]{:S(2)}) collective-permute-start(bf16[288,2176]{1,0:T(8,128)(2,1)S(1)} %pad_maximum_fusion.2), channel_id=1, source_target_pairs={{0,1},{1,0},{2,3},{3,2},{4,5},{5,4},{6,7},{7,6},{8,9},{9,8},{10,11... | collective-permute-start | bytes 3760136 | tf_op jit(solution)/shard_map/ppermute | solution.py:343
  67.8 12.2 %collective-permute-start.6 = (bf16[96,2048]{1,0:T(8,128)(2,1)S(1)}, bf16[96,2048]{1,0:T(8,128)(2,1)S(1)}, u32[]{:S(2)}, u32[]{:S(2)}) collective-permute-start(bf16[96,2048]{1,0:T(8,128)(2,1)S(1)} %pad_maximum_fusion.3.refs_11_), channel_id=1, source_target_pairs={{0,8},{1,9},{2,10},{3,11},{4,12},{5,13},{6,14},{7,15},{8,0},{9,1},... | collective-permute-start | bytes 1179656 | tf_op jit(solution)/shard_map/ppermute | solution.py:343
  73.0 35.4 %copy-start.13 = (bf16[96,2048]{1,0:T(8,128)(2,1)}, bf16[96,2048]{1,0:T(8,128)(2,1)S(1)}, u32[]{:S(2)}) copy-start(bf16[96,2048]{1,0:T(8,128)(2,1)S(1)} %collective-permute-done.8.refs_14_) | copy-start | bytes 1179652
  73.0 15.9 %collective-permute-start.10 = (bf16[96,2176]{1,0:T(8,128)(2,1)S(1)}, bf16[96,2176]{1,0:T(8,128)(2,1)S(1)}, u32[]{:S(2)}, u32[]{:S(2)}) collective-permute-start(bf16[96,2176]{1,0:T(8,128)(2,1)S(1)} %collective-permute-done.3.refs_6_), channel_id=1, source_target_pairs={{0,8},{1,9},{2,10},{3,11},{4,12},{5,13},{6,14},{7,15},{8,0},{9,1},... | collective-permute-start | bytes 1253384 | tf_op jit(solution)/shard_map/ppermute | solution.py:343
  74.2 14.7 %collective-permute-start.9 = (bf16[96,2048]{1,0:T(8,128)(2,1)S(1)}, bf16[96,2048]{1,0:T(8,128)(2,1)}, u32[]{:S(2)}, u32[]{:S(2)}) collective-permute-start(bf16[96,2048]{1,0:T(8,128)(2,1)S(1)} %broadcast_select_fusion.1), channel_id=1, source_target_pairs={{0,2},{1,7},{2,4},{3,1},{4,6},{5,3},{6,0},{7,5},{8,10},{9,15},{10,... | collective-permute-start | bytes 1179656 | tf_op jit(solution)/shard_map/ppermute | solution.py:343
  89.2 19.3 %collective-permute-start.17 = (bf16[384,2048]{1,0:T(8,128)(2,1)S(1)}, bf16[384,2048]{1,0:T(8,128)(2,1)}, u32[]{:S(2)}, u32[]{:S(2)}) collective-permute-start(bf16[384,2048]{1,0:T(8,128)(2,1)S(1)} %pad_maximum_fusion.1), channel_id=1, source_target_pairs={{0,1},{1,0},{2,3},{3,2},{4,5},{5,4},{6,7},{7,6},{8,9},{9,8},{10,11... | collective-permute-start | bytes 4718600 | tf_op jit(solution)/shard_map/ppermute | solution.py:343
  90.1 15.4 %collective-permute-start.13 = (bf16[96,2176]{1,0:T(8,128)(2,1)S(1)}, bf16[96,2176]{1,0:T(8,128)(2,1)S(1)}, u32[]{:S(2)}, u32[]{:S(2)}) collective-permute-start(bf16[96,2176]{1,0:T(8,128)(2,1)S(1)} %collective-permute-done.10.refs_7_), channel_id=1, source_target_pairs={{0,1},{1,0},{2,3},{3,2},{4,5},{5,4},{6,7},{7,6},{8,9},{9,8},{10,11... | collective-permute-start | bytes 1253384 | tf_op jit(solution)/shard_map/ppermute | solution.py:343
  90.2 10.4 %collective-permute-start.15 = (bf16[96,2048]{1,0:T(8,128)(2,1)S(1)}, bf16[96,2048]{1,0:T(8,128)(2,1)S(1)}, u32[]{:S(2)}, u32[]{:S(2)}) collective-permute-start(bf16[96,2048]{1,0:T(8,128)(2,1)S(1)} %collective-permute-done.6.refs_12_), channel_id=1, source_target_pairs={{0,6},{1,7},{2,0},{3,1},{4,2},{5,3},{6,4},{7,5},{8,14},{9,15},{10,... | collective-permute-start | bytes 1179656 | tf_op jit(solution)/shard_map/ppermute | solution.py:343
  92.1 11.9 %collective-permute-start.14 = (bf16[96,2048]{1,0:T(8,128)(2,1)S(1)}, bf16[96,2048]{1,0:T(8,128)(2,1)}, u32[]{:S(2)}, u32[]{:S(2)}) collective-permute-start(bf16[96,2048]{1,0:T(8,128)(2,1)S(1)} %collective-permute-done.6.refs_12_), channel_id=1, source_target_pairs={{0,2},{1,3},{2,4},{3,5},{4,6},{5,7},{6,0},{7,1},{8,10},{9,11},{10,... | collective-permute-start | bytes 1179656 | tf_op jit(solution)/shard_map/ppermute | solution.py:343
  92.1 11.9 %collective-permute-start.16 = (bf16[96,2048]{1,0:T(8,128)(2,1)}, bf16[96,2048]{1,0:T(8,128)(2,1)}, u32[]{:S(2)}, u32[]{:S(2)}) collective-permute-start(bf16[96,2048]{1,0:T(8,128)(2,1)} %collective-permute-done.9.refs_17_), channel_id=1, source_target_pairs={{0,8},{1,9},{2,10},{3,11},{4,12},{5,13},{6,14},{7,15},{8,0},{9,1},... | collective-permute-start | bytes 1179656 | tf_op jit(solution)/shard_map/ppermute | solution.py:343
  100.6 7.8 %collective-permute-start.20 = (bf16[96,2048]{1,0:T(8,128)(2,1)}, bf16[96,2048]{1,0:T(8,128)(2,1)}, u32[]{:S(2)}, u32[]{:S(2)}) collective-permute-start(bf16[96,2048]{1,0:T(8,128)(2,1)} %collective-permute-done.9.refs_17_), channel_id=1, source_target_pairs={{0,1},{1,0},{2,3},{3,2},{4,5},{5,4},{6,7},{7,6},{8,9},{9,8},{10,11... | collective-permute-start | bytes 1179656 | tf_op jit(solution)/shard_map/ppermute | solution.py:343
  104.0 4.4 %collective-permute-start.18 = (bf16[96,2048]{1,0:T(8,128)(2,1)}, bf16[96,2048]{1,0:T(8,128)(2,1)}, u32[]{:S(2)}, u32[]{:S(2)}) collective-permute-start(bf16[96,2048]{1,0:T(8,128)(2,1)} %collective-permute-done.14.refs_15_), channel_id=1, source_target_pairs={{0,1},{1,0},{2,3},{3,2},{4,5},{5,4},{6,7},{7,6},{8,9},{9,8},{10,11... | collective-permute-start | bytes 1179656 | tf_op jit(solution)/shard_map/ppermute | solution.py:343
  105.5 3.0 %collective-permute-start.19 = (bf16[96,2048]{1,0:T(8,128)(2,1)S(1)}, bf16[96,2048]{1,0:T(8,128)(2,1)}, u32[]{:S(2)}, u32[]{:S(2)}) collective-permute-start(bf16[96,2048]{1,0:T(8,128)(2,1)S(1)} %collective-permute-done.15.refs_16_), channel_id=1, source_target_pairs={{0,1},{1,0},{2,3},{3,2},{4,5},{5,4},{6,7},{7,6},{8,9},{9,8},{10,11... | collective-permute-start | bytes 1179656 | tf_op jit(solution)/shard_map/ppermute | solution.py:343
  105.6 2.9 %collective-permute-start.21 = (bf16[96,2048]{1,0:T(8,128)(2,1)}, bf16[96,2048]{1,0:T(8,128)(2,1)}, u32[]{:S(2)}, u32[]{:S(2)}) collective-permute-start(bf16[96,2048]{1,0:T(8,128)(2,1)} %collective-permute-done.16.refs_18_), channel_id=1, source_target_pairs={{0,1},{1,0},{2,3},{3,2},{4,5},{5,4},{6,7},{7,6},{8,9},{9,8},{10,11... | collective-permute-start | bytes 1179656 | tf_op jit(solution)/shard_map/ppermute | solution.py:343
  (23 other events, 362.6 us)

commit v5 on v3

--- a/solution.py
+++ b/solution.py
@@ -10,6 +10,7 @@
 ROWS = 96
 BLK = 16
 NBLK = 6
+WIDE = 112
 BF = jnp.bfloat16
 F32 = jnp.float32
 LAG = 3
@@ -19,7 +20,7 @@
     return lax.dot_general(a, b, dims, preferred_element_type=F32)
 
 
-def prep_kernel(rows_ref, labels_ref, filt_ref, img_hbm, win_ref, w_ref, sel_ref, lab_ref, nblk_ref, img_ref, x_ref, pick_ref, flat_ref, sem):
+def prep_kernel(rows_ref, labels_ref, filt_ref, img_hbm, win_ref, half_ref, w_ref, sel_ref, lab_ref, nblk_ref, img_ref, x_ref, pick_ref, flat_ref, sem):
     fetch = pltpu.make_async_copy(img_hbm, img_ref, sem)
     fetch.start()
     flat_ref[...] = jnp.zeros_like(flat_ref)
@@ -49,16 +50,20 @@
     upto = jnp.where(low <= high, 1.0, 0.0).astype(BF)
     rank = dot(jnp.broadcast_to(used, (16, 128)).astype(BF), upto)[0:1] - 1.0
     rank = rank.astype(jnp.int32)
-    compact = jnp.where((subs == rank) & (used > 0.0), 1.0, 0.0).astype(BF)
+    total = jnp.sum(used).astype(jnp.int32)
+    whole = (total + 7) // BLK
+    nblk_ref[0, 0] = whole
+    nblk_ref[0, 1] = total - whole * BLK
+    deep = lax.broadcasted_iota(jnp.int32, (WIDE, 128), 0)
+    deep = jnp.where(deep < ROWS, deep, jnp.where(deep < ROWS + 8, deep - ROWS + BLK * whole, -1))
+    take = jnp.where((deep == rank) & (used > 0.0), 1.0, 0.0).astype(BF)
+    compact = take[:ROWS]
     sel_ref[:, :ROWS] = dot(jnp.where(hit, 1.0, 0.0).astype(BF), compact, (((1,), (1,)), ((), ()))).astype(BF)
     sel_ref[:, ROWS:] = jnp.zeros((ROWS, 256 - ROWS), BF)
-    total = jnp.sum(used).astype(jnp.int32)
-    nblk_ref[0, 0] = (total + BLK - 1) // BLK
     label = jnp.sum(jnp.where(hit, labels_ref[...], 0), axis=1, keepdims=True)
     coarse = label // 8
     fine = label - coarse * 8
     lab_ref[...] = jnp.where(lanes == 0, coarse, jnp.where(lanes == 1, fine, 0)).astype(BF)
-    take = compact[:, :ROWS]
     col = lax.broadcasted_iota(jnp.int32, (1, 1280), 1)
     within = col % 32
     source = (col % 128) // 32 * 192 + 18 * (col // 128) + within
@@ -67,16 +72,21 @@
     pick_ref[...] = jnp.where(place == source, 1.0, 0.0).astype(BF)
     fetch.wait()
     for part in range(16):
-        x_ref[part * ROWS:(part + 1) * ROWS, :] = dot(take, img_ref[:, part * 768:(part + 1) * 768]).astype(BF)
+        x_ref[part * WIDE:(part + 1) * WIDE, :] = dot(take[:, :ROWS], img_ref[:, part * 768:(part + 1) * 768]).astype(BF)
 
     @pl.loop(0, 5)
     def _(n):
-        tile = dot(x_ref[...], pick_ref[:, pl.ds(pl.multiple_of(n * 256, 256), 256)]).astype(BF)
+        fine = dot(x_ref[...], pick_ref[:, pl.ds(pl.multiple_of(n * 256, 256), 256)])
+        tile = fine.astype(BF)
+        for part in range(16):
+            row = part * WIDE + ROWS
+            pair = jnp.concatenate([fine[row:row + 8, :128], fine[row:row + 8, 128:]], axis=0)
+            half_ref[part, pl.ds(pl.multiple_of(n * 16, 16), 16), :] = pair.astype(BF)
         for h in range(2):
             at = pl.multiple_of((2 * n + h) * 16, 16)
             for part in range(16):
                 for b in range(NBLK):
-                    row = part * ROWS + b * 16
+                    row = part * WIDE + b * 16
                     win_ref[part, b, pl.ds(at, 16), :] = tile[row:row + 16, h * 128:(h + 1) * 128]
 
 
@@ -86,16 +96,17 @@
         prep_kernel,
         out_shape=(
             jax.ShapeDtypeStruct((16, NBLK, 160, 128), BF),
+            jax.ShapeDtypeStruct((16, 80, 128), BF),
             jax.ShapeDtypeStruct((4, 1536, 256), BF),
             jax.ShapeDtypeStruct((ROWS, 256), BF),
             jax.ShapeDtypeStruct((ROWS, 128), BF),
-            jax.ShapeDtypeStruct((1, 1), jnp.int32),
+            jax.ShapeDtypeStruct((1, 2), jnp.int32),
         ),
         in_specs=[vmem, vmem, vmem, pl.BlockSpec(memory_space=pl.ANY)],
-        out_specs=(vmem, vmem, vmem, vmem, pl.BlockSpec(memory_space=pltpu.SMEM)),
+        out_specs=(vmem, vmem, vmem, vmem, vmem, pl.BlockSpec(memory_space=pltpu.SMEM)),
         scratch_shapes=[
             pltpu.VMEM((ROWS, 12288), BF),
-            pltpu.VMEM((16 * ROWS, 768), BF),
+            pltpu.VMEM((16 * WIDE, 768), BF),
             pltpu.VMEM((768, 1280), BF),
             pltpu.VMEM((128, 1024), F32),
             pltpu.SemaphoreType.DMA,
@@ -105,7 +116,7 @@
     )(jnp.pad(row_list, (0, 32)).reshape(1, 128), jnp.pad(labels, (0, 32)).reshape(1, 128), filters, images)
 
 
-def conv_kernel(first, count, nblk_ref, win_ref, w_ref, sel_ref, bias_ref, lab_ref, *refs):
+def conv_kernel(first, count, nblk_ref, win_ref, half_ref, w_ref, sel_ref, bias_ref, lab_ref, *refs):
     out_ref, uniq_ref = refs[-2:]
     uniq_ref[...] = jnp.zeros_like(uniq_ref)
     if out_ref.shape[1] > count * 1024:
@@ -143,6 +154,39 @@
                 mean = (total[qr][m] + 225.0 * bias) * (1.0 / 225.0)
                 uniq_ref[pl.ds(at, 16), q * 256:(q + 1) * 256] = mean.astype(BF)
 
+    def half_block(nc, b, bias, floor, acc):
+        total = [[jnp.zeros((8, 256), F32) for _ in range(2)] for _ in range(2)]
+        low = floor[:8]
+
+        def take(k):
+            d, j = k // 8, k % 8
+            for m in range(2):
+                w = 2 * j + m
+                if w < 15:
+                    qr = 0 if w <= (7 if d < 3 else 6) else 1
+                    got = jnp.maximum(pltpu.matmul_pop(acc[m][k % 8]).reshape(10, 8, 256), low[None])
+                    total[qr][0] = total[qr][0] + jnp.sum(got[:5], axis=0)
+                    total[qr][1] = total[qr][1] + jnp.sum(got[5:], axis=0)
+
+        for k in range(48):
+            d, j = k // 8, k % 8
+            if j == 0:
+                for m in range(2):
+                    pltpu.matmul_push_rhs(w_ref[first + nc, d * 256:(d + 1) * 256, :], d % 2, m)
+            for m in range(2):
+                w = 2 * j + m
+                if w < 15:
+                    lhs = jnp.concatenate([half_ref[w], half_ref[w + 1]], axis=1)
+                    pltpu.matmul_acc_lhs(acc[m][k % 8], lhs, load_staged_rhs=d % 2 if j == 0 else None)
+            if k >= LAG:
+                take(k - LAG)
+        for k in range(48 - LAG, 48):
+            take(k)
+        at = pl.multiple_of(b * 16, 16)
+        for q in range(4):
+            mean = (total[q // 2][q % 2] + 225.0 * bias) * (1.0 / 225.0)
+            uniq_ref[pl.ds(at, 16), q * 256:(q + 1) * 256] = jnp.concatenate([mean, jnp.zeros_like(mean)], axis=0).astype(BF)
+
     def scoped(*accs):
         @pl.loop(0, count)
         def _(nc):
@@ -152,6 +196,10 @@
             @pl.loop(0, nblk_ref[0, 0])
             def _(b):
                 block(nc, b, bias, floor, (accs[:8], accs[8:16]))
+
+            @pl.when(nblk_ref[0, 1] > 0)
+            def _():
+                half_block(nc, nblk_ref[0, 0], bias, floor, (accs[:8], accs[8:16]))
 
             for m in range(2):
                 for qr in range(2):
@@ -169,18 +217,18 @@
     )
 
 
-def conv(first, count, nblk, win, w, sel, bias, lab, extra, after=()):
+def conv(first, count, nblk, win, half, w, sel, bias, lab, extra, after=()):
     return pl.pallas_call(
         functools.partial(conv_kernel, first, count),
         out_shape=jax.ShapeDtypeStruct((ROWS, count * 1024 + extra), BF),
-        in_specs=[pl.BlockSpec(memory_space=pltpu.SMEM)] + [pl.BlockSpec(memory_space=pltpu.VMEM)] * 5
+        in_specs=[pl.BlockSpec(memory_space=pltpu.SMEM)] + [pl.BlockSpec(memory_space=pltpu.VMEM)] * 6
         + [pl.BlockSpec(memory_space=pl.ANY)] * len(after),
         out_specs=pl.BlockSpec(memory_space=pltpu.VMEM),
         scratch_shapes=[pltpu.VMEM((256, 1024), BF)],
         compiler_params=pltpu.CompilerParams(vmem_limit_bytes=40 * 2**20),
         cost_estimate=pl.CostEstimate(flops=count * 2 * 86400 * 256 * 256, bytes_accessed=8 * 2**20, transcendentals=0),
         name="conv",
-    )(nblk, win, w, sel, bias, lab, *after)
+    )(nblk, win, half, w, sel, bias, lab, *after)
 
 
 TILES = 16
@@ -369,13 +417,13 @@
 
 
 def body(images, row_list, labels, filters, bias, tile_owner):
-    win, w, sel, lab, nblk = prep(images, row_list, labels, filters)
+    win, half, w, sel, lab, nblk = prep(images, row_list, labels, filters)
     bias4 = bias.reshape(4, 1, 256)
-    own_a = conv(0, 2, nblk, win, w, sel, bias4, lab, 128)
+    own_a = conv(0, 2, nblk, win, half, w, sel, bias4, lab, 128)
     first_a = spread_first(own_a)
-    own_b2 = conv(2, 1, nblk, win, w, sel, bias4, lab, 0, (own_a,))
+    own_b2 = conv(2, 1, nblk, win, half, w, sel, bias4, lab, 0, (own_a,))
     second_a = spread_second(first_a)
-    own_b3 = conv(3, 1, nblk, win, w, sel, bias4, lab, 0, first_a[1:])
+    own_b3 = conv(3, 1, nblk, win, half, w, sel, bias4, lab, 0, first_a[1:])
     own_b = jnp.concatenate([own_b2, own_b3], axis=1)
     own_b, far, over_left, over_right = lax.optimization_barrier((own_b,) + second_a[:3])
     second_a = (far, over_left, over_right, second_a[3])

time: 166 us -> 169 us (1.018)
  the two profiles are of different devices: /device:TPU:4 before, /device:TPU:1 now
where the time goes in v5:
time: 169 us
  Pallas kernels  63.2 us (37%)
  starting transfers between devices  35.2 us (21%)
  blocking collectives  31.2 us (18%)
  waiting for transfers between devices  18.2 us (11%)
  other arithmetic  10.6 us (6%)
  local copies, waits for them, and re-layouts  7.67 us (5%)
  between operations  3.08 us (2%)
    pallas_call x3, Pallas kernels, conv(): pl.pallas_call(functools.partial(conv_kernel, first, count), out_shape=ja...  36.1 us
    ppermute x20, starting transfers between devices, send(): return lax.ppermute(block, 'tile', perm)  35.2 us
    all_to_all x1, blocking collectives, some(): got = lax.all_to_all(coded, 'feat', split_axis=0, concat_axis=0, tiled=True)  31.2 us
    pallas_call x1, Pallas kernels, gram(): pl.pallas_call(gram_kernel, out_shape=(jax.ShapeDtypeStruct((FEAT, SLOTS,...  19.4 us
    ppermute x20, waiting for transfers between devices, send(): return lax.ppermute(block, 'tile', perm)  18.2 us
    pallas_call x1, Pallas kernels, prep(): pl.pallas_call(prep_kernel, out_shape=(jax.ShapeDtypeStruct((16, NBLK, 16...  7.75 us
    unnamed x50, local copies, waits for them, and re-layouts  5.33 us
    convert_element_type x1, other arithmetic, some(): coded = jnp.where(note, exponent, used * scale).astype(HALF)  4.08 us
  transfers between devices with their start and end apart: 20, of which 7 were waited for; matrix products, arithmetic and copies ran while one was open for 3% of the time, Pallas kernels for 11%

profile of v5, /device:TPU:1, one launch (start us, length us, event | category | flops | bytes accessed | tf_op | source)
XLA Modules:
  0.0 169.3 jit_solution(10667322386005707902)
XLA Ops:
  3.9 7.8 %prep.1 = (bf16[16,6,160,128]{3,2,1,0:T(8,128)(2,1)S(1)}, bf16[16,80,128]{2,1,0:T(8,128)(2,1)S(1)}, bf16[4,1536,256]{2,1,0:T(8,128)(2,1)S(1)}, bf16[96,256]{1,0:...) custom-call(s32[1,128]{1,0:T(1,128)S(1)} %get-tuple-element.65.rows_ref, ...), custom_call_target="tpu_custom_call" | custom-call | tf_op jit(solution)/shard_map/prep/pallas_call | solution.py:95
  12.5 17.8 %conv.3.refs_0_ = bf16[96,2176]{1,0:T(8,128)(2,1)S(1)} custom-call(s32[1,2]{1,0:T(1,128)S(1)} %get-tuple-element.41.nblk_ref, bf16[16,6,160,128]{3,2,1,0:T(8,128)(2,1)S(1)} %get-tuple-element.42.win_ref, bf16[16,80,128]{2,1,0:T(8,128)(2,1)S(1)} %get-tuple-element.43.half_ref, bf16[4,1536,256]{2,1,0:T(8,128)(2,1)S(1)} %get-tuple-element.44.w_ref, ...), custom_call_target="tpu_custom_call" | custom-call | flops 22649241600 | bytes 8388608 | tf_op jit(solution)/shard_map/conv/pallas_call | solution.py:221
  30.2 3.4 %collective-permute-start.2 = (bf16[96,2176]{1,0:T(8,128)(2,1)S(1)}, bf16[96,2176]{1,0:T(8,128)(2,1)S(1)}, u32[]{:S(2)}, u32[]{:S(2)}) collective-permute-start(bf16[96,2176]{1,0:T(8,128)(2,1)S(1)} %conv.3.refs_0_), channel_id=1, source_target_pairs={{0,6},{1,7},{2,0},{3,1},{4,2},{5,3},{6,4},{7,5},{8,14},{9,15},{10,... | collective-permute-start | bytes 1253384 | tf_op jit(solution)/shard_map/ppermute | solution.py:389
  33.6 2.9 %collective-permute-start = (bf16[96,2176]{1,0:T(8,128)(2,1)S(1)}, bf16[96,2176]{1,0:T(8,128)(2,1)S(1)}, u32[]{:S(2)}, u32[]{:S(2)}) collective-permute-start(bf16[96,2176]{1,0:T(8,128)(2,1)S(1)} %conv.3.refs_0_), channel_id=1, source_target_pairs={{0,8},{1,9},{2,10},{3,11},{4,12},{5,13},{6,14},{7,15},{8,0},{9,1},... | collective-permute-start | bytes 1253384 | tf_op jit(solution)/shard_map/ppermute | solution.py:389
  36.5 9.2 %conv.4 = bf16[96,1024]{1,0:T(8,128)(2,1)S(1)} custom-call(s32[1,2]{1,0:T(1,128)S(1)} %get-tuple-element.41.nblk_ref, bf16[16,6,160,128]{3,2,1,0:T(8,128)(2,1)S(1)} %get-tuple-element.42.win_ref, bf16[16,80,128]{2,1,0:T(8,128)(2,1)S(1)} %get-tuple-element.43.half_ref, bf16[4,1536,256]{2,1,0:T(8,128)(2,1)S(1)} %get-tuple-element.44.w_ref, ...), custom_call_target="tpu_custom_call" | custom-call | flops 11324620800 | bytes 8388608 | tf_op jit(solution)/shard_map/conv/pallas_call | solution.py:221
  45.8 3.2 %collective-permute-start.3 = (bf16[96,2176]{1,0:T(8,128)(2,1)S(1)}, bf16[96,2176]{1,0:T(8,128)(2,1)S(1)}, u32[]{:S(2)}, u32[]{:S(2)}) collective-permute-start(bf16[96,2176]{1,0:T(8,128)(2,1)S(1)} %broadcast_select_fusion.1), channel_id=1, source_target_pairs={{0,2},{1,7},{2,4},{3,1},{4,6},{5,3},{6,0},{7,5},{8,10},{9,15},{10,... | collective-permute-start | bytes 1253384 | tf_op jit(solution)/shard_map/ppermute | solution.py:389
  50.4 2.6 %collective-permute-start.7 = (bf16[384,2176]{1,0:T(8,128)(2,1)}, bf16[384,2176]{1,0:T(8,128)(2,1)}, u32[]{:S(2)}, u32[]{:S(2)}) collective-permute-start(bf16[384,2176]{1,0:T(8,128)(2,1)} %pad_maximum_fusion), channel_id=1, source_target_pairs={{0,1},{1,0},{2,3},{3,2},{4,5},{5,4},{6,7},{7,6},{8,9},{9,8},{10,11... | collective-permute-start | bytes 5013512 | tf_op jit(solution)/shard_map/ppermute | solution.py:389
  54.5 1.9 %copy-done.9 = bf16[4,1536,256]{2,1,0:T(8,128)(2,1)S(1)} copy-done((bf16[4,1536,256]{2,1,0:T(8,128)(2,1)S(1)}, bf16[4,1536,256]{2,1,0:T(8,128)(2,1)}, u32[]{:S(2)}) %copy-start.9) | copy-done | bytes 3145752
  56.4 9.2 %conv.5 = bf16[96,1024]{1,0:T(8,128)(2,1)S(1)} custom-call(s32[1,2]{1,0:T(1,128)S(1)} %get-tuple-element.41.nblk_ref, bf16[16,6,160,128]{3,2,1,0:T(8,128)(2,1)S(1)} %copy-done.7, bf16[16,80,128]{2,1,0:T(8,128)(2,1)S(1)} %get-tuple-element.43.half_ref, bf16[4,1536,256]{2,1,0:T(8,128)(2,1)S(1)} %copy-done.9, bf16[96,256]{1,0:T(8,128)(2,1)S(1)} %get-tuple-element.45.sel_ref, ...), custom_call_target="tpu_custom_call" | custom-call | flops 11324620800 | bytes 8388608 | tf_op jit(solution)/shard_map/conv/pallas_call | solution.py:221
  69.2 2.3 %collective-permute-start.6 = (bf16[96,2176]{1,0:T(8,128)(2,1)S(1)}, bf16[96,2176]{1,0:T(8,128)(2,1)S(1)}, u32[]{:S(2)}, u32[]{:S(2)}) collective-permute-start(bf16[96,2176]{1,0:T(8,128)(2,1)S(1)} %broadcast_select_fusion), channel_id=1, source_target_pairs={{0,2},{1,7},{2,4},{3,1},{4,6},{5,3},{6,0},{7,5},{8,10},{9,15},{10,... | collective-permute-start | bytes 1253384 | tf_op jit(solution)/shard_map/ppermute | solution.py:389
  71.4 4.4 %collective-permute-done.12.refs_14_ = bf16[96,2048]{1,0:T(8,128)(2,1)S(1)} collective-permute-done((bf16[96,2048]{1,0:T(8,128)(2,1)S(1)}, bf16[96,2048]{1,0:T(8,128)(2,1)S(1)}, u32[]{:S(2)}, u32[]{:S(2)}) %collective-permute-start.12) | collective-permute-done | bytes 393248 | tf_op jit(solution)/shard_map/ppermute | solution.py:389
  75.8 2.4 %collective-permute-done.11.refs_13_ = bf16[96,2048]{1,0:T(8,128)(2,1)S(1)} collective-permute-done((bf16[96,2048]{1,0:T(8,128)(2,1)S(1)}, bf16[96,2048]{1,0:T(8,128)(2,1)S(1)}, u32[]{:S(2)}, u32[]{:S(2)}) %collective-permute-start.11) | collective-permute-done | bytes 393248 | tf_op jit(solution)/shard_map/ppermute | solution.py:389
  78.7 2.2 %collective-permute-start.14 = (bf16[96,2048]{1,0:T(8,128)(2,1)S(1)}, bf16[96,2048]{1,0:T(8,128)(2,1)S(1)}, u32[]{:S(2)}, u32[]{:S(2)}) collective-permute-start(bf16[96,2048]{1,0:T(8,128)(2,1)S(1)} %collective-permute-done.10.refs_12_), channel_id=1, source_target_pairs={{0,6},{1,7},{2,0},{3,1},{4,2},{5,3},{6,4},{7,5},{8,14},{9,15},{10,... | collective-permute-start | bytes 1179656 | tf_op jit(solution)/shard_map/ppermute | solution.py:389
  81.6 2.6 %collective-permute-start.17 = (bf16[384,2048]{1,0:T(8,128)(2,1)S(1)}, bf16[384,2048]{1,0:T(8,128)(2,1)}, u32[]{:S(2)}, u32[]{:S(2)}) collective-permute-start(bf16[384,2048]{1,0:T(8,128)(2,1)S(1)} %pad_maximum_fusion.1), channel_id=1, source_target_pairs={{0,1},{1,0},{2,3},{3,2},{4,5},{5,4},{6,7},{7,6},{8,9},{9,8},{10,11... | collective-permute-start | bytes 4718600 | tf_op jit(solution)/shard_map/ppermute | solution.py:389
  85.4 2.1 %collective-permute-done.15.refs_17_ = bf16[96,2048]{1,0:T(8,128)(2,1)S(1)} collective-permute-done((bf16[96,2048]{1,0:T(8,128)(2,1)S(1)}, bf16[96,2048]{1,0:T(8,128)(2,1)S(1)}, u32[]{:S(2)}, u32[]{:S(2)}) %collective-permute-start.15) | collective-permute-done | bytes 393248 | tf_op jit(solution)/shard_map/ppermute | solution.py:389
  87.5 5.0 %collective-permute-start.8 = (bf16[288,2176]{1,0:T(8,128)(2,1)}, bf16[288,2176]{1,0:T(8,128)(2,1)}, u32[]{:S(2)}, u32[]{:S(2)}) collective-permute-start(bf16[288,2176]{1,0:T(8,128)(2,1)} %pad_maximum_fusion.2), channel_id=1, source_target_pairs={{0,1},{1,0},{2,3},{3,2},{4,5},{5,4},{6,7},{7,6},{8,9},{9,8},{10,11... | collective-permute-start | bytes 3760136 | tf_op jit(solution)/shard_map/ppermute | solution.py:389
  92.5 1.7 collective-permute-done.14.refs_16_
  94.4 3.1 %collective-permute-start.18 = (bf16[288,2048]{1,0:T(8,128)(2,1)S(1)}, bf16[288,2048]{1,0:T(8,128)(2,1)}, u32[]{:S(2)}, u32[]{:S(2)}) collective-permute-start(bf16[288,2048]{1,0:T(8,128)(2,1)S(1)} %pad_maximum_fusion.3), channel_id=1, source_target_pairs={{0,1},{1,0},{2,3},{3,2},{4,5},{5,4},{6,7},{7,6},{8,9},{9,8},{10,11... | collective-permute-start | bytes 3538952 | tf_op jit(solution)/shard_map/ppermute | solution.py:389
  97.9 6.7 %collective-permute-done.16.refs_18_ = bf16[96,2048]{1,0:T(8,128)(2,1)} collective-permute-done((bf16[96,2048]{1,0:T(8,128)(2,1)S(1)}, bf16[96,2048]{1,0:T(8,128)(2,1)}, u32[]{:S(2)}, u32[]{:S(2)}) %collective-permute-start.16) | collective-permute-done | bytes 393248 | tf_op jit(solution)/shard_map/ppermute | solution.py:389
  104.6 2.5 %collective-permute-start.19 = (bf16[96,2048]{1,0:T(8,128)(2,1)}, bf16[96,2048]{1,0:T(8,128)(2,1)}, u32[]{:S(2)}, u32[]{:S(2)}) collective-permute-start(bf16[96,2048]{1,0:T(8,128)(2,1)} %collective-permute-done.16.refs_18_), channel_id=1, source_target_pairs={{0,1},{1,0},{2,3},{3,2},{4,5},{5,4},{6,7},{7,6},{8,9},{9,8},{10,11... | collective-permute-start | bytes 1179656 | tf_op jit(solution)/shard_map/ppermute | solution.py:389
  109.9 19.4 %gram.1 = (f32[8,25,32,256]{3,2,1,0:T(8,128)}, f32[8,256]{1,0:T(8,128)}) custom-call(s32[2]{0:T(128)} %pad_add_fusion.me_ref, s32[136]{0:T(256)} %owner_ref.1, bf16[96,2176]{1,0:T(8,128)(2,1)} %copy-done.3, bf16[96,2176]{1,0:T(8,128)(2,1)} %copy-done.4, bf16[96,2176]{1,0:T(8,128)(2,1)} %copy-done.2, bf16[96,2176]{1,0:T(8,128)(2,1)} %copy-done.1, ...), custom_call_target="tpu_custom_call" | custom-call | flops 5000000000 | bytes 20971520 | tf_op jit(solution)/shard_map/gram/pallas_call | solution.py:332
  131.3 38.0 %conditional.1 = (f32[20,32,256]{2,1,0:T(8,128)}, f32[32,1000]{1,0:T(8,128)}) conditional(s32[]{:T(128)} %clamp.3, (f32[]{:T(128)}, f32[8,25,32,256]{3,2,1,0:T(8,128)}, f32[]{:T(128)}) %tuple.21, (f32[]{:T(128)}, f32[8,25,32,256]{3,2,1,0:T(8,128)}, f32[]{:T(128)}) %tuple.21, (f32[]{:T(128)}, f32[]{:T(128)}, ...), branch_computations={%region_2.4_spmd, %region_4.6_spmd, %region_6.8_spmd} | conditional | flops 9625657 | bytes 22315226 | solution.py:374
  131.4 4.1 %select_convert_fusion.2 = f16[8,25,32,256]{3,2,1,0:T(8,128)(2,1)S(1)} fusion(f32[8,25,32,256]{3,2,1,0:T(8,128)} %get-tuple-element.25, f32[]{:T(128)} %get-tuple-element.26, f32[]{:T(128)} %get-tuple-element.24, pred[25]{0:T(512)(128)(4,1)S(1)} %iota_compare_fusion.2), kind=kLoop, calls=%fused_computation.11 | loop fusion | flops 4915200 | bytes 9830433 | tf_op jit(solution)/shard_map/cond/branch_2_fun/convert_element_type | solution.py:366
  135.5 31.2 %all_to_all.14 = f16[8,25,32,256]{3,2,1,0:T(8,128)(2,1)S(1)} all-to-all(f16[8,25,32,256]{3,2,1,0:T(8,128)(2,1)S(1)} %select_convert_fusion.2), channel_id=1, replica_groups=mesh['feat'=8,'tile'=16] {'feat'}, dimensions={0} | all-to-all | bytes 6553600 | tf_op jit(solution)/shard_map/cond/branch_2_fun/all_to_all | solution.py:367
  (95 shorter events, 18.6 us)
Async XLA Ops:
  11.7 24.8 %copy-start.6 = (bf16[16,6,160,128]{3,2,1,0:T(8,128)(2,1)}, bf16[16,6,160,128]{3,2,1,0:T(8,128)(2,1)S(1)}, u32[]{:S(2)}) copy-start(bf16[16,6,160,128]{3,2,1,0:T(8,128)(2,1)S(1)} %get-tuple-element.42.win_ref) | copy-start | bytes 11796484
  11.7 24.8 %copy-start.8 = (bf16[4,1536,256]{2,1,0:T(8,128)(2,1)}, bf16[4,1536,256]{2,1,0:T(8,128)(2,1)S(1)}, u32[]{:S(2)}) copy-start(bf16[4,1536,256]{2,1,0:T(8,128)(2,1)S(1)} %get-tuple-element.44.w_ref) | copy-start | bytes 9437188
  12.5 24.1 %copy-start.11 = (f32[1024]{0:T(1024)S(1)}, f32[1024]{0:T(1024)}, u32[]{:S(2)}) copy-start(f32[1024]{0:T(1024)} %param.13) | copy-start | bytes 12292
  30.2 15.5 %collective-permute-start.2 = (bf16[96,2176]{1,0:T(8,128)(2,1)S(1)}, bf16[96,2176]{1,0:T(8,128)(2,1)S(1)}, u32[]{:S(2)}, u32[]{:S(2)}) collective-permute-start(bf16[96,2176]{1,0:T(8,128)(2,1)S(1)} %conv.3.refs_0_), channel_id=1, source_target_pairs={{0,6},{1,7},{2,0},{3,1},{4,2},{5,3},{6,4},{7,5},{8,14},{9,15},{10,... | collective-permute-start | bytes 1253384 | tf_op jit(solution)/shard_map/ppermute | solution.py:389
  33.6 12.1 %collective-permute-start.1 = (bf16[96,2176]{1,0:T(8,128)(2,1)S(1)}, bf16[96,2176]{1,0:T(8,128)(2,1)S(1)}, u32[]{:S(2)}, u32[]{:S(2)}) collective-permute-start(bf16[96,2176]{1,0:T(8,128)(2,1)S(1)} %conv.3.refs_0_), channel_id=1, source_target_pairs={{0,2},{1,3},{2,4},{3,5},{4,6},{5,7},{6,0},{7,1},{8,10},{9,11},{10,... | collective-permute-start | bytes 1253384 | tf_op jit(solution)/shard_map/ppermute | solution.py:389
  33.6 15.4 %collective-permute-start = (bf16[96,2176]{1,0:T(8,128)(2,1)S(1)}, bf16[96,2176]{1,0:T(8,128)(2,1)S(1)}, u32[]{:S(2)}, u32[]{:S(2)}) collective-permute-start(bf16[96,2176]{1,0:T(8,128)(2,1)S(1)} %conv.3.refs_0_), channel_id=1, source_target_pairs={{0,8},{1,9},{2,10},{3,11},{4,12},{5,13},{6,14},{7,15},{8,0},{9,1},... | collective-permute-start | bytes 1253384 | tf_op jit(solution)/shard_map/ppermute | solution.py:389
  45.8 19.8 %collective-permute-start.3 = (bf16[96,2176]{1,0:T(8,128)(2,1)S(1)}, bf16[96,2176]{1,0:T(8,128)(2,1)S(1)}, u32[]{:S(2)}, u32[]{:S(2)}) collective-permute-start(bf16[96,2176]{1,0:T(8,128)(2,1)S(1)} %broadcast_select_fusion.1), channel_id=1, source_target_pairs={{0,2},{1,7},{2,4},{3,1},{4,6},{5,3},{6,0},{7,5},{8,10},{9,15},{10,... | collective-permute-start | bytes 1253384 | tf_op jit(solution)/shard_map/ppermute | solution.py:389
  50.4 59.5 %collective-permute-start.7 = (bf16[384,2176]{1,0:T(8,128)(2,1)}, bf16[384,2176]{1,0:T(8,128)(2,1)}, u32[]{:S(2)}, u32[]{:S(2)}) collective-permute-start(bf16[384,2176]{1,0:T(8,128)(2,1)} %pad_maximum_fusion), channel_id=1, source_target_pairs={{0,1},{1,0},{2,3},{3,2},{4,5},{5,4},{6,7},{7,6},{8,9},{9,8},{10,11... | collective-permute-start | bytes 5013512 | tf_op jit(solution)/shard_map/ppermute | solution.py:389
  53.0 12.6 %collective-permute-start.5 = (bf16[96,2176]{1,0:T(8,128)(2,1)S(1)}, bf16[96,2176]{1,0:T(8,128)(2,1)S(1)}, u32[]{:S(2)}, u32[]{:S(2)}) collective-permute-start(bf16[96,2176]{1,0:T(8,128)(2,1)S(1)} %collective-permute-done.refs_0_.refs_1_), channel_id=1, source_target_pairs={{0,6},{1,7},{2,0},{3,1},{4,2},{5,3},{6,4},{7,5},{8,14},{9,15},{10,... | collective-permute-start | bytes 1253384 | tf_op jit(solution)/shard_map/ppermute | solution.py:389
  53.0 13.0 %collective-permute-start.4 = (bf16[96,2176]{1,0:T(8,128)(2,1)S(1)}, bf16[96,2176]{1,0:T(8,128)(2,1)S(1)}, u32[]{:S(2)}, u32[]{:S(2)}) collective-permute-start(bf16[96,2176]{1,0:T(8,128)(2,1)S(1)} %collective-permute-done.refs_0_.refs_1_), channel_id=1, source_target_pairs={{0,2},{1,3},{2,4},{3,5},{4,6},{5,7},{6,0},{7,1},{8,10},{9,11},{10,... | collective-permute-start | bytes 1253384 | tf_op jit(solution)/shard_map/ppermute | solution.py:389
  66.0 9.9 %collective-permute-start.12 = (bf16[96,2048]{1,0:T(8,128)(2,1)S(1)}, bf16[96,2048]{1,0:T(8,128)(2,1)S(1)}, u32[]{:S(2)}, u32[]{:S(2)}) collective-permute-start(bf16[96,2048]{1,0:T(8,128)(2,1)S(1)} %pad_maximum_fusion.4.refs_11_), channel_id=1, source_target_pairs={{0,6},{1,7},{2,0},{3,1},{4,2},{5,3},{6,4},{7,5},{8,14},{9,15},{10,... | collective-permute-start | bytes 1179656 | tf_op jit(solution)/shard_map/ppermute | solution.py:389
  67.0 11.2 %collective-permute-start.11 = (bf16[96,2048]{1,0:T(8,128)(2,1)S(1)}, bf16[96,2048]{1,0:T(8,128)(2,1)S(1)}, u32[]{:S(2)}, u32[]{:S(2)}) collective-permute-start(bf16[96,2048]{1,0:T(8,128)(2,1)S(1)} %pad_maximum_fusion.4.refs_11_), channel_id=1, source_target_pairs={{0,2},{1,3},{2,4},{3,5},{4,6},{5,7},{6,0},{7,1},{8,10},{9,11},{10,... | collective-permute-start | bytes 1179656 | tf_op jit(solution)/shard_map/ppermute | solution.py:389
  67.4 11.2 %collective-permute-start.10 = (bf16[96,2048]{1,0:T(8,128)(2,1)S(1)}, bf16[96,2048]{1,0:T(8,128)(2,1)S(1)}, u32[]{:S(2)}, u32[]{:S(2)}) collective-permute-start(bf16[96,2048]{1,0:T(8,128)(2,1)S(1)} %pad_maximum_fusion.4.refs_11_), channel_id=1, source_target_pairs={{0,8},{1,9},{2,10},{3,11},{4,12},{5,13},{6,14},{7,15},{8,0},{9,1},... | collective-permute-start | bytes 1179656 | tf_op jit(solution)/shard_map/ppermute | solution.py:389
  69.2 12.4 %collective-permute-start.6 = (bf16[96,2176]{1,0:T(8,128)(2,1)S(1)}, bf16[96,2176]{1,0:T(8,128)(2,1)S(1)}, u32[]{:S(2)}, u32[]{:S(2)}) collective-permute-start(bf16[96,2176]{1,0:T(8,128)(2,1)S(1)} %broadcast_select_fusion), channel_id=1, source_target_pairs={{0,2},{1,7},{2,4},{3,1},{4,6},{5,3},{6,0},{7,5},{8,10},{9,15},{10,... | collective-permute-start | bytes 1253384 | tf_op jit(solution)/shard_map/ppermute | solution.py:389
  78.3 9.2 %collective-permute-start.15 = (bf16[96,2048]{1,0:T(8,128)(2,1)S(1)}, bf16[96,2048]{1,0:T(8,128)(2,1)S(1)}, u32[]{:S(2)}, u32[]{:S(2)}) collective-permute-start(bf16[96,2048]{1,0:T(8,128)(2,1)S(1)} %broadcast_select_fusion.3), channel_id=1, source_target_pairs={{0,2},{1,7},{2,4},{3,1},{4,6},{5,3},{6,0},{7,5},{8,10},{9,15},{10,... | collective-permute-start | bytes 1179656 | tf_op jit(solution)/shard_map/ppermute | solution.py:389
  78.7 15.6 %collective-permute-start.14 = (bf16[96,2048]{1,0:T(8,128)(2,1)S(1)}, bf16[96,2048]{1,0:T(8,128)(2,1)S(1)}, u32[]{:S(2)}, u32[]{:S(2)}) collective-permute-start(bf16[96,2048]{1,0:T(8,128)(2,1)S(1)} %collective-permute-done.10.refs_12_), channel_id=1, source_target_pairs={{0,6},{1,7},{2,0},{3,1},{4,2},{5,3},{6,4},{7,5},{8,14},{9,15},{10,... | collective-permute-start | bytes 1179656 | tf_op jit(solution)/shard_map/ppermute | solution.py:389
  80.8 13.4 %collective-permute-start.13 = (bf16[96,2048]{1,0:T(8,128)(2,1)S(1)}, bf16[96,2048]{1,0:T(8,128)(2,1)S(1)}, u32[]{:S(2)}, u32[]{:S(2)}) collective-permute-start(bf16[96,2048]{1,0:T(8,128)(2,1)S(1)} %collective-permute-done.10.refs_12_), channel_id=1, source_target_pairs={{0,2},{1,3},{2,4},{3,5},{4,6},{5,7},{6,0},{7,1},{8,10},{9,11},{10,... | collective-permute-start | bytes 1179656 | tf_op jit(solution)/shard_map/ppermute | solution.py:389
  81.0 26.2 %copy-start.22 = (s32[136]{0:T(256)S(1)}, s32[136]{0:T(256)}, u32[]{:S(2)}) copy-start(s32[136]{0:T(256)} %owner_ref.1) | copy-start | bytes 1636
  81.6 28.3 %collective-permute-start.17 = (bf16[384,2048]{1,0:T(8,128)(2,1)S(1)}, bf16[384,2048]{1,0:T(8,128)(2,1)}, u32[]{:S(2)}, u32[]{:S(2)}) collective-permute-start(bf16[384,2048]{1,0:T(8,128)(2,1)S(1)} %pad_maximum_fusion.1), channel_id=1, source_target_pairs={{0,1},{1,0},{2,3},{3,2},{4,5},{5,4},{6,7},{7,6},{8,9},{9,8},{10,11... | collective-permute-start | bytes 4718600 | tf_op jit(solution)/shard_map/ppermute | solution.py:389
  87.5 22.3 %collective-permute-start.8 = (bf16[288,2176]{1,0:T(8,128)(2,1)}, bf16[288,2176]{1,0:T(8,128)(2,1)}, u32[]{:S(2)}, u32[]{:S(2)}) collective-permute-start(bf16[288,2176]{1,0:T(8,128)(2,1)} %pad_maximum_fusion.2), channel_id=1, source_target_pairs={{0,1},{1,0},{2,3},{3,2},{4,5},{5,4},{6,7},{7,6},{8,9},{9,8},{10,11... | collective-permute-start | bytes 3760136 | tf_op jit(solution)/shard_map/ppermute | solution.py:389
  94.2 3.3 %collective-permute-start.9 = (bf16[96,2176]{1,0:T(8,128)(2,1)S(1)}, bf16[96,2176]{1,0:T(8,128)(2,1)S(1)}, u32[]{:S(2)}, u32[]{:S(2)}) collective-permute-start(bf16[96,2176]{1,0:T(8,128)(2,1)S(1)} %collective-permute-done.6.refs_7_), channel_id=1, source_target_pairs={{0,1},{1,0},{2,3},{3,2},{4,5},{5,4},{6,7},{7,6},{8,9},{9,8},{10,11... | collective-permute-start | bytes 1253384 | tf_op jit(solution)/shard_map/ppermute | solution.py:389
  94.4 15.5 %collective-permute-start.18 = (bf16[288,2048]{1,0:T(8,128)(2,1)S(1)}, bf16[288,2048]{1,0:T(8,128)(2,1)}, u32[]{:S(2)}, u32[]{:S(2)}) collective-permute-start(bf16[288,2048]{1,0:T(8,128)(2,1)S(1)} %pad_maximum_fusion.3), channel_id=1, source_target_pairs={{0,1},{1,0},{2,3},{3,2},{4,5},{5,4},{6,7},{7,6},{8,9},{9,8},{10,11... | collective-permute-start | bytes 3538952 | tf_op jit(solution)/shard_map/ppermute | solution.py:389
  97.5 7.1 %collective-permute-start.16 = (bf16[96,2048]{1,0:T(8,128)(2,1)S(1)}, bf16[96,2048]{1,0:T(8,128)(2,1)}, u32[]{:S(2)}, u32[]{:S(2)}) collective-permute-start(bf16[96,2048]{1,0:T(8,128)(2,1)S(1)} %broadcast_select_fusion.2), channel_id=1, source_target_pairs={{0,2},{1,7},{2,4},{3,1},{4,6},{5,3},{6,0},{7,5},{8,10},{9,15},{10,... | collective-permute-start | bytes 1179656 | tf_op jit(solution)/shard_map/ppermute | solution.py:389
  104.6 5.2 %collective-permute-start.19 = (bf16[96,2048]{1,0:T(8,128)(2,1)}, bf16[96,2048]{1,0:T(8,128)(2,1)}, u32[]{:S(2)}, u32[]{:S(2)}) collective-permute-start(bf16[96,2048]{1,0:T(8,128)(2,1)} %collective-permute-done.16.refs_18_), channel_id=1, source_target_pairs={{0,1},{1,0},{2,3},{3,2},{4,5},{5,4},{6,7},{7,6},{8,9},{9,8},{10,11... | collective-permute-start | bytes 1179656 | tf_op jit(solution)/shard_map/ppermute | solution.py:389
  (21 other events, 251.9 us)

commit v6 on v5

--- a/solution.py
+++ b/solution.py
@@ -242,19 +242,21 @@
 FEAT = 8
 
 
-BLOCKS = ((0, 96), (96, 96), (192, 96), (288, 96), (384, 96), (480, 96), (576, 96), (672, 96), (768, 384), (1152, 288), (1440, 96))
+COMMON = tuple((96 * k, 96) for k in range(8)) + ((768, 384),)
+BLOCKS = (COMMON + ((1152, 288), (1440, 96)), COMMON + tuple((1152 + 96 * k, 96) for k in range(4)))
+COUNT = len(BLOCKS[0]) + len(BLOCKS[1])
 
 
 def gram_kernel(me_ref, owner_ref, *refs):
-    n = len(BLOCKS)
-    parts, (out_ref, peak_ref) = (refs[:n], refs[n:2 * n]), refs[2 * n:2 * n + 2]
-    fa_ref, fb_ref, ft_ref, target_ref, left_ref, list_i, list_j, sem = refs[2 * n + 2:]
+    n = len(BLOCKS[0])
+    parts, (out_ref, peak_ref) = (refs[:n], refs[n:COUNT]), refs[COUNT:COUNT + 2]
+    fa_ref, fb_ref, ft_ref, target_ref, left_ref, list_i, list_j, sem = refs[COUNT + 2:]
     held = (fa_ref, fb_ref)
     me_tile = me_ref[0]
     copies = [
         [
             pltpu.make_async_copy(ref, held[part].at[start:start + size], sem.at[part * n + k])
-            for k, (ref, (start, size)) in enumerate(zip(parts[part], BLOCKS))
+            for k, (ref, (start, size)) in enumerate(zip(parts[part], BLOCKS[part]))
         ]
         for part in range(2)
     ]
@@ -332,7 +334,7 @@
     return pl.pallas_call(
         gram_kernel,
         out_shape=(jax.ShapeDtypeStruct((FEAT, SLOTS, 32, 256), F32), jax.ShapeDtypeStruct((8, 256), F32)),
-        in_specs=[smem, smem] + [pl.BlockSpec(memory_space=pltpu.HBM)] * (2 * len(BLOCKS)),
+        in_specs=[smem, smem] + [pl.BlockSpec(memory_space=pltpu.HBM)] * COUNT,
         out_specs=(vmem, vmem),
         scratch_shapes=[
             pltpu.VMEM((GROUP, 2176), BF),
@@ -342,7 +344,7 @@
             pltpu.VMEM((256, GROUP), BF),
             pltpu.SMEM((OWNED,), jnp.int32),
             pltpu.SMEM((OWNED,), jnp.int32),
-            pltpu.SemaphoreType.DMA((2 * len(BLOCKS),)),
+            pltpu.SemaphoreType.DMA((COUNT,)),
         ],
         compiler_params=pltpu.CompilerParams(vmem_limit_bytes=56 * 2**20),
         cost_estimate=pl.CostEstimate(flops=5 * 10**9, bytes_accessed=20 * 2**20, transcendentals=0),
@@ -396,24 +398,31 @@
     return own, over, left, right
 
 
-def spread_second(first):
+def spread_second(first, earlier=None):
     own, over, left, right = first
     even = lax.axis_index("tile") % 2 == 0
     far = send(jnp.where(even, left, right), onward())
+    if earlier is not None:
+        over, far, *earlier[7:10] = lax.optimization_barrier((over, far, *earlier[7:10]))
     over_left = send(over, hop(dx=1))
     over_right = send(over, hop(dx=-1))
     swap_a = send(jnp.concatenate([own, over, left, right], axis=0), hop(core=1))
     return far, over_left, over_right, swap_a
 
 
-def spread_third(first, second):
+def spread_third(first, second, apart):
     own, over, left, right = first
     far, over_left, over_right, swap_a = second
     even = lax.axis_index("tile") % 2 == 0
-    over_far = send(jnp.where(even, over_left, over_right), onward())
+    over_far = send(far, hop(dy=1)) if apart else send(jnp.where(even, over_left, over_right), onward())
+    held = [own, over, left, right, over_left, over_right, far, over_far, swap_a]
+    if apart:
+        far_swap = send(far, hop(core=1))
+        rest = lax.optimization_barrier((over_left, over_right, over_far))
+        swaps = [send(block, hop(core=1)) for block in rest]
+        return held + [swaps[0], swaps[1], far_swap, swaps[2]]
     swap_b = send(jnp.concatenate([over_left, over_right, far], axis=0), hop(core=1))
-    swap_c = send(over_far, hop(core=1))
-    return [own, over, left, right, over_left, over_right, far, over_far, swap_a, swap_b, swap_c]
+    return held + [swap_b, send(over_far, hop(core=1))]
 
 
 def body(images, row_list, labels, filters, bias, tile_owner):
@@ -428,9 +437,9 @@
     own_b, far, over_left, over_right = lax.optimization_barrier((own_b,) + second_a[:3])
     second_a = (far, over_left, over_right, second_a[3])
     first_b = spread_first(own_b)
-    part_a = spread_third(first_a, second_a)
-    second_b = spread_second(first_b)
-    part_b = spread_third(first_b, second_b)
+    part_a = spread_third(first_a, second_a, False)
+    second_b = spread_second(first_b, part_a)
+    part_b = spread_third(first_b, second_b, True)
     me = jnp.stack([lax.axis_index("tile"), lax.axis_index("feat")]).astype(jnp.int32)
     partial, peak = gram(me, tile_owner, (part_a, part_b))
     owned = jnp.sum((tile_owner == me[0]).astype(jnp.int32))

time: 169 us -> 167 us (0.988)
  the two profiles are of different devices: /device:TPU:1 before, /device:TPU:0 now
where the time goes in v6:
time: 167 us
  Pallas kernels  63.2 us (38%)
  waiting for transfers between devices  35.6 us (21%)
  blocking collectives  32.1 us (19%)
  starting transfers between devices  17.4 us (10%)
  other arithmetic  8.1 us (5%)
  local copies, waits for them, and re-layouts  7.68 us (5%)
  between operations  2.98 us (2%)
    pallas_call x3, Pallas kernels, conv(): pl.pallas_call(functools.partial(conv_kernel, first, count), out_shape=ja...  36.1 us
    ppermute x22, waiting for transfers between devices, send(): return lax.ppermute(block, 'tile', perm)  35.6 us
    all_to_all x1, blocking collectives, some(): got = lax.all_to_all(coded, 'feat', split_axis=0, concat_axis=0, tiled=True)  32.1 us
    pallas_call x1, Pallas kernels, gram(): pl.pallas_call(gram_kernel, out_shape=(jax.ShapeDtypeStruct((FEAT, SLOTS,...  19.4 us
    ppermute x22, starting transfers between devices, send(): return lax.ppermute(block, 'tile', perm)  17.4 us
    pallas_call x1, Pallas kernels, prep(): pl.pallas_call(prep_kernel, out_shape=(jax.ShapeDtypeStruct((16, NBLK, 16...  7.76 us
    unnamed x52, local copies, waits for them, and re-layouts  5.33 us
    convert_element_type x1, other arithmetic, some(): coded = jnp.where(note, exponent, used * scale).astype(HALF)  4.08 us
  transfers between devices with their start and end apart: 22, of which 10 were waited for; matrix products, arithmetic and copies ran while one was open for 1% of the time, Pallas kernels for 11%

profile of v6, /device:TPU:0, one launch (start us, length us, event | category | flops | bytes accessed | tf_op | source)
XLA Modules:
  0.0 167.1 jit_solution(16603280126167093366)
XLA Ops:
  1.3 1.7 copy-done
  3.9 7.8 %prep.1 = (bf16[16,6,160,128]{3,2,1,0:T(8,128)(2,1)S(1)}, bf16[16,80,128]{2,1,0:T(8,128)(2,1)S(1)}, bf16[4,1536,256]{2,1,0:T(8,128)(2,1)S(1)}, bf16[96,256]{1,0:...) custom-call(s32[1,128]{1,0:T(1,128)S(1)} %get-tuple-element.81.rows_ref, ...), custom_call_target="tpu_custom_call" | custom-call | tf_op jit(solution)/shard_map/prep/pallas_call | solution.py:95
  12.5 17.8 %conv.3.refs_0_ = bf16[96,2176]{1,0:T(8,128)(2,1)S(1)} custom-call(s32[1,2]{1,0:T(1,128)S(1)} %get-tuple-element.49.nblk_ref, bf16[16,6,160,128]{3,2,1,0:T(8,128)(2,1)S(1)} %get-tuple-element.50.win_ref, bf16[16,80,128]{2,1,0:T(8,128)(2,1)S(1)} %get-tuple-element.51.half_ref, bf16[4,1536,256]{2,1,0:T(8,128)(2,1)S(1)} %get-tuple-element.52.w_ref, ...), custom_call_target="tpu_custom_call" | custom-call | flops 22649241600 | bytes 8388608 | tf_op jit(solution)/shard_map/conv/pallas_call | solution.py:221
  30.2 2.9 %collective-permute-start.2 = (bf16[96,2176]{1,0:T(8,128)(2,1)S(1)}, bf16[96,2176]{1,0:T(8,128)(2,1)S(1)}, u32[]{:S(2)}, u32[]{:S(2)}) collective-permute-start(bf16[96,2176]{1,0:T(8,128)(2,1)S(1)} %conv.3.refs_0_), channel_id=1, source_target_pairs={{0,6},{1,7},{2,0},{3,1},{4,2},{5,3},{6,4},{7,5},{8,14},{9,15},{10,... | collective-permute-start | bytes 1253384 | tf_op jit(solution)/shard_map/ppermute | solution.py:391
  33.1 4.4 %collective-permute-start = (bf16[96,2176]{1,0:T(8,128)(2,1)S(1)}, bf16[96,2176]{1,0:T(8,128)(2,1)S(1)}, u32[]{:S(2)}, u32[]{:S(2)}) collective-permute-start(bf16[96,2176]{1,0:T(8,128)(2,1)S(1)} %conv.3.refs_0_), channel_id=1, source_target_pairs={{0,8},{1,9},{2,10},{3,11},{4,12},{5,13},{6,14},{7,15},{8,0},{9,1},... | collective-permute-start | bytes 1253384 | tf_op jit(solution)/shard_map/ppermute | solution.py:391
  37.5 9.2 %conv.4 = bf16[96,1024]{1,0:T(8,128)(2,1)S(1)} custom-call(s32[1,2]{1,0:T(1,128)S(1)} %get-tuple-element.49.nblk_ref, bf16[16,6,160,128]{3,2,1,0:T(8,128)(2,1)S(1)} %get-tuple-element.50.win_ref, bf16[16,80,128]{2,1,0:T(8,128)(2,1)S(1)} %get-tuple-element.51.half_ref, bf16[4,1536,256]{2,1,0:T(8,128)(2,1)S(1)} %get-tuple-element.52.w_ref, ...), custom_call_target="tpu_custom_call" | custom-call | flops 11324620800 | bytes 8388608 | tf_op jit(solution)/shard_map/conv/pallas_call | solution.py:221
  46.9 2.2 %collective-permute-start.3 = (bf16[96,2176]{1,0:T(8,128)(2,1)S(1)}, bf16[96,2176]{1,0:T(8,128)(2,1)S(1)}, u32[]{:S(2)}, u32[]{:S(2)}) collective-permute-start(bf16[96,2176]{1,0:T(8,128)(2,1)S(1)} %broadcast_select_fusion.1), channel_id=1, source_target_pairs={{0,2},{1,7},{2,4},{3,1},{4,6},{5,3},{6,0},{7,5},{8,10},{9,15},{10,... | collective-permute-start | bytes 1253384 | tf_op jit(solution)/shard_map/ppermute | solution.py:391
  49.3 1.4 collective-permute-start.5
  51.4 1.9 %copy-done.9 = bf16[4,1536,256]{2,1,0:T(8,128)(2,1)S(1)} copy-done((bf16[4,1536,256]{2,1,0:T(8,128)(2,1)S(1)}, bf16[4,1536,256]{2,1,0:T(8,128)(2,1)}, u32[]{:S(2)}) %copy-start.9) | copy-done | bytes 3145752
  53.3 9.2 %conv.5 = bf16[96,1024]{1,0:T(8,128)(2,1)S(1)} custom-call(s32[1,2]{1,0:T(1,128)S(1)} %get-tuple-element.49.nblk_ref, bf16[16,6,160,128]{3,2,1,0:T(8,128)(2,1)S(1)} %copy-done.7, bf16[16,80,128]{2,1,0:T(8,128)(2,1)S(1)} %get-tuple-element.51.half_ref, bf16[4,1536,256]{2,1,0:T(8,128)(2,1)S(1)} %copy-done.9, bf16[96,256]{1,0:T(8,128)(2,1)S(1)} %get-tuple-element.53.sel_ref, ...), custom_call_target="tpu_custom_call" | custom-call | flops 11324620800 | bytes 8388608 | tf_op jit(solution)/shard_map/conv/pallas_call | solution.py:221
  62.5 2.8 %collective-permute-done.4.refs_4_ = bf16[96,2176]{1,0:T(8,128)(2,1)S(1)} collective-permute-done((bf16[96,2176]{1,0:T(8,128)(2,1)S(1)}, bf16[96,2176]{1,0:T(8,128)(2,1)S(1)}, u32[]{:S(2)}, u32[]{:S(2)}) %collective-permute-start.4) | collective-permute-done | bytes 417824 | tf_op jit(solution)/shard_map/ppermute | solution.py:391
  66.1 1.2 collective-permute-start.7
  67.7 7.1 %collective-permute-done.8.refs_14_ = bf16[96,2048]{1,0:T(8,128)(2,1)S(1)} collective-permute-done((bf16[96,2048]{1,0:T(8,128)(2,1)S(1)}, bf16[96,2048]{1,0:T(8,128)(2,1)S(1)}, u32[]{:S(2)}, u32[]{:S(2)}) %collective-permute-start.8) | collective-permute-done | bytes 393248 | tf_op jit(solution)/shard_map/ppermute | solution.py:391
  74.8 2.2 %collective-permute-done.7.refs_13_ = bf16[96,2048]{1,0:T(8,128)(2,1)S(1)} collective-permute-done((bf16[96,2048]{1,0:T(8,128)(2,1)S(1)}, bf16[96,2048]{1,0:T(8,128)(2,1)S(1)}, u32[]{:S(2)}, u32[]{:S(2)}) %collective-permute-start.7) | collective-permute-done | bytes 393248 | tf_op jit(solution)/shard_map/ppermute | solution.py:391
  77.7 6.3 %collective-permute-done.10.refs_7_ = bf16[96,2176]{1,0:T(8,128)(2,1)S(1)} collective-permute-done((bf16[96,2176]{1,0:T(8,128)(2,1)S(1)}, bf16[96,2176]{1,0:T(8,128)(2,1)S(1)}, u32[]{:S(2)}, u32[]{:S(2)}) %collective-permute-start.10) | collective-permute-done | bytes 417824 | tf_op jit(solution)/shard_map/ppermute | solution.py:391
  84.0 4.3 %collective-permute-done.9.refs_17_ = bf16[96,2048]{1,0:T(8,128)(2,1)} collective-permute-done((bf16[96,2048]{1,0:T(8,128)(2,1)S(1)}, bf16[96,2048]{1,0:T(8,128)(2,1)}, u32[]{:S(2)}, u32[]{:S(2)}) %collective-permute-start.9) | collective-permute-done | bytes 393248 | tf_op jit(solution)/shard_map/ppermute | solution.py:391
  89.1 1.3 collective-permute-start.15
  91.3 8.9 %collective-permute-done.15.refs_16_ = bf16[96,2048]{1,0:T(8,128)(2,1)S(1)} collective-permute-done((bf16[96,2048]{1,0:T(8,128)(2,1)S(1)}, bf16[96,2048]{1,0:T(8,128)(2,1)S(1)}, u32[]{:S(2)}, u32[]{:S(2)}) %collective-permute-start.15) | collective-permute-done | bytes 393248 | tf_op jit(solution)/shard_map/ppermute | solution.py:391
  100.2 2.2 %collective-permute-done.14.refs_15_ = bf16[96,2048]{1,0:T(8,128)(2,1)S(1)} collective-permute-done((bf16[96,2048]{1,0:T(8,128)(2,1)S(1)}, bf16[96,2048]{1,0:T(8,128)(2,1)S(1)}, u32[]{:S(2)}, u32[]{:S(2)}) %collective-permute-start.14) | collective-permute-done | bytes 393248 | tf_op jit(solution)/shard_map/ppermute | solution.py:391
  106.7 19.4 %gram.1 = (f32[8,25,32,256]{3,2,1,0:T(8,128)}, f32[8,256]{1,0:T(8,128)}) custom-call(s32[2]{0:T(128)} %pad_add_fusion.me_ref, s32[136]{0:T(256)} %owner_ref.1, bf16[96,2176]{1,0:T(8,128)(2,1)} %copy-done.3, bf16[96,2176]{1,0:T(8,128)(2,1)} %copy-done.4, bf16[96,2176]{1,0:T(8,128)(2,1)} %copy-done.2, bf16[96,2176]{1,0:T(8,128)(2,1)} %copy-done.1, ...), custom_call_target="tpu_custom_call" | custom-call | flops 5000000000 | bytes 20971520 | tf_op jit(solution)/shard_map/gram/pallas_call | solution.py:334
  126.1 1.3 reduce_max.9
  128.2 38.9 %conditional.1 = (f32[20,32,256]{2,1,0:T(8,128)}, f32[32,1000]{1,0:T(8,128)}) conditional(s32[]{:T(128)} %clamp.3, (f32[]{:T(128)}, f32[8,25,32,256]{3,2,1,0:T(8,128)}, f32[]{:T(128)}) %tuple.25, (f32[]{:T(128)}, f32[8,25,32,256]{3,2,1,0:T(8,128)}, f32[]{:T(128)}) %tuple.25, (f32[]{:T(128)}, f32[]{:T(128)}, ...), branch_computations={%region_2.4_spmd, %region_4.6_spmd, %region_6.8_spmd} | conditional | flops 9625657 | bytes 22315226 | solution.py:376
  128.2 4.1 %select_convert_fusion.2 = f16[8,25,32,256]{3,2,1,0:T(8,128)(2,1)S(1)} fusion(f32[8,25,32,256]{3,2,1,0:T(8,128)} %get-tuple-element.25, f32[]{:T(128)} %get-tuple-element.26, f32[]{:T(128)} %get-tuple-element.24, pred[25]{0:T(512)(128)(4,1)S(1)} %iota_compare_fusion.2), kind=kLoop, calls=%fused_computation.11 | loop fusion | flops 4915200 | bytes 9830433 | tf_op jit(solution)/shard_map/cond/branch_2_fun/convert_element_type | solution.py:368
  132.3 32.1 %all_to_all.14 = f16[8,25,32,256]{3,2,1,0:T(8,128)(2,1)S(1)} all-to-all(f16[8,25,32,256]{3,2,1,0:T(8,128)(2,1)S(1)} %select_convert_fusion.2), channel_id=1, replica_groups=mesh['feat'=8,'tile'=16] {'feat'}, dimensions={0} | all-to-all | bytes 6553600 | tf_op jit(solution)/shard_map/cond/branch_2_fun/all_to_all | solution.py:369
  (99 shorter events, 12.7 us)
Async XLA Ops:
  30.2 16.5 %collective-permute-start.2 = (bf16[96,2176]{1,0:T(8,128)(2,1)S(1)}, bf16[96,2176]{1,0:T(8,128)(2,1)S(1)}, u32[]{:S(2)}, u32[]{:S(2)}) collective-permute-start(bf16[96,2176]{1,0:T(8,128)(2,1)S(1)} %conv.3.refs_0_), channel_id=1, source_target_pairs={{0,6},{1,7},{2,0},{3,1},{4,2},{5,3},{6,4},{7,5},{8,14},{9,15},{10,... | collective-permute-start | bytes 1253384 | tf_op jit(solution)/shard_map/ppermute | solution.py:391
  33.1 13.6 %collective-permute-start.1 = (bf16[96,2176]{1,0:T(8,128)(2,1)S(1)}, bf16[96,2176]{1,0:T(8,128)(2,1)S(1)}, u32[]{:S(2)}, u32[]{:S(2)}) collective-permute-start(bf16[96,2176]{1,0:T(8,128)(2,1)S(1)} %conv.3.refs_0_), channel_id=1, source_target_pairs={{0,2},{1,3},{2,4},{3,5},{4,6},{5,7},{6,0},{7,1},{8,10},{9,11},{10,... | collective-permute-start | bytes 1253384 | tf_op jit(solution)/shard_map/ppermute | solution.py:391
  33.1 15.9 %collective-permute-start = (bf16[96,2176]{1,0:T(8,128)(2,1)S(1)}, bf16[96,2176]{1,0:T(8,128)(2,1)S(1)}, u32[]{:S(2)}, u32[]{:S(2)}) collective-permute-start(bf16[96,2176]{1,0:T(8,128)(2,1)S(1)} %conv.3.refs_0_), channel_id=1, source_target_pairs={{0,8},{1,9},{2,10},{3,11},{4,12},{5,13},{6,14},{7,15},{8,0},{9,1},... | collective-permute-start | bytes 1253384 | tf_op jit(solution)/shard_map/ppermute | solution.py:391
  46.9 15.7 %collective-permute-start.3 = (bf16[96,2176]{1,0:T(8,128)(2,1)S(1)}, bf16[96,2176]{1,0:T(8,128)(2,1)S(1)}, u32[]{:S(2)}, u32[]{:S(2)}) collective-permute-start(bf16[96,2176]{1,0:T(8,128)(2,1)S(1)} %broadcast_select_fusion.1), channel_id=1, source_target_pairs={{0,2},{1,7},{2,4},{3,1},{4,6},{5,3},{6,0},{7,5},{8,10},{9,15},{10,... | collective-permute-start | bytes 1253384 | tf_op jit(solution)/shard_map/ppermute | solution.py:391
  49.2 39.1 %collective-permute-start.11 = (bf16[384,2176]{1,0:T(8,128)(2,1)S(1)}, bf16[384,2176]{1,0:T(8,128)(2,1)S(1)}, u32[]{:S(2)}, u32[]{:S(2)}) collective-permute-start(bf16[384,2176]{1,0:T(8,128)(2,1)S(1)} %pad_maximum_fusion), channel_id=1, source_target_pairs={{0,1},{1,0},{2,3},{3,2},{4,5},{5,4},{6,7},{7,6},{8,9},{9,8},{10,11... | collective-permute-start | bytes 5013512 | tf_op jit(solution)/shard_map/ppermute | solution.py:391
  49.3 13.2 %collective-permute-start.5 = (bf16[96,2176]{1,0:T(8,128)(2,1)S(1)}, bf16[96,2176]{1,0:T(8,128)(2,1)S(1)}, u32[]{:S(2)}, u32[]{:S(2)}) collective-permute-start(bf16[96,2176]{1,0:T(8,128)(2,1)S(1)} %collective-permute-done.refs_0_.refs_1_), channel_id=1, source_target_pairs={{0,6},{1,7},{2,0},{3,1},{4,2},{5,3},{6,4},{7,5},{8,14},{9,15},{10,... | collective-permute-start | bytes 1253384 | tf_op jit(solution)/shard_map/ppermute | solution.py:391
  50.6 14.7 %collective-permute-start.4 = (bf16[96,2176]{1,0:T(8,128)(2,1)S(1)}, bf16[96,2176]{1,0:T(8,128)(2,1)S(1)}, u32[]{:S(2)}, u32[]{:S(2)}) collective-permute-start(bf16[96,2176]{1,0:T(8,128)(2,1)S(1)} %collective-permute-done.refs_0_.refs_1_), channel_id=1, source_target_pairs={{0,2},{1,3},{2,4},{3,5},{4,6},{5,7},{6,0},{7,1},{8,10},{9,11},{10,... | collective-permute-start | bytes 1253384 | tf_op jit(solution)/shard_map/ppermute | solution.py:391
  65.3 9.5 %collective-permute-start.8 = (bf16[96,2048]{1,0:T(8,128)(2,1)S(1)}, bf16[96,2048]{1,0:T(8,128)(2,1)S(1)}, u32[]{:S(2)}, u32[]{:S(2)}) collective-permute-start(bf16[96,2048]{1,0:T(8,128)(2,1)S(1)} %pad_maximum_fusion.3.refs_11_), channel_id=1, source_target_pairs={{0,6},{1,7},{2,0},{3,1},{4,2},{5,3},{6,4},{7,5},{8,14},{9,15},{10,... | collective-permute-start | bytes 1179656 | tf_op jit(solution)/shard_map/ppermute | solution.py:391
  66.1 10.8 %collective-permute-start.7 = (bf16[96,2048]{1,0:T(8,128)(2,1)S(1)}, bf16[96,2048]{1,0:T(8,128)(2,1)S(1)}, u32[]{:S(2)}, u32[]{:S(2)}) collective-permute-start(bf16[96,2048]{1,0:T(8,128)(2,1)S(1)} %pad_maximum_fusion.3.refs_11_), channel_id=1, source_target_pairs={{0,2},{1,3},{2,4},{3,5},{4,6},{5,7},{6,0},{7,1},{8,10},{9,11},{10,... | collective-permute-start | bytes 1179656 | tf_op jit(solution)/shard_map/ppermute | solution.py:391
  67.3 10.4 %collective-permute-start.6 = (bf16[96,2048]{1,0:T(8,128)(2,1)S(1)}, bf16[96,2048]{1,0:T(8,128)(2,1)S(1)}, u32[]{:S(2)}, u32[]{:S(2)}) collective-permute-start(bf16[96,2048]{1,0:T(8,128)(2,1)S(1)} %pad_maximum_fusion.3.refs_11_), channel_id=1, source_target_pairs={{0,8},{1,9},{2,10},{3,11},{4,12},{5,13},{6,14},{7,15},{8,0},{9,1},... | collective-permute-start | bytes 1179656 | tf_op jit(solution)/shard_map/ppermute | solution.py:391
  67.5 36.6 %copy-start.19 = (s32[136]{0:T(256)S(1)}, s32[136]{0:T(256)}, u32[]{:S(2)}) copy-start(s32[136]{0:T(256)} %owner_ref.1) | copy-start | bytes 1636
  67.5 20.8 %collective-permute-start.12 = (bf16[288,2176]{1,0:T(8,128)(2,1)S(1)}, bf16[288,2176]{1,0:T(8,128)(2,1)S(1)}, u32[]{:S(2)}, u32[]{:S(2)}) collective-permute-start(bf16[288,2176]{1,0:T(8,128)(2,1)S(1)} %pad_maximum_fusion.2), channel_id=1, source_target_pairs={{0,1},{1,0},{2,3},{3,2},{4,5},{5,4},{6,7},{7,6},{8,9},{9,8},{10,11... | collective-permute-start | bytes 3760136 | tf_op jit(solution)/shard_map/ppermute | solution.py:391
  74.8 31.9 %copy-start.15 = (bf16[96,2048]{1,0:T(8,128)(2,1)}, bf16[96,2048]{1,0:T(8,128)(2,1)S(1)}, u32[]{:S(2)}) copy-start(bf16[96,2048]{1,0:T(8,128)(2,1)S(1)} %collective-permute-done.8.refs_14_) | copy-start | bytes 1179652
  74.8 9.3 %collective-permute-start.10 = (bf16[96,2176]{1,0:T(8,128)(2,1)S(1)}, bf16[96,2176]{1,0:T(8,128)(2,1)S(1)}, u32[]{:S(2)}, u32[]{:S(2)}) collective-permute-start(bf16[96,2176]{1,0:T(8,128)(2,1)S(1)} %broadcast_select_fusion), channel_id=1, source_target_pairs={{0,2},{1,7},{2,4},{3,1},{4,6},{5,3},{6,0},{7,5},{8,10},{9,15},{10,... | collective-permute-start | bytes 1253384 | tf_op jit(solution)/shard_map/ppermute | solution.py:391
  77.0 11.3 %collective-permute-start.9 = (bf16[96,2048]{1,0:T(8,128)(2,1)S(1)}, bf16[96,2048]{1,0:T(8,128)(2,1)}, u32[]{:S(2)}, u32[]{:S(2)}) collective-permute-start(bf16[96,2048]{1,0:T(8,128)(2,1)S(1)} %broadcast_select_fusion.2), channel_id=1, source_target_pairs={{0,2},{1,7},{2,4},{3,1},{4,6},{5,3},{6,0},{7,5},{8,10},{9,15},{10,... | collective-permute-start | bytes 1179656 | tf_op jit(solution)/shard_map/ppermute | solution.py:391
  88.5 18.2 %collective-permute-start.17 = (bf16[384,2048]{1,0:T(8,128)(2,1)S(1)}, bf16[384,2048]{1,0:T(8,128)(2,1)}, u32[]{:S(2)}, u32[]{:S(2)}) collective-permute-start(bf16[384,2048]{1,0:T(8,128)(2,1)S(1)} %pad_maximum_fusion.1), channel_id=1, source_target_pairs={{0,1},{1,0},{2,3},{3,2},{4,5},{5,4},{6,7},{7,6},{8,9},{9,8},{10,11... | collective-permute-start | bytes 4718600 | tf_op jit(solution)/shard_map/ppermute | solution.py:391
  88.6 15.4 %collective-permute-start.13 = (bf16[96,2176]{1,0:T(8,128)(2,1)S(1)}, bf16[96,2176]{1,0:T(8,128)(2,1)S(1)}, u32[]{:S(2)}, u32[]{:S(2)}) collective-permute-start(bf16[96,2176]{1,0:T(8,128)(2,1)S(1)} %collective-permute-done.10.refs_7_), channel_id=1, source_target_pairs={{0,1},{1,0},{2,3},{3,2},{4,5},{5,4},{6,7},{7,6},{8,9},{9,8},{10,11... | collective-permute-start | bytes 1253384 | tf_op jit(solution)/shard_map/ppermute | solution.py:391
  89.1 11.1 %collective-permute-start.15 = (bf16[96,2048]{1,0:T(8,128)(2,1)S(1)}, bf16[96,2048]{1,0:T(8,128)(2,1)S(1)}, u32[]{:S(2)}, u32[]{:S(2)}) collective-permute-start(bf16[96,2048]{1,0:T(8,128)(2,1)S(1)} %collective-permute-done.6.refs_12_), channel_id=1, source_target_pairs={{0,6},{1,7},{2,0},{3,1},{4,2},{5,3},{6,4},{7,5},{8,14},{9,15},{10,... | collective-permute-start | bytes 1179656 | tf_op jit(solution)/shard_map/ppermute | solution.py:391
  90.4 12.1 %collective-permute-start.14 = (bf16[96,2048]{1,0:T(8,128)(2,1)S(1)}, bf16[96,2048]{1,0:T(8,128)(2,1)S(1)}, u32[]{:S(2)}, u32[]{:S(2)}) collective-permute-start(bf16[96,2048]{1,0:T(8,128)(2,1)S(1)} %collective-permute-done.6.refs_12_), channel_id=1, source_target_pairs={{0,2},{1,3},{2,4},{3,5},{4,6},{5,7},{6,0},{7,1},{8,10},{9,11},{10,... | collective-permute-start | bytes 1179656 | tf_op jit(solution)/shard_map/ppermute | solution.py:391
  91.1 12.4 %collective-permute-start.16 = (bf16[96,2048]{1,0:T(8,128)(2,1)}, bf16[96,2048]{1,0:T(8,128)(2,1)}, u32[]{:S(2)}, u32[]{:S(2)}) collective-permute-start(bf16[96,2048]{1,0:T(8,128)(2,1)} %collective-permute-done.9.refs_17_), channel_id=1, source_target_pairs={{0,8},{1,9},{2,10},{3,11},{4,12},{5,13},{6,14},{7,15},{8,0},{9,1},... | collective-permute-start | bytes 1179656 | tf_op jit(solution)/shard_map/ppermute | solution.py:391
  100.2 6.4 %collective-permute-start.20 = (bf16[96,2048]{1,0:T(8,128)(2,1)}, bf16[96,2048]{1,0:T(8,128)(2,1)}, u32[]{:S(2)}, u32[]{:S(2)}) collective-permute-start(bf16[96,2048]{1,0:T(8,128)(2,1)} %collective-permute-done.9.refs_17_), channel_id=1, source_target_pairs={{0,1},{1,0},{2,3},{3,2},{4,5},{5,4},{6,7},{7,6},{8,9},{9,8},{10,11... | collective-permute-start | bytes 1179656 | tf_op jit(solution)/shard_map/ppermute | solution.py:391
  103.5 3.1 %collective-permute-start.18 = (bf16[96,2048]{1,0:T(8,128)(2,1)S(1)}, bf16[96,2048]{1,0:T(8,128)(2,1)}, u32[]{:S(2)}, u32[]{:S(2)}) collective-permute-start(bf16[96,2048]{1,0:T(8,128)(2,1)S(1)} %collective-permute-done.14.refs_15_), channel_id=1, source_target_pairs={{0,1},{1,0},{2,3},{3,2},{4,5},{5,4},{6,7},{7,6},{8,9},{9,8},{10,11... | collective-permute-start | bytes 1179656 | tf_op jit(solution)/shard_map/ppermute | solution.py:391
  103.5 3.1 %collective-permute-start.19 = (bf16[96,2048]{1,0:T(8,128)(2,1)S(1)}, bf16[96,2048]{1,0:T(8,128)(2,1)}, u32[]{:S(2)}, u32[]{:S(2)}) collective-permute-start(bf16[96,2048]{1,0:T(8,128)(2,1)S(1)} %collective-permute-done.15.refs_16_), channel_id=1, source_target_pairs={{0,1},{1,0},{2,3},{3,2},{4,5},{5,4},{6,7},{7,6},{8,9},{9,8},{10,11... | collective-permute-start | bytes 1179656 | tf_op jit(solution)/shard_map/ppermute | solution.py:391
  104.0 2.7 %collective-permute-start.21 = (bf16[96,2048]{1,0:T(8,128)(2,1)}, bf16[96,2048]{1,0:T(8,128)(2,1)}, u32[]{:S(2)}, u32[]{:S(2)}) collective-permute-start(bf16[96,2048]{1,0:T(8,128)(2,1)} %collective-permute-done.16.refs_18_), channel_id=1, source_target_pairs={{0,1},{1,0},{2,3},{3,2},{4,5},{5,4},{6,7},{7,6},{8,9},{9,8},{10,11... | collective-permute-start | bytes 1179656 | tf_op jit(solution)/shard_map/ppermute | solution.py:391
  (24 other events, 337.9 us)

commit v7 on v5

--- a/solution.py
+++ b/solution.py
@@ -20,7 +20,7 @@
     return lax.dot_general(a, b, dims, preferred_element_type=F32)
 
 
-def prep_kernel(rows_ref, labels_ref, filt_ref, img_hbm, win_ref, half_ref, w_ref, sel_ref, lab_ref, nblk_ref, img_ref, x_ref, pick_ref, flat_ref, sem):
+def prep_kernel(me_ref, owner_ref, rows_ref, labels_ref, filt_ref, img_hbm, win_ref, half_ref, w_ref, sel_ref, lab_ref, nblk_ref, img_ref, x_ref, pick_ref, flat_ref, sem):
     fetch = pltpu.make_async_copy(img_hbm, img_ref, sem)
     fetch.start()
     flat_ref[...] = jnp.zeros_like(flat_ref)
@@ -54,6 +54,8 @@
     whole = (total + 7) // BLK
     nblk_ref[0, 0] = whole
     nblk_ref[0, 1] = total - whole * BLK
+    nblk_ref[0, 2] = me_ref[0]
+    nblk_ref[0, 3] = jnp.sum(jnp.where(owner_ref[...] == me_ref[0], 1.0, 0.0)).astype(jnp.int32)
     deep = lax.broadcasted_iota(jnp.int32, (WIDE, 128), 0)
     deep = jnp.where(deep < ROWS, deep, jnp.where(deep < ROWS + 8, deep - ROWS + BLK * whole, -1))
     take = jnp.where((deep == rank) & (used > 0.0), 1.0, 0.0).astype(BF)
@@ -90,7 +92,7 @@
                     win_ref[part, b, pl.ds(at, 16), :] = tile[row:row + 16, h * 128:(h + 1) * 128]
 
 
-def prep(images, row_list, labels, filters):
+def prep(me, tile_owner, images, row_list, labels, filters):
     vmem = pl.BlockSpec(memory_space=pltpu.VMEM)
     return pl.pallas_call(
         prep_kernel,
@@ -100,9 +102,9 @@
             jax.ShapeDtypeStruct((4, 1536, 256), BF),
             jax.ShapeDtypeStruct((ROWS, 256), BF),
             jax.ShapeDtypeStruct((ROWS, 128), BF),
-            jax.ShapeDtypeStruct((1, 2), jnp.int32),
+            jax.ShapeDtypeStruct((1, 4), jnp.int32),
         ),
-        in_specs=[vmem, vmem, vmem, pl.BlockSpec(memory_space=pl.ANY)],
+        in_specs=[pl.BlockSpec(memory_space=pltpu.SMEM), vmem, vmem, vmem, vmem, pl.BlockSpec(memory_space=pl.ANY)],
         out_specs=(vmem, vmem, vmem, vmem, vmem, pl.BlockSpec(memory_space=pltpu.SMEM)),
         scratch_shapes=[
             pltpu.VMEM((ROWS, 12288), BF),
@@ -113,7 +115,7 @@
         ],
         compiler_params=pltpu.CompilerParams(vmem_limit_bytes=40 * 2**20),
         name="prep",
-    )(jnp.pad(row_list, (0, 32)).reshape(1, 128), jnp.pad(labels, (0, 32)).reshape(1, 128), filters, images)
+    )(me, jnp.pad(tile_owner, (0, 256 - NTILES), constant_values=-1).reshape(1, 256), jnp.pad(row_list, (0, 32)).reshape(1, 128), jnp.pad(labels, (0, 32)).reshape(1, 128), filters, images)
 
 
 def conv_kernel(first, count, nblk_ref, win_ref, half_ref, w_ref, sel_ref, bias_ref, lab_ref, *refs):
@@ -250,7 +252,7 @@
     parts, (out_ref, peak_ref) = (refs[:n], refs[n:2 * n]), refs[2 * n:2 * n + 2]
     fa_ref, fb_ref, ft_ref, target_ref, left_ref, list_i, list_j, sem = refs[2 * n + 2:]
     held = (fa_ref, fb_ref)
-    me_tile = me_ref[0]
+    me_tile = me_ref[0, 2]
     copies = [
         [
             pltpu.make_async_copy(ref, held[part].at[start:start + size], sem.at[part * n + k])
@@ -324,6 +326,11 @@
         @pl.when(jnp.logical_not(second))
         def _():
             put(slot + FIRST, dot(ft_ref[list_i[slot]], fa_ref[:, pl.ds(at, 256)]))
+
+    top = jnp.max(jnp.max(peak_ref[...], axis=1, keepdims=True), axis=0, keepdims=True)
+    exponent = jnp.floor(jnp.log2(jnp.maximum(jnp.broadcast_to(top, (8, 256)), 1e-30)))
+    row = lax.broadcasted_iota(jnp.int32, (8, 256), 0)
+    peak_ref[...] = jnp.where(row == 0, exponent, jnp.exp2(13.0 - exponent))
 
 
 def gram(me, tile_owner, parts):
@@ -357,8 +364,8 @@
 
 
 def exchange(partial, peak, owned):
-    exponent = jnp.floor(jnp.log2(jnp.maximum(jnp.max(peak), 1e-30)))
-    scale = jnp.exp2(13.0 - exponent)
+    exponent = peak[0].reshape(1, 1, 1, 256)
+    scale = peak[1].reshape(1, 1, 1, 256)
 
     def some(count, partial):
         used = partial[:, :FIRST + count]
@@ -417,7 +424,8 @@
 
 
 def body(images, row_list, labels, filters, bias, tile_owner):
-    win, half, w, sel, lab, nblk = prep(images, row_list, labels, filters)
+    me = lax.axis_index("tile").astype(jnp.int32).reshape(1)
+    win, half, w, sel, lab, nblk = prep(me, tile_owner, images, row_list, labels, filters)
     bias4 = bias.reshape(4, 1, 256)
     own_a = conv(0, 2, nblk, win, half, w, sel, bias4, lab, 128)
     first_a = spread_first(own_a)
@@ -431,10 +439,8 @@
     part_a = spread_third(first_a, second_a)
     second_b = spread_second(first_b)
     part_b = spread_third(first_b, second_b)
-    me = jnp.stack([lax.axis_index("tile"), lax.axis_index("feat")]).astype(jnp.int32)
-    partial, peak = gram(me, tile_owner, (part_a, part_b))
-    owned = jnp.sum((tile_owner == me[0]).astype(jnp.int32))
-    return exchange(partial, peak, owned)
+    partial, peak = gram(nblk, tile_owner, (part_a, part_b))
+    return exchange(partial, peak, nblk[0, 3])
 
 
 def solution(mesh):

time: 169 us -> 160 us (0.947)
  the two profiles are of different devices: /device:TPU:1 before, /device:TPU:19 now
where the time goes in v7:
time: 160 us
  Pallas kernels  61.1 us (38%)
  starting transfers between devices  36.5 us (23%)
  blocking collectives  34.5 us (22%)
  local copies, waits for them, and re-layouts  12 us (8%)
  waiting for transfers between devices  11 us (7%)
  other arithmetic  2.87 us (2%)
  between operations  2.36 us (1%)
    ppermute x20, starting transfers between devices, send(): return lax.ppermute(block, 'tile', perm)  36.5 us
    pallas_call x3, Pallas kernels, conv(): pl.pallas_call(functools.partial(conv_kernel, first, count), out_shape=ja...  36.1 us
    all_to_all x1, blocking collectives, some(): got = lax.all_to_all(coded, 'feat', split_axis=0, concat_axis=0, tiled=True)  34.5 us
    pallas_call x1, Pallas kernels, gram(): pl.pallas_call(gram_kernel, out_shape=(jax.ShapeDtypeStruct((FEAT, SLOTS,...  17.3 us
    ppermute x20, waiting for transfers between devices, send(): return lax.ppermute(block, 'tile', perm)  11 us
    pallas_call x1, Pallas kernels, prep(): pl.pallas_call(prep_kernel, out_shape=(jax.ShapeDtypeStruct((16, NBLK, 16...  7.75 us
    unnamed x60, local copies, waits for them, and re-layouts  7.59 us
  transfers between devices with their start and end apart: 20, of which 7 were waited for; matrix products, arithmetic and copies ran while one was open for 1% of the time, Pallas kernels for 11%

profile of v7, /device:TPU:19, one launch (start us, length us, event | category | flops | bytes accessed | tf_op | source)
XLA Modules:
  0.0 160.3 jit_solution(14280540896885026773)
XLA Ops:
  2.0 1.7 %copy-done = bf16[96,12288]{1,0:T(8,128)(2,1)S(1)} copy-done((bf16[96,12288]{1,0:T(8,128)(2,1)S(1)}, bf16[96,12288]{1,0:T(8,128)(2,1)}, u32[]{:S(2)}) %copy-start) | copy-done | bytes 2359320
  4.6 7.8 %prep.1 = (bf16[16,6,160,128]{3,2,1,0:T(8,128)(2,1)S(1)}, bf16[16,80,128]{2,1,0:T(8,128)(2,1)S(1)}, bf16[4,1536,256]{2,1,0:T(8,128)(2,1)S(1)}, bf16[96,256]{1,0:...) custom-call(s32[1]{0:T(128)} %bitcast.12.me_ref, s32[1,256]{1,0:T(1,128)S(1)} %bitcast.39, ...), custom_call_target="tpu_custom_call" | custom-call | tf_op jit(solution)/shard_map/prep/pallas_call | solution.py:97
  13.1 17.8 %conv.3.refs_0_ = bf16[96,2176]{1,0:T(8,128)(2,1)S(1)} custom-call(s32[1,4]{1,0:T(1,128)S(1)} %get-tuple-element.41.nblk_ref.me_ref, bf16[16,6,160,128]{3,2,1,0:T(8,128)(2,1)S(1)} %get-tuple-element.42.win_ref, bf16[16,80,128]{2,1,0:T(8,128)(2,1)S(1)} %get-tuple-element.43.half_ref, bf16[4,1536,256]{2,1,0:T(8,128)(2,1)S(1)} %get-tuple-element.44.w_ref, ...), custom_call_target="tpu_custom_call" | custom-call | flops 22649241600 | bytes 8388608 | tf_op jit(solution)/shard_map/conv/pallas_call | solution.py:223
  30.9 1.3 collective-permute-start.1
  32.5 9.2 %conv.4 = bf16[96,1024]{1,0:T(8,128)(2,1)S(1)} custom-call(s32[1,4]{1,0:T(1,128)S(1)} %get-tuple-element.41.nblk_ref.me_ref, bf16[16,6,160,128]{3,2,1,0:T(8,128)(2,1)S(1)} %get-tuple-element.42.win_ref, bf16[16,80,128]{2,1,0:T(8,128)(2,1)S(1)} %get-tuple-element.43.half_ref, bf16[4,1536,256]{2,1,0:T(8,128)(2,1)S(1)} %get-tuple-element.44.w_ref, ...), custom_call_target="tpu_custom_call" | custom-call | flops 11324620800 | bytes 8388608 | tf_op jit(solution)/shard_map/conv/pallas_call | solution.py:223
  44.0 2.3 %collective-permute-start.7 = (bf16[384,2176]{1,0:T(8,128)(2,1)S(1)}, bf16[384,2176]{1,0:T(8,128)(2,1)S(1)}, u32[]{:S(2)}, u32[]{:S(2)}) collective-permute-start(bf16[384,2176]{1,0:T(8,128)(2,1)S(1)} %pad_maximum_fusion), channel_id=1, source_target_pairs={{0,1},{1,0},{2,3},{3,2},{4,5},{5,4},{6,7},{7,6},{8,9},{9,8},{10,11... | collective-permute-start | bytes 5013512 | tf_op jit(solution)/shard_map/ppermute | solution.py:396
  47.9 1.9 %copy-done.9 = bf16[4,1536,256]{2,1,0:T(8,128)(2,1)S(1)} copy-done((bf16[4,1536,256]{2,1,0:T(8,128)(2,1)S(1)}, bf16[4,1536,256]{2,1,0:T(8,128)(2,1)}, u32[]{:S(2)}) %copy-start.9) | copy-done | bytes 3145752
  49.8 9.2 %conv.5 = bf16[96,1024]{1,0:T(8,128)(2,1)S(1)} custom-call(s32[1,4]{1,0:T(1,128)S(1)} %get-tuple-element.41.nblk_ref.me_ref, bf16[16,6,160,128]{3,2,1,0:T(8,128)(2,1)S(1)} %copy-done.7, bf16[16,80,128]{2,1,0:T(8,128)(2,1)S(1)} %get-tuple-element.43.half_ref, bf16[4,1536,256]{2,1,0:T(8,128)(2,1)S(1)} %copy-done.9, ...), custom_call_target="tpu_custom_call" | custom-call | flops 11324620800 | bytes 8388608 | tf_op jit(solution)/shard_map/conv/pallas_call | solution.py:223
  60.2 1.8 %collective-permute-start.12 = (bf16[96,2048]{1,0:T(8,128)(2,1)S(1)}, bf16[96,2048]{1,0:T(8,128)(2,1)S(1)}, u32[]{:S(2)}, u32[]{:S(2)}) collective-permute-start(bf16[96,2048]{1,0:T(8,128)(2,1)S(1)} %pad_maximum_fusion.4.refs_11_), channel_id=1, source_target_pairs={{0,6},{1,7},{2,0},{3,1},{4,2},{5,3},{6,4},{7,5},{8,14},{9,15},{10,... | collective-permute-start | bytes 1179656 | tf_op jit(solution)/shard_map/ppermute | solution.py:396
  61.9 1.7 %collective-permute-start.10 = (bf16[96,2048]{1,0:T(8,128)(2,1)S(1)}, bf16[96,2048]{1,0:T(8,128)(2,1)S(1)}, u32[]{:S(2)}, u32[]{:S(2)}) collective-permute-start(bf16[96,2048]{1,0:T(8,128)(2,1)S(1)} %pad_maximum_fusion.4.refs_11_), channel_id=1, source_target_pairs={{0,8},{1,9},{2,10},{3,11},{4,12},{5,13},{6,14},{7,15},{8,0},{9,1},... | collective-permute-start | bytes 1179656 | tf_op jit(solution)/shard_map/ppermute | solution.py:396
  63.7 2.7 %collective-permute-start.6 = (bf16[96,2176]{1,0:T(8,128)(2,1)S(1)}, bf16[96,2176]{1,0:T(8,128)(2,1)S(1)}, u32[]{:S(2)}, u32[]{:S(2)}) collective-permute-start(bf16[96,2176]{1,0:T(8,128)(2,1)S(1)} %broadcast_select_fusion), channel_id=1, source_target_pairs={{0,2},{1,7},{2,4},{3,1},{4,6},{5,3},{6,0},{7,5},{8,10},{9,15},{10,... | collective-permute-start | bytes 1253384 | tf_op jit(solution)/shard_map/ppermute | solution.py:396
  66.4 2.0 %collective-permute-done.11.refs_13_ = bf16[96,2048]{1,0:T(8,128)(2,1)S(1)} collective-permute-done((bf16[96,2048]{1,0:T(8,128)(2,1)S(1)}, bf16[96,2048]{1,0:T(8,128)(2,1)S(1)}, u32[]{:S(2)}, u32[]{:S(2)}) %collective-permute-start.11) | collective-permute-done | bytes 393248 | tf_op jit(solution)/shard_map/ppermute | solution.py:396
  68.8 2.9 %collective-permute-start.15 = (bf16[96,2048]{1,0:T(8,128)(2,1)S(1)}, bf16[96,2048]{1,0:T(8,128)(2,1)S(1)}, u32[]{:S(2)}, u32[]{:S(2)}) collective-permute-start(bf16[96,2048]{1,0:T(8,128)(2,1)S(1)} %broadcast_select_fusion.3), channel_id=1, source_target_pairs={{0,2},{1,7},{2,4},{3,1},{4,6},{5,3},{6,0},{7,5},{8,10},{9,15},{10,... | collective-permute-start | bytes 1179656 | tf_op jit(solution)/shard_map/ppermute | solution.py:396
  71.7 2.5 %collective-permute-start.14 = (bf16[96,2048]{1,0:T(8,128)(2,1)S(1)}, bf16[96,2048]{1,0:T(8,128)(2,1)S(1)}, u32[]{:S(2)}, u32[]{:S(2)}) collective-permute-start(bf16[96,2048]{1,0:T(8,128)(2,1)S(1)} %collective-permute-done.10.refs_12_), channel_id=1, source_target_pairs={{0,6},{1,7},{2,0},{3,1},{4,2},{5,3},{6,4},{7,5},{8,14},{9,15},{10,... | collective-permute-start | bytes 1179656 | tf_op jit(solution)/shard_map/ppermute | solution.py:396
  74.3 1.9 %collective-permute-done.6.refs_7_ = bf16[96,2176]{1,0:T(8,128)(2,1)S(1)} collective-permute-done((bf16[96,2176]{1,0:T(8,128)(2,1)S(1)}, bf16[96,2176]{1,0:T(8,128)(2,1)S(1)}, u32[]{:S(2)}, u32[]{:S(2)}) %collective-permute-start.6) | collective-permute-done | bytes 417824 | tf_op jit(solution)/shard_map/ppermute | solution.py:396
  76.2 4.3 %collective-permute-start.17 = (bf16[384,2048]{1,0:T(8,128)(2,1)S(1)}, bf16[384,2048]{1,0:T(8,128)(2,1)}, u32[]{:S(2)}, u32[]{:S(2)}) collective-permute-start(bf16[384,2048]{1,0:T(8,128)(2,1)S(1)} %pad_maximum_fusion.1), channel_id=1, source_target_pairs={{0,1},{1,0},{2,3},{3,2},{4,5},{5,4},{6,7},{7,6},{8,9},{9,8},{10,11... | collective-permute-start | bytes 4718600 | tf_op jit(solution)/shard_map/ppermute | solution.py:396
  80.7 4.2 %collective-permute-start.8 = (bf16[288,2176]{1,0:T(8,128)(2,1)S(1)}, bf16[288,2176]{1,0:T(8,128)(2,1)S(1)}, u32[]{:S(2)}, u32[]{:S(2)}) collective-permute-start(bf16[288,2176]{1,0:T(8,128)(2,1)S(1)} %pad_maximum_fusion.2), channel_id=1, source_target_pairs={{0,1},{1,0},{2,3},{3,2},{4,5},{5,4},{6,7},{7,6},{8,9},{9,8},{10,11... | collective-permute-start | bytes 3760136 | tf_op jit(solution)/shard_map/ppermute | solution.py:396
  84.8 4.2 %collective-permute-start.9 = (bf16[96,2176]{1,0:T(8,128)(2,1)S(1)}, bf16[96,2176]{1,0:T(8,128)(2,1)S(1)}, u32[]{:S(2)}, u32[]{:S(2)}) collective-permute-start(bf16[96,2176]{1,0:T(8,128)(2,1)S(1)} %collective-permute-done.6.refs_7_), channel_id=1, source_target_pairs={{0,1},{1,0},{2,3},{3,2},{4,5},{5,4},{6,7},{7,6},{8,9},{9,8},{10,11... | collective-permute-start | bytes 1253384 | tf_op jit(solution)/shard_map/ppermute | solution.py:396
  90.4 2.7 %collective-permute-start.16 = (bf16[96,2048]{1,0:T(8,128)(2,1)S(1)}, bf16[96,2048]{1,0:T(8,128)(2,1)S(1)}, u32[]{:S(2)}, u32[]{:S(2)}) collective-permute-start(bf16[96,2048]{1,0:T(8,128)(2,1)S(1)} %broadcast_select_fusion.2), channel_id=1, source_target_pairs={{0,2},{1,7},{2,4},{3,1},{4,6},{5,3},{6,0},{7,5},{8,10},{9,15},{10,... | collective-permute-start | bytes 1179656 | tf_op jit(solution)/shard_map/ppermute | solution.py:396
  93.2 4.7 %collective-permute-done.16.refs_18_ = bf16[96,2048]{1,0:T(8,128)(2,1)S(1)} collective-permute-done((bf16[96,2048]{1,0:T(8,128)(2,1)S(1)}, bf16[96,2048]{1,0:T(8,128)(2,1)S(1)}, u32[]{:S(2)}, u32[]{:S(2)}) %collective-permute-start.16) | collective-permute-done | bytes 393248 | tf_op jit(solution)/shard_map/ppermute | solution.py:396
  97.9 1.7 %collective-permute-start.19 = (bf16[96,2048]{1,0:T(8,128)(2,1)S(1)}, bf16[96,2048]{1,0:T(8,128)(2,1)S(1)}, u32[]{:S(2)}, u32[]{:S(2)}) collective-permute-start(bf16[96,2048]{1,0:T(8,128)(2,1)S(1)} %collective-permute-done.16.refs_18_), channel_id=1, source_target_pairs={{0,1},{1,0},{2,3},{3,2},{4,5},{5,4},{6,7},{7,6},{8,9},{9,8},{10,11... | collective-permute-start | bytes 1179656 | tf_op jit(solution)/shard_map/ppermute | solution.py:396
  103.8 17.3 %gram.1 = (f32[8,25,32,256]{3,2,1,0:T(8,128)S(1)}, f32[8,256]{1,0:T(8,128)}) custom-call(s32[1,4]{1,0:T(1,128)} %copy-done.12, s32[136]{0:T(256)} %owner_ref.1, bf16[96,2176]{1,0:T(8,128)(2,1)} %copy-done.3, bf16[96,2176]{1,0:T(8,128)(2,1)} %copy-done.4, bf16[96,2176]{1,0:T(8,128)(2,1)} %copy-done.1, bf16[96,2176]{1,0:T(8,128)(2,1)} %copy-done.2, ...), custom_call_target="tpu_custom_call" | custom-call | flops 5000000000 | bytes 20971520 | tf_op jit(solution)/shard_map/gram/pallas_call | solution.py:339
  122.0 38.4 %conditional.1 = (f32[20,32,256]{2,1,0:T(8,128)}, f32[32,1000]{1,0:T(8,128)}) conditional(s32[]{:T(128)} %bitcast.16, (f32[1,1,1,256]{3,2,1,0:T(1,128)S(1)}, f32[8,25,32,256]{3,2,1,0:T(8,128)S(1)}, f32[1,1,1,256]{3,2,1,0:T(1,128)S(1)}) %tuple.21, (f32[1,1,1,256]{3,2,1,0:T(1,128)S(1)}, f32[8,25,32,256]{3,2,1,0:T(8,128)S(1)}, ...), branch_computations={%region_0.2_spmd, %region_2.4_spmd, %region_4.6_spmd} | conditional | flops 9625657 | bytes 22317266 | solution.py:381
  123.2 34.5 %all_to_all.14 = f16[8,25,32,256]{3,2,1,0:T(8,128)(2,1)S(1)} all-to-all(f16[8,25,32,256]{3,2,1,0:T(8,128)(2,1)S(1)} %select_convert_fusion.2), channel_id=1, replica_groups=mesh['feat'=8,'tile'=16] {'feat'}, dimensions={0} | all-to-all | bytes 6553600 | tf_op jit(solution)/shard_map/cond/branch_2_fun/all_to_all | solution.py:374
  (105 shorter events, 18.0 us)
Async XLA Ops:
  12.4 87.2 %copy-start.12 = (s32[1,4]{1,0:T(1,128)}, s32[1,4]{1,0:T(1,128)S(1)}, u32[]{:S(2)}) copy-start(s32[1,4]{1,0:T(1,128)S(1)} %get-tuple-element.41.nblk_ref.me_ref) | copy-start | bytes 52
  30.9 10.8 %collective-permute-start.1 = (bf16[96,2176]{1,0:T(8,128)(2,1)S(1)}, bf16[96,2176]{1,0:T(8,128)(2,1)S(1)}, u32[]{:S(2)}, u32[]{:S(2)}) collective-permute-start(bf16[96,2176]{1,0:T(8,128)(2,1)S(1)} %conv.3.refs_0_), channel_id=1, source_target_pairs={{0,2},{1,3},{2,4},{3,5},{4,6},{5,7},{6,0},{7,1},{8,10},{9,11},{10,... | collective-permute-start | bytes 1253384 | tf_op jit(solution)/shard_map/ppermute | solution.py:396
  32.2 10.2 %collective-permute-start.2 = (bf16[96,2176]{1,0:T(8,128)(2,1)S(1)}, bf16[96,2176]{1,0:T(8,128)(2,1)S(1)}, u32[]{:S(2)}, u32[]{:S(2)}) collective-permute-start(bf16[96,2176]{1,0:T(8,128)(2,1)S(1)} %conv.3.refs_0_), channel_id=1, source_target_pairs={{0,6},{1,7},{2,0},{3,1},{4,2},{5,3},{6,4},{7,5},{8,14},{9,15},{10,... | collective-permute-start | bytes 1253384 | tf_op jit(solution)/shard_map/ppermute | solution.py:396
  32.4 11.4 %collective-permute-start = (bf16[96,2176]{1,0:T(8,128)(2,1)S(1)}, bf16[96,2176]{1,0:T(8,128)(2,1)S(1)}, u32[]{:S(2)}, u32[]{:S(2)}) collective-permute-start(bf16[96,2176]{1,0:T(8,128)(2,1)S(1)} %conv.3.refs_0_), channel_id=1, source_target_pairs={{0,8},{1,9},{2,10},{3,11},{4,12},{5,13},{6,14},{7,15},{8,0},{9,1},... | collective-permute-start | bytes 1253384 | tf_op jit(solution)/shard_map/ppermute | solution.py:396
  42.5 16.6 %collective-permute-start.3 = (bf16[96,2176]{1,0:T(8,128)(2,1)S(1)}, bf16[96,2176]{1,0:T(8,128)(2,1)S(1)}, u32[]{:S(2)}, u32[]{:S(2)}) collective-permute-start(bf16[96,2176]{1,0:T(8,128)(2,1)S(1)} %broadcast_select_fusion.1), channel_id=1, source_target_pairs={{0,2},{1,7},{2,4},{3,1},{4,6},{5,3},{6,0},{7,5},{8,10},{9,15},{10,... | collective-permute-start | bytes 1253384 | tf_op jit(solution)/shard_map/ppermute | solution.py:396
  44.0 57.5 %collective-permute-start.7 = (bf16[384,2176]{1,0:T(8,128)(2,1)S(1)}, bf16[384,2176]{1,0:T(8,128)(2,1)S(1)}, u32[]{:S(2)}, u32[]{:S(2)}) collective-permute-start(bf16[384,2176]{1,0:T(8,128)(2,1)S(1)} %pad_maximum_fusion), channel_id=1, source_target_pairs={{0,1},{1,0},{2,3},{3,2},{4,5},{5,4},{6,7},{7,6},{8,9},{9,8},{10,11... | collective-permute-start | bytes 5013512 | tf_op jit(solution)/shard_map/ppermute | solution.py:396
  46.3 12.8 %collective-permute-start.4 = (bf16[96,2176]{1,0:T(8,128)(2,1)S(1)}, bf16[96,2176]{1,0:T(8,128)(2,1)S(1)}, u32[]{:S(2)}, u32[]{:S(2)}) collective-permute-start(bf16[96,2176]{1,0:T(8,128)(2,1)S(1)} %collective-permute-done.refs_0_.refs_1_), channel_id=1, source_target_pairs={{0,2},{1,3},{2,4},{3,5},{4,6},{5,7},{6,0},{7,1},{8,10},{9,11},{10,... | collective-permute-start | bytes 1253384 | tf_op jit(solution)/shard_map/ppermute | solution.py:396
  47.4 11.6 %collective-permute-start.5 = (bf16[96,2176]{1,0:T(8,128)(2,1)S(1)}, bf16[96,2176]{1,0:T(8,128)(2,1)S(1)}, u32[]{:S(2)}, u32[]{:S(2)}) collective-permute-start(bf16[96,2176]{1,0:T(8,128)(2,1)S(1)} %collective-permute-done.refs_0_.refs_1_), channel_id=1, source_target_pairs={{0,6},{1,7},{2,0},{3,1},{4,2},{5,3},{6,4},{7,5},{8,14},{9,15},{10,... | collective-permute-start | bytes 1253384 | tf_op jit(solution)/shard_map/ppermute | solution.py:396
  59.0 21.6 %copy-start.15 = (bf16[96,2048]{1,0:T(8,128)(2,1)}, bf16[96,2048]{1,0:T(8,128)(2,1)S(1)}, u32[]{:S(2)}) copy-start(bf16[96,2048]{1,0:T(8,128)(2,1)S(1)} %pad_maximum_fusion.4.refs_11_) | copy-start | bytes 1179652
  59.1 21.5 %copy-start.20 = (bf16[96,2176]{1,0:T(8,128)(2,1)}, bf16[96,2176]{1,0:T(8,128)(2,1)S(1)}, u32[]{:S(2)}) copy-start(bf16[96,2176]{1,0:T(8,128)(2,1)S(1)} %collective-permute-done.3.refs_6_) | copy-start | bytes 1253380
  59.1 9.3 %collective-permute-start.11 = (bf16[96,2048]{1,0:T(8,128)(2,1)S(1)}, bf16[96,2048]{1,0:T(8,128)(2,1)S(1)}, u32[]{:S(2)}, u32[]{:S(2)}) collective-permute-start(bf16[96,2048]{1,0:T(8,128)(2,1)S(1)} %pad_maximum_fusion.4.refs_11_), channel_id=1, source_target_pairs={{0,2},{1,3},{2,4},{3,5},{4,6},{5,7},{6,0},{7,1},{8,10},{9,11},{10,... | collective-permute-start | bytes 1179656 | tf_op jit(solution)/shard_map/ppermute | solution.py:396
  60.2 8.6 %collective-permute-start.12 = (bf16[96,2048]{1,0:T(8,128)(2,1)S(1)}, bf16[96,2048]{1,0:T(8,128)(2,1)S(1)}, u32[]{:S(2)}, u32[]{:S(2)}) collective-permute-start(bf16[96,2048]{1,0:T(8,128)(2,1)S(1)} %pad_maximum_fusion.4.refs_11_), channel_id=1, source_target_pairs={{0,6},{1,7},{2,0},{3,1},{4,2},{5,3},{6,4},{7,5},{8,14},{9,15},{10,... | collective-permute-start | bytes 1179656 | tf_op jit(solution)/shard_map/ppermute | solution.py:396
  61.9 9.8 %collective-permute-start.10 = (bf16[96,2048]{1,0:T(8,128)(2,1)S(1)}, bf16[96,2048]{1,0:T(8,128)(2,1)S(1)}, u32[]{:S(2)}, u32[]{:S(2)}) collective-permute-start(bf16[96,2048]{1,0:T(8,128)(2,1)S(1)} %pad_maximum_fusion.4.refs_11_), channel_id=1, source_target_pairs={{0,8},{1,9},{2,10},{3,11},{4,12},{5,13},{6,14},{7,15},{8,0},{9,1},... | collective-permute-start | bytes 1179656 | tf_op jit(solution)/shard_map/ppermute | solution.py:396
  63.7 12.5 %collective-permute-start.6 = (bf16[96,2176]{1,0:T(8,128)(2,1)S(1)}, bf16[96,2176]{1,0:T(8,128)(2,1)S(1)}, u32[]{:S(2)}, u32[]{:S(2)}) collective-permute-start(bf16[96,2176]{1,0:T(8,128)(2,1)S(1)} %broadcast_select_fusion), channel_id=1, source_target_pairs={{0,2},{1,7},{2,4},{3,1},{4,6},{5,3},{6,0},{7,5},{8,10},{9,15},{10,... | collective-permute-start | bytes 1253384 | tf_op jit(solution)/shard_map/ppermute | solution.py:396
  68.8 11.8 %collective-permute-start.15 = (bf16[96,2048]{1,0:T(8,128)(2,1)S(1)}, bf16[96,2048]{1,0:T(8,128)(2,1)S(1)}, u32[]{:S(2)}, u32[]{:S(2)}) collective-permute-start(bf16[96,2048]{1,0:T(8,128)(2,1)S(1)} %broadcast_select_fusion.3), channel_id=1, source_target_pairs={{0,2},{1,7},{2,4},{3,1},{4,6},{5,3},{6,0},{7,5},{8,10},{9,15},{10,... | collective-permute-start | bytes 1179656 | tf_op jit(solution)/shard_map/ppermute | solution.py:396
  71.7 13.1 %collective-permute-start.13 = (bf16[96,2048]{1,0:T(8,128)(2,1)S(1)}, bf16[96,2048]{1,0:T(8,128)(2,1)S(1)}, u32[]{:S(2)}, u32[]{:S(2)}) collective-permute-start(bf16[96,2048]{1,0:T(8,128)(2,1)S(1)} %collective-permute-done.10.refs_12_), channel_id=1, source_target_pairs={{0,2},{1,3},{2,4},{3,5},{4,6},{5,7},{6,0},{7,1},{8,10},{9,11},{10,... | collective-permute-start | bytes 1179656 | tf_op jit(solution)/shard_map/ppermute | solution.py:396
  71.7 17.3 %collective-permute-start.14 = (bf16[96,2048]{1,0:T(8,128)(2,1)S(1)}, bf16[96,2048]{1,0:T(8,128)(2,1)S(1)}, u32[]{:S(2)}, u32[]{:S(2)}) collective-permute-start(bf16[96,2048]{1,0:T(8,128)(2,1)S(1)} %collective-permute-done.10.refs_12_), channel_id=1, source_target_pairs={{0,6},{1,7},{2,0},{3,1},{4,2},{5,3},{6,4},{7,5},{8,14},{9,15},{10,... | collective-permute-start | bytes 1179656 | tf_op jit(solution)/shard_map/ppermute | solution.py:396
  76.2 25.3 %copy-start.26 = (bf16[96,2176]{1,0:T(8,128)(2,1)}, bf16[96,2176]{1,0:T(8,128)(2,1)S(1)}, u32[]{:S(2)}) copy-start(bf16[96,2176]{1,0:T(8,128)(2,1)S(1)} %collective-permute-done.6.refs_7_) | copy-start | bytes 1253380
  76.2 27.6 %collective-permute-start.17 = (bf16[384,2048]{1,0:T(8,128)(2,1)S(1)}, bf16[384,2048]{1,0:T(8,128)(2,1)}, u32[]{:S(2)}, u32[]{:S(2)}) collective-permute-start(bf16[384,2048]{1,0:T(8,128)(2,1)S(1)} %pad_maximum_fusion.1), channel_id=1, source_target_pairs={{0,1},{1,0},{2,3},{3,2},{4,5},{5,4},{6,7},{7,6},{8,9},{9,8},{10,11... | collective-permute-start | bytes 4718600 | tf_op jit(solution)/shard_map/ppermute | solution.py:396
  80.7 20.8 %collective-permute-start.8 = (bf16[288,2176]{1,0:T(8,128)(2,1)S(1)}, bf16[288,2176]{1,0:T(8,128)(2,1)S(1)}, u32[]{:S(2)}, u32[]{:S(2)}) collective-permute-start(bf16[288,2176]{1,0:T(8,128)(2,1)S(1)} %pad_maximum_fusion.2), channel_id=1, source_target_pairs={{0,1},{1,0},{2,3},{3,2},{4,5},{5,4},{6,7},{7,6},{8,9},{9,8},{10,11... | collective-permute-start | bytes 3760136 | tf_op jit(solution)/shard_map/ppermute | solution.py:396
  84.8 5.6 %collective-permute-start.9 = (bf16[96,2176]{1,0:T(8,128)(2,1)S(1)}, bf16[96,2176]{1,0:T(8,128)(2,1)S(1)}, u32[]{:S(2)}, u32[]{:S(2)}) collective-permute-start(bf16[96,2176]{1,0:T(8,128)(2,1)S(1)} %collective-permute-done.6.refs_7_), channel_id=1, source_target_pairs={{0,1},{1,0},{2,3},{3,2},{4,5},{5,4},{6,7},{7,6},{8,9},{9,8},{10,11... | collective-permute-start | bytes 1253384 | tf_op jit(solution)/shard_map/ppermute | solution.py:396
  89.2 12.4 %collective-permute-start.18 = (bf16[288,2048]{1,0:T(8,128)(2,1)S(1)}, bf16[288,2048]{1,0:T(8,128)(2,1)S(1)}, u32[]{:S(2)}, u32[]{:S(2)}) collective-permute-start(bf16[288,2048]{1,0:T(8,128)(2,1)S(1)} %pad_maximum_fusion.3), channel_id=1, source_target_pairs={{0,1},{1,0},{2,3},{3,2},{4,5},{5,4},{6,7},{7,6},{8,9},{9,8},{10,11... | collective-permute-start | bytes 3538952 | tf_op jit(solution)/shard_map/ppermute | solution.py:396
  90.4 7.4 %collective-permute-start.16 = (bf16[96,2048]{1,0:T(8,128)(2,1)S(1)}, bf16[96,2048]{1,0:T(8,128)(2,1)S(1)}, u32[]{:S(2)}, u32[]{:S(2)}) collective-permute-start(bf16[96,2048]{1,0:T(8,128)(2,1)S(1)} %broadcast_select_fusion.2), channel_id=1, source_target_pairs={{0,2},{1,7},{2,4},{3,1},{4,6},{5,3},{6,0},{7,5},{8,10},{9,15},{10,... | collective-permute-start | bytes 1179656 | tf_op jit(solution)/shard_map/ppermute | solution.py:396
  97.9 3.6 %collective-permute-start.19 = (bf16[96,2048]{1,0:T(8,128)(2,1)S(1)}, bf16[96,2048]{1,0:T(8,128)(2,1)S(1)}, u32[]{:S(2)}, u32[]{:S(2)}) collective-permute-start(bf16[96,2048]{1,0:T(8,128)(2,1)S(1)} %collective-permute-done.16.refs_18_), channel_id=1, source_target_pairs={{0,1},{1,0},{2,3},{3,2},{4,5},{5,4},{6,7},{7,6},{8,9},{9,8},{10,11... | collective-permute-start | bytes 1179656 | tf_op jit(solution)/shard_map/ppermute | solution.py:396
  (26 other events, 290.6 us)

commit v8 on v7

--- a/solution.py
+++ b/solution.py
@@ -115,7 +115,7 @@
         ],
         compiler_params=pltpu.CompilerParams(vmem_limit_bytes=40 * 2**20),
         name="prep",
-    )(me, jnp.pad(tile_owner, (0, 256 - NTILES), constant_values=-1).reshape(1, 256), jnp.pad(row_list, (0, 32)).reshape(1, 128), jnp.pad(labels, (0, 32)).reshape(1, 128), filters, images)
+    )(me, tile_owner.reshape(1, NTILES), jnp.pad(row_list, (0, 32)).reshape(1, 128), jnp.pad(labels, (0, 32)).reshape(1, 128), filters, images)
 
 
 def conv_kernel(first, count, nblk_ref, win_ref, half_ref, w_ref, sel_ref, bias_ref, lab_ref, *refs):
@@ -351,7 +351,7 @@
             pltpu.SMEM((OWNED,), jnp.int32),
             pltpu.SemaphoreType.DMA((2 * len(BLOCKS),)),
         ],
-        compiler_params=pltpu.CompilerParams(vmem_limit_bytes=56 * 2**20),
+        compiler_params=pltpu.CompilerParams(vmem_limit_bytes=40 * 2**20),
         cost_estimate=pl.CostEstimate(flops=5 * 10**9, bytes_accessed=20 * 2**20, transcendentals=0),
         name="gram",
     )(me, tile_owner, *parts[0], *parts[1])

time: 160 us -> 162 us (1.012)
  the two profiles are of different devices: /device:TPU:19 before, /device:TPU:0 now
where the time goes in v8:
time: 162 us; the launch traced here: 163 us
  Pallas kernels  63.8 us (39%)
  blocking collectives  32.5 us (20%)
  waiting for transfers between devices  32 us (20%)
  starting transfers between devices  20.3 us (13%)
  local copies, waits for them, and re-layouts  8.87 us (5%)
  other arithmetic  2.95 us (2%)
  between operations  2.19 us (1%)
    pallas_call x3, Pallas kernels, conv(): pl.pallas_call(functools.partial(conv_kernel, first, count), out_shape=ja...  36.1 us
    all_to_all x1, blocking collectives, some(): got = lax.all_to_all(coded, 'feat', split_axis=0, concat_axis=0, tiled=True)  32.5 us
    ppermute x20, waiting for transfers between devices, send(): return lax.ppermute(block, 'tile', perm)  32 us
    ppermute x20, starting transfers between devices, send(): return lax.ppermute(block, 'tile', perm)  20.3 us
    pallas_call x1, Pallas kernels, gram(): pl.pallas_call(gram_kernel, out_shape=(jax.ShapeDtypeStruct((FEAT, SLOTS,...  20 us
    pallas_call x1, Pallas kernels, prep(): pl.pallas_call(prep_kernel, out_shape=(jax.ShapeDtypeStruct((16, NBLK, 16...  7.75 us
    unnamed x20, local copies, waits for them, and re-layouts  5.94 us
  transfers between devices with their start and end apart: 20, of which 9 were waited for; matrix products, arithmetic and copies ran while one was open for 1% of the time, Pallas kernels for 11%

profile of v8, /device:TPU:0, one launch (start us, length us, event | category | flops | bytes accessed | tf_op | source)
XLA Modules:
  0.0 162.8 jit_solution(3987387091646691614)
XLA Ops:
  1.3 1.7 %copy-done = bf16[96,12288]{1,0:T(8,128)(2,1)S(1)} copy-done((bf16[96,12288]{1,0:T(8,128)(2,1)S(1)}, bf16[96,12288]{1,0:T(8,128)(2,1)}, u32[]{:S(2)}) %copy-start) | copy-done | bytes 2359320
  4.6 7.8 %prep.1 = (bf16[16,6,160,128]{3,2,1,0:T(8,128)(2,1)S(1)}, bf16[16,80,128]{2,1,0:T(8,128)(2,1)S(1)}, bf16[4,1536,256]{2,1,0:T(8,128)(2,1)S(1)}, bf16[96,256]{1,0:...) custom-call(s32[1]{0:T(128)} %bitcast.12.me_ref, s32[1,136]{1,0:T(1,128)S(1)} %bitcast.39, ...), custom_call_target="tpu_custom_call" | custom-call | tf_op jit(solution)/shard_map/prep/pallas_call | solution.py:97
  13.1 17.8 %conv.3.refs_0_ = bf16[96,2176]{1,0:T(8,128)(2,1)S(1)} custom-call(s32[1,4]{1,0:T(1,128)S(1)} %get-tuple-element.41.nblk_ref.me_ref, bf16[16,6,160,128]{3,2,1,0:T(8,128)(2,1)S(1)} %get-tuple-element.42.win_ref, bf16[16,80,128]{2,1,0:T(8,128)(2,1)S(1)} %get-tuple-element.43.half_ref, bf16[4,1536,256]{2,1,0:T(8,128)(2,1)S(1)} %get-tuple-element.44.w_ref, ...), custom_call_target="tpu_custom_call" | custom-call | flops 22649241600 | bytes 8388608 | tf_op jit(solution)/shard_map/conv/pallas_call | solution.py:223
  30.9 1.6 %collective-permute-start.1 = (bf16[96,2176]{1,0:T(8,128)(2,1)S(1)}, bf16[96,2176]{1,0:T(8,128)(2,1)S(1)}, u32[]{:S(2)}, u32[]{:S(2)}) collective-permute-start(bf16[96,2176]{1,0:T(8,128)(2,1)S(1)} %conv.3.refs_0_), channel_id=1, source_target_pairs={{0,2},{1,3},{2,4},{3,5},{4,6},{5,7},{6,0},{7,1},{8,10},{9,11},{10,... | collective-permute-start | bytes 1253384 | tf_op jit(solution)/shard_map/ppermute | solution.py:396
  32.5 1.7 %collective-permute-start.2 = (bf16[96,2176]{1,0:T(8,128)(2,1)S(1)}, bf16[96,2176]{1,0:T(8,128)(2,1)S(1)}, u32[]{:S(2)}, u32[]{:S(2)}) collective-permute-start(bf16[96,2176]{1,0:T(8,128)(2,1)S(1)} %conv.3.refs_0_), channel_id=1, source_target_pairs={{0,6},{1,7},{2,0},{3,1},{4,2},{5,3},{6,4},{7,5},{8,14},{9,15},{10,... | collective-permute-start | bytes 1253384 | tf_op jit(solution)/shard_map/ppermute | solution.py:396
  34.2 3.3 %collective-permute-start = (bf16[96,2176]{1,0:T(8,128)(2,1)S(1)}, bf16[96,2176]{1,0:T(8,128)(2,1)S(1)}, u32[]{:S(2)}, u32[]{:S(2)}) collective-permute-start(bf16[96,2176]{1,0:T(8,128)(2,1)S(1)} %conv.3.refs_0_), channel_id=1, source_target_pairs={{0,8},{1,9},{2,10},{3,11},{4,12},{5,13},{6,14},{7,15},{8,0},{9,1},... | collective-permute-start | bytes 1253384 | tf_op jit(solution)/shard_map/ppermute | solution.py:396
  37.5 9.2 %conv.4 = bf16[96,1024]{1,0:T(8,128)(2,1)S(1)} custom-call(s32[1,4]{1,0:T(1,128)S(1)} %get-tuple-element.41.nblk_ref.me_ref, bf16[16,6,160,128]{3,2,1,0:T(8,128)(2,1)S(1)} %get-tuple-element.42.win_ref, bf16[16,80,128]{2,1,0:T(8,128)(2,1)S(1)} %get-tuple-element.43.half_ref, bf16[4,1536,256]{2,1,0:T(8,128)(2,1)S(1)} %get-tuple-element.44.w_ref, ...), custom_call_target="tpu_custom_call" | custom-call | flops 11324620800 | bytes 8388608 | tf_op jit(solution)/shard_map/conv/pallas_call | solution.py:223
  49.0 1.2 collective-permute-start.4
  50.3 2.0 %collective-permute-start.5 = (bf16[96,2176]{1,0:T(8,128)(2,1)S(1)}, bf16[96,2176]{1,0:T(8,128)(2,1)S(1)}, u32[]{:S(2)}, u32[]{:S(2)}) collective-permute-start(bf16[96,2176]{1,0:T(8,128)(2,1)S(1)} %collective-permute-done.refs_0_.refs_1_), channel_id=1, source_target_pairs={{0,6},{1,7},{2,0},{3,1},{4,2},{5,3},{6,4},{7,5},{8,14},{9,15},{10,... | collective-permute-start | bytes 1253384 | tf_op jit(solution)/shard_map/ppermute | solution.py:396
  52.3 1.9 %copy-done.7 = bf16[4,1536,256]{2,1,0:T(8,128)(2,1)S(1)} copy-done((bf16[4,1536,256]{2,1,0:T(8,128)(2,1)S(1)}, bf16[4,1536,256]{2,1,0:T(8,128)(2,1)}, u32[]{:S(2)}) %copy-start.7) | copy-done | bytes 3145752
  54.2 9.2 %conv.5 = bf16[96,1024]{1,0:T(8,128)(2,1)S(1)} custom-call(s32[1,4]{1,0:T(1,128)S(1)} %get-tuple-element.41.nblk_ref.me_ref, bf16[16,6,160,128]{3,2,1,0:T(8,128)(2,1)S(1)} %copy-done.5, bf16[16,80,128]{2,1,0:T(8,128)(2,1)S(1)} %get-tuple-element.43.half_ref, bf16[4,1536,256]{2,1,0:T(8,128)(2,1)S(1)} %copy-done.7, ...), custom_call_target="tpu_custom_call" | custom-call | flops 11324620800 | bytes 8388608 | tf_op jit(solution)/shard_map/conv/pallas_call | solution.py:223
  63.4 1.8 %collective-permute-done.4.refs_4_ = bf16[96,2176]{1,0:T(8,128)(2,1)S(1)} collective-permute-done((bf16[96,2176]{1,0:T(8,128)(2,1)S(1)}, bf16[96,2176]{1,0:T(8,128)(2,1)S(1)}, u32[]{:S(2)}, u32[]{:S(2)}) %collective-permute-start.4) | collective-permute-done | bytes 417824 | tf_op jit(solution)/shard_map/ppermute | solution.py:396
  65.2 3.2 %collective-permute-start.12 = (bf16[96,2048]{1,0:T(8,128)(2,1)S(1)}, bf16[96,2048]{1,0:T(8,128)(2,1)S(1)}, u32[]{:S(2)}, u32[]{:S(2)}) collective-permute-start(bf16[96,2048]{1,0:T(8,128)(2,1)S(1)} %pad_maximum_fusion.4.refs_11_), channel_id=1, source_target_pairs={{0,6},{1,7},{2,0},{3,1},{4,2},{5,3},{6,4},{7,5},{8,14},{9,15},{10,... | collective-permute-start | bytes 1179656 | tf_op jit(solution)/shard_map/ppermute | solution.py:396
  69.5 6.9 %collective-permute-done.11.refs_13_ = bf16[96,2048]{1,0:T(8,128)(2,1)S(1)} collective-permute-done((bf16[96,2048]{1,0:T(8,128)(2,1)S(1)}, bf16[96,2048]{1,0:T(8,128)(2,1)S(1)}, u32[]{:S(2)}, u32[]{:S(2)}) %collective-permute-start.11) | collective-permute-done | bytes 393248 | tf_op jit(solution)/shard_map/ppermute | solution.py:396
  76.4 1.6 collective-permute-done.12.refs_14_
  78.1 1.1 collective-permute-start.15
  80.0 2.6 %collective-permute-start.14 = (bf16[96,2048]{1,0:T(8,128)(2,1)S(1)}, bf16[96,2048]{1,0:T(8,128)(2,1)S(1)}, u32[]{:S(2)}, u32[]{:S(2)}) collective-permute-start(bf16[96,2048]{1,0:T(8,128)(2,1)S(1)} %collective-permute-done.10.refs_12_), channel_id=1, source_target_pairs={{0,6},{1,7},{2,0},{3,1},{4,2},{5,3},{6,4},{7,5},{8,14},{9,15},{10,... | collective-permute-start | bytes 1179656 | tf_op jit(solution)/shard_map/ppermute | solution.py:396
  83.0 6.3 %collective-permute-done.15.refs_17_ = bf16[96,2048]{1,0:T(8,128)(2,1)S(1)} collective-permute-done((bf16[96,2048]{1,0:T(8,128)(2,1)S(1)}, bf16[96,2048]{1,0:T(8,128)(2,1)S(1)}, u32[]{:S(2)}, u32[]{:S(2)}) %collective-permute-start.15) | collective-permute-done | bytes 393248 | tf_op jit(solution)/shard_map/ppermute | solution.py:396
  89.3 4.2 %collective-permute-done.13.refs_15_ = bf16[96,2048]{1,0:T(8,128)(2,1)S(1)} collective-permute-done((bf16[96,2048]{1,0:T(8,128)(2,1)S(1)}, bf16[96,2048]{1,0:T(8,128)(2,1)S(1)}, u32[]{:S(2)}, u32[]{:S(2)}) %collective-permute-start.13) | collective-permute-done | bytes 393248 | tf_op jit(solution)/shard_map/ppermute | solution.py:396
  95.3 9.0 %collective-permute-done.16.refs_18_ = bf16[96,2048]{1,0:T(8,128)(2,1)S(1)} collective-permute-done((bf16[96,2048]{1,0:T(8,128)(2,1)S(1)}, bf16[96,2048]{1,0:T(8,128)(2,1)S(1)}, u32[]{:S(2)}, u32[]{:S(2)}) %collective-permute-start.16) | collective-permute-done | bytes 393248 | tf_op jit(solution)/shard_map/ppermute | solution.py:396
  106.2 20.0 %gram.1 = (f32[8,25,32,256]{3,2,1,0:T(8,128)S(1)}, f32[8,256]{1,0:T(8,128)S(1)}) custom-call(s32[1,4]{1,0:T(1,128)S(1)} %get-tuple-element.41.nblk_ref.me_ref, s32[136]{0:T(256)S(1)} %copy-done.3, bf16[96,2176]{1,0:T(8,128)(2,1)S(1)} %conv.3.refs_0_, bf16[96,2176]{1,0:T(8,128)(2,1)S(1)} %collective-permute-done.refs_0_.refs_1_, ...), custom_call_target="tpu_custom_call" | custom-call | flops 5000000000 | bytes 20971520 | tf_op jit(solution)/shard_map/gram/pallas_call | solution.py:339
  126.3 36.5 %conditional.1 = (f32[20,32,256]{2,1,0:T(8,128)}, f32[32,1000]{1,0:T(8,128)}) conditional(s32[]{:T(128)} %bitcast.16, (f32[1,1,1,256]{3,2,1,0:T(1,128)S(1)}, f32[8,25,32,256]{3,2,1,0:T(8,128)S(1)}, f32[1,1,1,256]{3,2,1,0:T(1,128)S(1)}) %tuple.21, (f32[1,1,1,256]{3,2,1,0:T(1,128)S(1)}, f32[8,25,32,256]{3,2,1,0:T(8,128)S(1)}, ...), branch_computations={%region_0.2_spmd, %region_2.4_spmd, %region_4.6_spmd} | conditional | flops 9625657 | bytes 22317266 | solution.py:381
  126.3 1.3 select_convert_fusion.2
  127.7 32.5 %all_to_all.14 = f16[8,25,32,256]{3,2,1,0:T(8,128)(2,1)S(1)} all-to-all(f16[8,25,32,256]{3,2,1,0:T(8,128)(2,1)S(1)} %select_convert_fusion.2), channel_id=1, replica_groups=mesh['feat'=8,'tile'=16] {'feat'}, dimensions={0} | all-to-all | bytes 6553600 | tf_op jit(solution)/shard_map/cond/branch_2_fun/all_to_all | solution.py:374
  (64 shorter events, 12.7 us)
Async XLA Ops:
  12.4 25.1 %copy-start.4 = (bf16[16,6,160,128]{3,2,1,0:T(8,128)(2,1)}, bf16[16,6,160,128]{3,2,1,0:T(8,128)(2,1)S(1)}, u32[]{:S(2)}) copy-start(bf16[16,6,160,128]{3,2,1,0:T(8,128)(2,1)S(1)} %get-tuple-element.42.win_ref) | copy-start | bytes 11796484
  12.4 25.1 %copy-start.6 = (bf16[4,1536,256]{2,1,0:T(8,128)(2,1)}, bf16[4,1536,256]{2,1,0:T(8,128)(2,1)S(1)}, u32[]{:S(2)}) copy-start(bf16[4,1536,256]{2,1,0:T(8,128)(2,1)S(1)} %get-tuple-element.44.w_ref) | copy-start | bytes 9437188
  13.1 24.3 %copy-start.9 = (f32[1024]{0:T(1024)S(1)}, f32[1024]{0:T(1024)}, u32[]{:S(2)}) copy-start(f32[1024]{0:T(1024)} %param.13) | copy-start | bytes 12292
  30.9 15.8 %collective-permute-start.1 = (bf16[96,2176]{1,0:T(8,128)(2,1)S(1)}, bf16[96,2176]{1,0:T(8,128)(2,1)S(1)}, u32[]{:S(2)}, u32[]{:S(2)}) collective-permute-start(bf16[96,2176]{1,0:T(8,128)(2,1)S(1)} %conv.3.refs_0_), channel_id=1, source_target_pairs={{0,2},{1,3},{2,4},{3,5},{4,6},{5,7},{6,0},{7,1},{8,10},{9,11},{10,... | collective-permute-start | bytes 1253384 | tf_op jit(solution)/shard_map/ppermute | solution.py:396
  32.5 14.1 %collective-permute-start.2 = (bf16[96,2176]{1,0:T(8,128)(2,1)S(1)}, bf16[96,2176]{1,0:T(8,128)(2,1)S(1)}, u32[]{:S(2)}, u32[]{:S(2)}) collective-permute-start(bf16[96,2176]{1,0:T(8,128)(2,1)S(1)} %conv.3.refs_0_), channel_id=1, source_target_pairs={{0,6},{1,7},{2,0},{3,1},{4,2},{5,3},{6,4},{7,5},{8,14},{9,15},{10,... | collective-permute-start | bytes 1253384 | tf_op jit(solution)/shard_map/ppermute | solution.py:396
  34.2 14.0 %collective-permute-start = (bf16[96,2176]{1,0:T(8,128)(2,1)S(1)}, bf16[96,2176]{1,0:T(8,128)(2,1)S(1)}, u32[]{:S(2)}, u32[]{:S(2)}) collective-permute-start(bf16[96,2176]{1,0:T(8,128)(2,1)S(1)} %conv.3.refs_0_), channel_id=1, source_target_pairs={{0,8},{1,9},{2,10},{3,11},{4,12},{5,13},{6,14},{7,15},{8,0},{9,1},... | collective-permute-start | bytes 1253384 | tf_op jit(solution)/shard_map/ppermute | solution.py:396
  46.7 16.6 %collective-permute-start.3 = (bf16[96,2176]{1,0:T(8,128)(2,1)S(1)}, bf16[96,2176]{1,0:T(8,128)(2,1)S(1)}, u32[]{:S(2)}, u32[]{:S(2)}) collective-permute-start(bf16[96,2176]{1,0:T(8,128)(2,1)S(1)} %broadcast_select_fusion.1), channel_id=1, source_target_pairs={{0,2},{1,7},{2,4},{3,1},{4,6},{5,3},{6,0},{7,5},{8,10},{9,15},{10,... | collective-permute-start | bytes 1253384 | tf_op jit(solution)/shard_map/ppermute | solution.py:396
  48.3 57.9 %collective-permute-start.7 = (bf16[384,2176]{1,0:T(8,128)(2,1)S(1)}, bf16[384,2176]{1,0:T(8,128)(2,1)S(1)}, u32[]{:S(2)}, u32[]{:S(2)}) collective-permute-start(bf16[384,2176]{1,0:T(8,128)(2,1)S(1)} %pad_maximum_fusion), channel_id=1, source_target_pairs={{0,1},{1,0},{2,3},{3,2},{4,5},{5,4},{6,7},{7,6},{8,9},{9,8},{10,11... | collective-permute-start | bytes 5013512 | tf_op jit(solution)/shard_map/ppermute | solution.py:396
  49.0 16.2 %collective-permute-start.4 = (bf16[96,2176]{1,0:T(8,128)(2,1)S(1)}, bf16[96,2176]{1,0:T(8,128)(2,1)S(1)}, u32[]{:S(2)}, u32[]{:S(2)}) collective-permute-start(bf16[96,2176]{1,0:T(8,128)(2,1)S(1)} %collective-permute-done.refs_0_.refs_1_), channel_id=1, source_target_pairs={{0,2},{1,3},{2,4},{3,5},{4,6},{5,7},{6,0},{7,1},{8,10},{9,11},{10,... | collective-permute-start | bytes 1253384 | tf_op jit(solution)/shard_map/ppermute | solution.py:396
  50.3 14.9 %collective-permute-start.5 = (bf16[96,2176]{1,0:T(8,128)(2,1)S(1)}, bf16[96,2176]{1,0:T(8,128)(2,1)S(1)}, u32[]{:S(2)}, u32[]{:S(2)}) collective-permute-start(bf16[96,2176]{1,0:T(8,128)(2,1)S(1)} %collective-permute-done.refs_0_.refs_1_), channel_id=1, source_target_pairs={{0,6},{1,7},{2,0},{3,1},{4,2},{5,3},{6,4},{7,5},{8,14},{9,15},{10,... | collective-permute-start | bytes 1253384 | tf_op jit(solution)/shard_map/ppermute | solution.py:396
  65.2 11.2 %collective-permute-start.11 = (bf16[96,2048]{1,0:T(8,128)(2,1)S(1)}, bf16[96,2048]{1,0:T(8,128)(2,1)S(1)}, u32[]{:S(2)}, u32[]{:S(2)}) collective-permute-start(bf16[96,2048]{1,0:T(8,128)(2,1)S(1)} %pad_maximum_fusion.4.refs_11_), channel_id=1, source_target_pairs={{0,2},{1,3},{2,4},{3,5},{4,6},{5,7},{6,0},{7,1},{8,10},{9,11},{10,... | collective-permute-start | bytes 1179656 | tf_op jit(solution)/shard_map/ppermute | solution.py:396
  65.2 12.8 %collective-permute-start.12 = (bf16[96,2048]{1,0:T(8,128)(2,1)S(1)}, bf16[96,2048]{1,0:T(8,128)(2,1)S(1)}, u32[]{:S(2)}, u32[]{:S(2)}) collective-permute-start(bf16[96,2048]{1,0:T(8,128)(2,1)S(1)} %pad_maximum_fusion.4.refs_11_), channel_id=1, source_target_pairs={{0,6},{1,7},{2,0},{3,1},{4,2},{5,3},{6,4},{7,5},{8,14},{9,15},{10,... | collective-permute-start | bytes 1179656 | tf_op jit(solution)/shard_map/ppermute | solution.py:396
  68.4 10.9 %collective-permute-start.10 = (bf16[96,2048]{1,0:T(8,128)(2,1)S(1)}, bf16[96,2048]{1,0:T(8,128)(2,1)S(1)}, u32[]{:S(2)}, u32[]{:S(2)}) collective-permute-start(bf16[96,2048]{1,0:T(8,128)(2,1)S(1)} %pad_maximum_fusion.4.refs_11_), channel_id=1, source_target_pairs={{0,8},{1,9},{2,10},{3,11},{4,12},{5,13},{6,14},{7,15},{8,0},{9,1},... | collective-permute-start | bytes 1179656 | tf_op jit(solution)/shard_map/ppermute | solution.py:396
  69.4 13.4 %collective-permute-start.6 = (bf16[96,2176]{1,0:T(8,128)(2,1)S(1)}, bf16[96,2176]{1,0:T(8,128)(2,1)S(1)}, u32[]{:S(2)}, u32[]{:S(2)}) collective-permute-start(bf16[96,2176]{1,0:T(8,128)(2,1)S(1)} %broadcast_select_fusion), channel_id=1, source_target_pairs={{0,2},{1,7},{2,4},{3,1},{4,6},{5,3},{6,0},{7,5},{8,10},{9,15},{10,... | collective-permute-start | bytes 1253384 | tf_op jit(solution)/shard_map/ppermute | solution.py:396
  78.1 11.3 %collective-permute-start.15 = (bf16[96,2048]{1,0:T(8,128)(2,1)S(1)}, bf16[96,2048]{1,0:T(8,128)(2,1)S(1)}, u32[]{:S(2)}, u32[]{:S(2)}) collective-permute-start(bf16[96,2048]{1,0:T(8,128)(2,1)S(1)} %broadcast_select_fusion.3), channel_id=1, source_target_pairs={{0,2},{1,7},{2,4},{3,1},{4,6},{5,3},{6,0},{7,5},{8,10},{9,15},{10,... | collective-permute-start | bytes 1179656 | tf_op jit(solution)/shard_map/ppermute | solution.py:396
  79.4 14.1 %collective-permute-start.13 = (bf16[96,2048]{1,0:T(8,128)(2,1)S(1)}, bf16[96,2048]{1,0:T(8,128)(2,1)S(1)}, u32[]{:S(2)}, u32[]{:S(2)}) collective-permute-start(bf16[96,2048]{1,0:T(8,128)(2,1)S(1)} %collective-permute-done.10.refs_12_), channel_id=1, source_target_pairs={{0,2},{1,3},{2,4},{3,5},{4,6},{5,7},{6,0},{7,1},{8,10},{9,11},{10,... | collective-permute-start | bytes 1179656 | tf_op jit(solution)/shard_map/ppermute | solution.py:396
  80.0 13.5 %collective-permute-start.14 = (bf16[96,2048]{1,0:T(8,128)(2,1)S(1)}, bf16[96,2048]{1,0:T(8,128)(2,1)S(1)}, u32[]{:S(2)}, u32[]{:S(2)}) collective-permute-start(bf16[96,2048]{1,0:T(8,128)(2,1)S(1)} %collective-permute-done.10.refs_12_), channel_id=1, source_target_pairs={{0,6},{1,7},{2,0},{3,1},{4,2},{5,3},{6,4},{7,5},{8,14},{9,15},{10,... | collective-permute-start | bytes 1179656 | tf_op jit(solution)/shard_map/ppermute | solution.py:396
  82.8 23.4 %copy-start.3 = (s32[136]{0:T(256)S(1)}, s32[136]{0:T(256)}, u32[]{:S(2)}) copy-start(s32[136]{0:T(256)} %owner_ref.1) | copy-start | bytes 1636
  82.8 23.4 %collective-permute-start.17 = (bf16[384,2048]{1,0:T(8,128)(2,1)S(1)}, bf16[384,2048]{1,0:T(8,128)(2,1)S(1)}, u32[]{:S(2)}, u32[]{:S(2)}) collective-permute-start(bf16[384,2048]{1,0:T(8,128)(2,1)S(1)} %pad_maximum_fusion.1), channel_id=1, source_target_pairs={{0,1},{1,0},{2,3},{3,2},{4,5},{5,4},{6,7},{7,6},{8,9},{9,8},{10,11... | collective-permute-start | bytes 4718600 | tf_op jit(solution)/shard_map/ppermute | solution.py:396
  89.3 16.9 %collective-permute-start.8 = (bf16[288,2176]{1,0:T(8,128)(2,1)S(1)}, bf16[288,2176]{1,0:T(8,128)(2,1)S(1)}, u32[]{:S(2)}, u32[]{:S(2)}) collective-permute-start(bf16[288,2176]{1,0:T(8,128)(2,1)S(1)} %pad_maximum_fusion.2), channel_id=1, source_target_pairs={{0,1},{1,0},{2,3},{3,2},{4,5},{5,4},{6,7},{7,6},{8,9},{9,8},{10,11... | collective-permute-start | bytes 3760136 | tf_op jit(solution)/shard_map/ppermute | solution.py:396
  93.5 1.8 %collective-permute-start.9 = (bf16[96,2176]{1,0:T(8,128)(2,1)S(1)}, bf16[96,2176]{1,0:T(8,128)(2,1)S(1)}, u32[]{:S(2)}, u32[]{:S(2)}) collective-permute-start(bf16[96,2176]{1,0:T(8,128)(2,1)S(1)} %collective-permute-done.6.refs_7_), channel_id=1, source_target_pairs={{0,1},{1,0},{2,3},{3,2},{4,5},{5,4},{6,7},{7,6},{8,9},{9,8},{10,11... | collective-permute-start | bytes 1253384 | tf_op jit(solution)/shard_map/ppermute | solution.py:396
  93.6 12.6 %collective-permute-start.18 = (bf16[288,2048]{1,0:T(8,128)(2,1)S(1)}, bf16[288,2048]{1,0:T(8,128)(2,1)S(1)}, u32[]{:S(2)}, u32[]{:S(2)}) collective-permute-start(bf16[288,2048]{1,0:T(8,128)(2,1)S(1)} %pad_maximum_fusion.3), channel_id=1, source_target_pairs={{0,1},{1,0},{2,3},{3,2},{4,5},{5,4},{6,7},{7,6},{8,9},{9,8},{10,11... | collective-permute-start | bytes 3538952 | tf_op jit(solution)/shard_map/ppermute | solution.py:396
  95.3 9.0 %collective-permute-start.16 = (bf16[96,2048]{1,0:T(8,128)(2,1)S(1)}, bf16[96,2048]{1,0:T(8,128)(2,1)S(1)}, u32[]{:S(2)}, u32[]{:S(2)}) collective-permute-start(bf16[96,2048]{1,0:T(8,128)(2,1)S(1)} %broadcast_select_fusion.2), channel_id=1, source_target_pairs={{0,2},{1,7},{2,4},{3,1},{4,6},{5,3},{6,0},{7,5},{8,10},{9,15},{10,... | collective-permute-start | bytes 1179656 | tf_op jit(solution)/shard_map/ppermute | solution.py:396
  104.3 1.9 %collective-permute-start.19 = (bf16[96,2048]{1,0:T(8,128)(2,1)S(1)}, bf16[96,2048]{1,0:T(8,128)(2,1)S(1)}, u32[]{:S(2)}, u32[]{:S(2)}) collective-permute-start(bf16[96,2048]{1,0:T(8,128)(2,1)S(1)} %collective-permute-done.16.refs_18_), channel_id=1, source_target_pairs={{0,1},{1,0},{2,3},{3,2},{4,5},{5,4},{6,7},{7,6},{8,9},{9,8},{10,11... | collective-permute-start | bytes 1179656 | tf_op jit(solution)/shard_map/ppermute | solution.py:396
  (6 other events, 11.6 us)

commit v9 on v8

--- a/solution.py
+++ b/solution.py
@@ -351,7 +351,7 @@
             pltpu.SMEM((OWNED,), jnp.int32),
             pltpu.SemaphoreType.DMA((2 * len(BLOCKS),)),
         ],
-        compiler_params=pltpu.CompilerParams(vmem_limit_bytes=40 * 2**20),
+        compiler_params=pltpu.CompilerParams(vmem_limit_bytes=56 * 2**20),
         cost_estimate=pl.CostEstimate(flops=5 * 10**9, bytes_accessed=20 * 2**20, transcendentals=0),
         name="gram",
     )(me, tile_owner, *parts[0], *parts[1])

time: 162 us -> 160 us (0.988)
  the two profiles are of different devices: /device:TPU:0 before, /device:TPU:19 now
where the time goes in v9:
time: 160 us; the launch traced here: 159 us
  Pallas kernels  61.2 us (38%)
  starting transfers between devices  36 us (22%)
  blocking collectives  31.6 us (20%)
  waiting for transfers between devices  13.5 us (8%)
  local copies, waits for them, and re-layouts  12 us (8%)
  other arithmetic  2.87 us (2%)
  between operations  2.36 us (1%)
    pallas_call x3, Pallas kernels, conv(): pl.pallas_call(functools.partial(conv_kernel, first, count), out_shape=ja...  36.1 us
    ppermute x20, starting transfers between devices, send(): return lax.ppermute(block, 'tile', perm)  36 us
    all_to_all x1, blocking collectives, some(): got = lax.all_to_all(coded, 'feat', split_axis=0, concat_axis=0, tiled=True)  31.6 us
    pallas_call x1, Pallas kernels, gram(): pl.pallas_call(gram_kernel, out_shape=(jax.ShapeDtypeStruct((FEAT, SLOTS,...  17.4 us
    ppermute x20, waiting for transfers between devices, send(): return lax.ppermute(block, 'tile', perm)  13.5 us
    unnamed x62, local copies, waits for them, and re-layouts  8.26 us
    pallas_call x1, Pallas kernels, prep(): pl.pallas_call(prep_kernel, out_shape=(jax.ShapeDtypeStruct((16, NBLK, 16...  7.75 us
  transfers between devices with their start and end apart: 20, of which 6 were waited for; matrix products, arithmetic and copies ran while one was open for 1% of the time, Pallas kernels for 11%

profile of v9, /device:TPU:19, one launch (start us, length us, event | category | flops | bytes accessed | tf_op | source)
XLA Modules:
  0.0 159.5 jit_solution(6620318950374368010)
XLA Ops:
  1.3 1.7 %copy-done = bf16[96,12288]{1,0:T(8,128)(2,1)S(1)} copy-done((bf16[96,12288]{1,0:T(8,128)(2,1)S(1)}, bf16[96,12288]{1,0:T(8,128)(2,1)}, u32[]{:S(2)}) %copy-start) | copy-done | bytes 2359320
  4.6 7.8 %prep.1 = (bf16[16,6,160,128]{3,2,1,0:T(8,128)(2,1)S(1)}, bf16[16,80,128]{2,1,0:T(8,128)(2,1)S(1)}, bf16[4,1536,256]{2,1,0:T(8,128)(2,1)S(1)}, bf16[96,256]{1,0:...) custom-call(s32[1]{0:T(128)} %bitcast.12.me_ref, s32[1,136]{1,0:T(1,128)S(1)} %bitcast.39, ...), custom_call_target="tpu_custom_call" | custom-call | tf_op jit(solution)/shard_map/prep/pallas_call | solution.py:97
  13.1 17.8 %conv.3.refs_0_ = bf16[96,2176]{1,0:T(8,128)(2,1)S(1)} custom-call(s32[1,4]{1,0:T(1,128)S(1)} %get-tuple-element.41.nblk_ref.me_ref, bf16[16,6,160,128]{3,2,1,0:T(8,128)(2,1)S(1)} %get-tuple-element.42.win_ref, bf16[16,80,128]{2,1,0:T(8,128)(2,1)S(1)} %get-tuple-element.43.half_ref, bf16[4,1536,256]{2,1,0:T(8,128)(2,1)S(1)} %get-tuple-element.44.w_ref, ...), custom_call_target="tpu_custom_call" | custom-call | flops 22649241600 | bytes 8388608 | tf_op jit(solution)/shard_map/conv/pallas_call | solution.py:223
  32.5 9.2 %conv.4 = bf16[96,1024]{1,0:T(8,128)(2,1)S(1)} custom-call(s32[1,4]{1,0:T(1,128)S(1)} %get-tuple-element.41.nblk_ref.me_ref, bf16[16,6,160,128]{3,2,1,0:T(8,128)(2,1)S(1)} %get-tuple-element.42.win_ref, bf16[16,80,128]{2,1,0:T(8,128)(2,1)S(1)} %get-tuple-element.43.half_ref, bf16[4,1536,256]{2,1,0:T(8,128)(2,1)S(1)} %get-tuple-element.44.w_ref, ...), custom_call_target="tpu_custom_call" | custom-call | flops 11324620800 | bytes 8388608 | tf_op jit(solution)/shard_map/conv/pallas_call | solution.py:223
  41.8 3.1 %collective-permute-start.3 = (bf16[96,2176]{1,0:T(8,128)(2,1)S(1)}, bf16[96,2176]{1,0:T(8,128)(2,1)S(1)}, u32[]{:S(2)}, u32[]{:S(2)}) collective-permute-start(bf16[96,2176]{1,0:T(8,128)(2,1)S(1)} %broadcast_select_fusion.1), channel_id=1, source_target_pairs={{0,2},{1,7},{2,4},{3,1},{4,6},{5,3},{6,0},{7,5},{8,10},{9,15},{10,... | collective-permute-start | bytes 1253384 | tf_op jit(solution)/shard_map/ppermute | solution.py:396
  45.0 2.1 %collective-permute-start.7 = (bf16[384,2176]{1,0:T(8,128)(2,1)S(1)}, bf16[384,2176]{1,0:T(8,128)(2,1)S(1)}, u32[]{:S(2)}, u32[]{:S(2)}) collective-permute-start(bf16[384,2176]{1,0:T(8,128)(2,1)S(1)} %pad_maximum_fusion), channel_id=1, source_target_pairs={{0,1},{1,0},{2,3},{3,2},{4,5},{5,4},{6,7},{7,6},{8,9},{9,8},{10,11... | collective-permute-start | bytes 5013512 | tf_op jit(solution)/shard_map/ppermute | solution.py:396
  47.1 2.4 %collective-permute-start.4 = (bf16[96,2176]{1,0:T(8,128)(2,1)S(1)}, bf16[96,2176]{1,0:T(8,128)(2,1)S(1)}, u32[]{:S(2)}, u32[]{:S(2)}) collective-permute-start(bf16[96,2176]{1,0:T(8,128)(2,1)S(1)} %collective-permute-done.refs_0_.refs_1_), channel_id=1, source_target_pairs={{0,2},{1,3},{2,4},{3,5},{4,6},{5,7},{6,0},{7,1},{8,10},{9,11},{10,... | collective-permute-start | bytes 1253384 | tf_op jit(solution)/shard_map/ppermute | solution.py:396
  49.5 1.9 %copy-done.10 = bf16[4,1536,256]{2,1,0:T(8,128)(2,1)S(1)} copy-done((bf16[4,1536,256]{2,1,0:T(8,128)(2,1)S(1)}, bf16[4,1536,256]{2,1,0:T(8,128)(2,1)}, u32[]{:S(2)}) %copy-start.10) | copy-done | bytes 3145752
  51.4 9.2 %conv.5 = bf16[96,1024]{1,0:T(8,128)(2,1)S(1)} custom-call(s32[1,4]{1,0:T(1,128)S(1)} %get-tuple-element.41.nblk_ref.me_ref, bf16[16,6,160,128]{3,2,1,0:T(8,128)(2,1)S(1)} %copy-done.8, bf16[16,80,128]{2,1,0:T(8,128)(2,1)S(1)} %get-tuple-element.43.half_ref, bf16[4,1536,256]{2,1,0:T(8,128)(2,1)S(1)} %copy-done.10, ...), custom_call_target="tpu_custom_call" | custom-call | flops 11324620800 | bytes 8388608 | tf_op jit(solution)/shard_map/conv/pallas_call | solution.py:223
  60.7 1.5 collective-permute-start.11
  62.2 2.7 %collective-permute-start.10 = (bf16[96,2048]{1,0:T(8,128)(2,1)S(1)}, bf16[96,2048]{1,0:T(8,128)(2,1)S(1)}, u32[]{:S(2)}, u32[]{:S(2)}) collective-permute-start(bf16[96,2048]{1,0:T(8,128)(2,1)S(1)} %pad_maximum_fusion.4.refs_11_), channel_id=1, source_target_pairs={{0,8},{1,9},{2,10},{3,11},{4,12},{5,13},{6,14},{7,15},{8,0},{9,1},... | collective-permute-start | bytes 1179656 | tf_op jit(solution)/shard_map/ppermute | solution.py:396
  64.9 2.7 %collective-permute-start.6 = (bf16[96,2176]{1,0:T(8,128)(2,1)S(1)}, bf16[96,2176]{1,0:T(8,128)(2,1)S(1)}, u32[]{:S(2)}, u32[]{:S(2)}) collective-permute-start(bf16[96,2176]{1,0:T(8,128)(2,1)S(1)} %broadcast_select_fusion), channel_id=1, source_target_pairs={{0,2},{1,7},{2,4},{3,1},{4,6},{5,3},{6,0},{7,5},{8,10},{9,15},{10,... | collective-permute-start | bytes 1253384 | tf_op jit(solution)/shard_map/ppermute | solution.py:396
  67.6 1.4 collective-permute-done.11.refs_13_
  70.7 2.4 %collective-permute-start.13 = (bf16[96,2048]{1,0:T(8,128)(2,1)S(1)}, bf16[96,2048]{1,0:T(8,128)(2,1)S(1)}, u32[]{:S(2)}, u32[]{:S(2)}) collective-permute-start(bf16[96,2048]{1,0:T(8,128)(2,1)S(1)} %collective-permute-done.10.refs_12_), channel_id=1, source_target_pairs={{0,2},{1,3},{2,4},{3,5},{4,6},{5,7},{6,0},{7,1},{8,10},{9,11},{10,... | collective-permute-start | bytes 1179656 | tf_op jit(solution)/shard_map/ppermute | solution.py:396
  73.3 4.5 %collective-permute-done.6.refs_7_ = bf16[96,2176]{1,0:T(8,128)(2,1)S(1)} collective-permute-done((bf16[96,2176]{1,0:T(8,128)(2,1)S(1)}, bf16[96,2176]{1,0:T(8,128)(2,1)S(1)}, u32[]{:S(2)}, u32[]{:S(2)}) %collective-permute-start.6) | collective-permute-done | bytes 417824 | tf_op jit(solution)/shard_map/ppermute | solution.py:396
  77.8 3.8 %collective-permute-start.17 = (bf16[384,2048]{1,0:T(8,128)(2,1)S(1)}, bf16[384,2048]{1,0:T(8,128)(2,1)}, u32[]{:S(2)}, u32[]{:S(2)}) collective-permute-start(bf16[384,2048]{1,0:T(8,128)(2,1)S(1)} %pad_maximum_fusion.1), channel_id=1, source_target_pairs={{0,1},{1,0},{2,3},{3,2},{4,5},{5,4},{6,7},{7,6},{8,9},{9,8},{10,11... | collective-permute-start | bytes 4718600 | tf_op jit(solution)/shard_map/ppermute | solution.py:396
  82.0 4.6 %collective-permute-start.8 = (bf16[288,2176]{1,0:T(8,128)(2,1)S(1)}, bf16[288,2176]{1,0:T(8,128)(2,1)S(1)}, u32[]{:S(2)}, u32[]{:S(2)}) collective-permute-start(bf16[288,2176]{1,0:T(8,128)(2,1)S(1)} %pad_maximum_fusion.2), channel_id=1, source_target_pairs={{0,1},{1,0},{2,3},{3,2},{4,5},{5,4},{6,7},{7,6},{8,9},{9,8},{10,11... | collective-permute-start | bytes 3760136 | tf_op jit(solution)/shard_map/ppermute | solution.py:396
  86.6 4.2 %collective-permute-start.9 = (bf16[96,2176]{1,0:T(8,128)(2,1)S(1)}, bf16[96,2176]{1,0:T(8,128)(2,1)S(1)}, u32[]{:S(2)}, u32[]{:S(2)}) collective-permute-start(bf16[96,2176]{1,0:T(8,128)(2,1)S(1)} %collective-permute-done.6.refs_7_), channel_id=1, source_target_pairs={{0,1},{1,0},{2,3},{3,2},{4,5},{5,4},{6,7},{7,6},{8,9},{9,8},{10,11... | collective-permute-start | bytes 1253384 | tf_op jit(solution)/shard_map/ppermute | solution.py:396
  92.2 3.0 %collective-permute-start.16 = (bf16[96,2048]{1,0:T(8,128)(2,1)S(1)}, bf16[96,2048]{1,0:T(8,128)(2,1)S(1)}, u32[]{:S(2)}, u32[]{:S(2)}) collective-permute-start(bf16[96,2048]{1,0:T(8,128)(2,1)S(1)} %broadcast_select_fusion.2), channel_id=1, source_target_pairs={{0,2},{1,7},{2,4},{3,1},{4,6},{5,3},{6,0},{7,5},{8,10},{9,15},{10,... | collective-permute-start | bytes 1179656 | tf_op jit(solution)/shard_map/ppermute | solution.py:396
  95.1 4.7 %collective-permute-done.16.refs_18_ = bf16[96,2048]{1,0:T(8,128)(2,1)S(1)} collective-permute-done((bf16[96,2048]{1,0:T(8,128)(2,1)S(1)}, bf16[96,2048]{1,0:T(8,128)(2,1)S(1)}, u32[]{:S(2)}, u32[]{:S(2)}) %collective-permute-start.16) | collective-permute-done | bytes 393248 | tf_op jit(solution)/shard_map/ppermute | solution.py:396
  99.9 1.7 %collective-permute-start.19 = (bf16[96,2048]{1,0:T(8,128)(2,1)S(1)}, bf16[96,2048]{1,0:T(8,128)(2,1)S(1)}, u32[]{:S(2)}, u32[]{:S(2)}) collective-permute-start(bf16[96,2048]{1,0:T(8,128)(2,1)S(1)} %collective-permute-done.16.refs_18_), channel_id=1, source_target_pairs={{0,1},{1,0},{2,3},{3,2},{4,5},{5,4},{6,7},{7,6},{8,9},{9,8},{10,11... | collective-permute-start | bytes 1179656 | tf_op jit(solution)/shard_map/ppermute | solution.py:396
  105.8 17.4 %gram.1 = (f32[8,25,32,256]{3,2,1,0:T(8,128)S(1)}, f32[8,256]{1,0:T(8,128)}) custom-call(s32[1,4]{1,0:T(1,128)} %copy-done.13, s32[136]{0:T(256)} %owner_ref.1, bf16[96,2176]{1,0:T(8,128)(2,1)} %copy-done.3, bf16[96,2176]{1,0:T(8,128)(2,1)} %copy-done.4, bf16[96,2176]{1,0:T(8,128)(2,1)} %copy-done.1, bf16[96,2176]{1,0:T(8,128)(2,1)} %copy-done.2, ...), custom_call_target="tpu_custom_call" | custom-call | flops 5000000000 | bytes 20971520 | tf_op jit(solution)/shard_map/gram/pallas_call | solution.py:339
  124.0 35.5 %conditional.1 = (f32[20,32,256]{2,1,0:T(8,128)}, f32[32,1000]{1,0:T(8,128)}) conditional(s32[]{:T(128)} %bitcast.16, (f32[1,1,1,256]{3,2,1,0:T(1,128)S(1)}, f32[8,25,32,256]{3,2,1,0:T(8,128)S(1)}, f32[1,1,1,256]{3,2,1,0:T(1,128)S(1)}) %tuple.21, (f32[1,1,1,256]{3,2,1,0:T(1,128)S(1)}, f32[8,25,32,256]{3,2,1,0:T(8,128)S(1)}, ...), branch_computations={%region_0.2_spmd, %region_2.4_spmd, %region_4.6_spmd} | conditional | flops 9625657 | bytes 22317266 | solution.py:381
  125.2 31.6 %all_to_all.14 = f16[8,25,32,256]{3,2,1,0:T(8,128)(2,1)S(1)} all-to-all(f16[8,25,32,256]{3,2,1,0:T(8,128)(2,1)S(1)} %select_convert_fusion.2), channel_id=1, replica_groups=mesh['feat'=8,'tile'=16] {'feat'}, dimensions={0} | all-to-all | bytes 6553600 | tf_op jit(solution)/shard_map/cond/branch_2_fun/all_to_all | solution.py:374
  (106 shorter events, 16.0 us)
Async XLA Ops:
  12.4 89.2 %copy-start.13 = (s32[1,4]{1,0:T(1,128)}, s32[1,4]{1,0:T(1,128)S(1)}, u32[]{:S(2)}) copy-start(s32[1,4]{1,0:T(1,128)S(1)} %get-tuple-element.41.nblk_ref.me_ref) | copy-start | bytes 52
  30.9 10.8 %collective-permute-start.1 = (bf16[96,2176]{1,0:T(8,128)(2,1)S(1)}, bf16[96,2176]{1,0:T(8,128)(2,1)S(1)}, u32[]{:S(2)}, u32[]{:S(2)}) collective-permute-start(bf16[96,2176]{1,0:T(8,128)(2,1)S(1)} %conv.3.refs_0_), channel_id=1, source_target_pairs={{0,2},{1,3},{2,4},{3,5},{4,6},{5,7},{6,0},{7,1},{8,10},{9,11},{10,... | collective-permute-start | bytes 1253384 | tf_op jit(solution)/shard_map/ppermute | solution.py:396
  32.2 9.5 %collective-permute-start.2 = (bf16[96,2176]{1,0:T(8,128)(2,1)S(1)}, bf16[96,2176]{1,0:T(8,128)(2,1)S(1)}, u32[]{:S(2)}, u32[]{:S(2)}) collective-permute-start(bf16[96,2176]{1,0:T(8,128)(2,1)S(1)} %conv.3.refs_0_), channel_id=1, source_target_pairs={{0,6},{1,7},{2,0},{3,1},{4,2},{5,3},{6,4},{7,5},{8,14},{9,15},{10,... | collective-permute-start | bytes 1253384 | tf_op jit(solution)/shard_map/ppermute | solution.py:396
  32.4 12.5 %collective-permute-start = (bf16[96,2176]{1,0:T(8,128)(2,1)S(1)}, bf16[96,2176]{1,0:T(8,128)(2,1)S(1)}, u32[]{:S(2)}, u32[]{:S(2)}) collective-permute-start(bf16[96,2176]{1,0:T(8,128)(2,1)S(1)} %conv.3.refs_0_), channel_id=1, source_target_pairs={{0,8},{1,9},{2,10},{3,11},{4,12},{5,13},{6,14},{7,15},{8,0},{9,1},... | collective-permute-start | bytes 1253384 | tf_op jit(solution)/shard_map/ppermute | solution.py:396
  41.8 18.8 %collective-permute-start.3 = (bf16[96,2176]{1,0:T(8,128)(2,1)S(1)}, bf16[96,2176]{1,0:T(8,128)(2,1)S(1)}, u32[]{:S(2)}, u32[]{:S(2)}) collective-permute-start(bf16[96,2176]{1,0:T(8,128)(2,1)S(1)} %broadcast_select_fusion.1), channel_id=1, source_target_pairs={{0,2},{1,7},{2,4},{3,1},{4,6},{5,3},{6,0},{7,5},{8,10},{9,15},{10,... | collective-permute-start | bytes 1253384 | tf_op jit(solution)/shard_map/ppermute | solution.py:396
  45.0 58.4 %collective-permute-start.7 = (bf16[384,2176]{1,0:T(8,128)(2,1)S(1)}, bf16[384,2176]{1,0:T(8,128)(2,1)S(1)}, u32[]{:S(2)}, u32[]{:S(2)}) collective-permute-start(bf16[384,2176]{1,0:T(8,128)(2,1)S(1)} %pad_maximum_fusion), channel_id=1, source_target_pairs={{0,1},{1,0},{2,3},{3,2},{4,5},{5,4},{6,7},{7,6},{8,9},{9,8},{10,11... | collective-permute-start | bytes 5013512 | tf_op jit(solution)/shard_map/ppermute | solution.py:396
  47.1 13.5 %collective-permute-start.4 = (bf16[96,2176]{1,0:T(8,128)(2,1)S(1)}, bf16[96,2176]{1,0:T(8,128)(2,1)S(1)}, u32[]{:S(2)}, u32[]{:S(2)}) collective-permute-start(bf16[96,2176]{1,0:T(8,128)(2,1)S(1)} %collective-permute-done.refs_0_.refs_1_), channel_id=1, source_target_pairs={{0,2},{1,3},{2,4},{3,5},{4,6},{5,7},{6,0},{7,1},{8,10},{9,11},{10,... | collective-permute-start | bytes 1253384 | tf_op jit(solution)/shard_map/ppermute | solution.py:396
  49.5 11.2 %collective-permute-start.5 = (bf16[96,2176]{1,0:T(8,128)(2,1)S(1)}, bf16[96,2176]{1,0:T(8,128)(2,1)S(1)}, u32[]{:S(2)}, u32[]{:S(2)}) collective-permute-start(bf16[96,2176]{1,0:T(8,128)(2,1)S(1)} %collective-permute-done.refs_0_.refs_1_), channel_id=1, source_target_pairs={{0,6},{1,7},{2,0},{3,1},{4,2},{5,3},{6,4},{7,5},{8,14},{9,15},{10,... | collective-permute-start | bytes 1253384 | tf_op jit(solution)/shard_map/ppermute | solution.py:396
  60.6 21.1 %copy-start.16 = (bf16[96,2048]{1,0:T(8,128)(2,1)}, bf16[96,2048]{1,0:T(8,128)(2,1)S(1)}, u32[]{:S(2)}) copy-start(bf16[96,2048]{1,0:T(8,128)(2,1)S(1)} %pad_maximum_fusion.4.refs_11_) | copy-start | bytes 1179652
  60.7 8.4 %collective-permute-start.11 = (bf16[96,2048]{1,0:T(8,128)(2,1)S(1)}, bf16[96,2048]{1,0:T(8,128)(2,1)S(1)}, u32[]{:S(2)}, u32[]{:S(2)}) collective-permute-start(bf16[96,2048]{1,0:T(8,128)(2,1)S(1)} %pad_maximum_fusion.4.refs_11_), channel_id=1, source_target_pairs={{0,2},{1,3},{2,4},{3,5},{4,6},{5,7},{6,0},{7,1},{8,10},{9,11},{10,... | collective-permute-start | bytes 1179656 | tf_op jit(solution)/shard_map/ppermute | solution.py:396
  62.2 8.2 %collective-permute-start.12 = (bf16[96,2048]{1,0:T(8,128)(2,1)S(1)}, bf16[96,2048]{1,0:T(8,128)(2,1)S(1)}, u32[]{:S(2)}, u32[]{:S(2)}) collective-permute-start(bf16[96,2048]{1,0:T(8,128)(2,1)S(1)} %pad_maximum_fusion.4.refs_11_), channel_id=1, source_target_pairs={{0,6},{1,7},{2,0},{3,1},{4,2},{5,3},{6,4},{7,5},{8,14},{9,15},{10,... | collective-permute-start | bytes 1179656 | tf_op jit(solution)/shard_map/ppermute | solution.py:396
  62.2 8.5 %collective-permute-start.10 = (bf16[96,2048]{1,0:T(8,128)(2,1)S(1)}, bf16[96,2048]{1,0:T(8,128)(2,1)S(1)}, u32[]{:S(2)}, u32[]{:S(2)}) collective-permute-start(bf16[96,2048]{1,0:T(8,128)(2,1)S(1)} %pad_maximum_fusion.4.refs_11_), channel_id=1, source_target_pairs={{0,8},{1,9},{2,10},{3,11},{4,12},{5,13},{6,14},{7,15},{8,0},{9,1},... | collective-permute-start | bytes 1179656 | tf_op jit(solution)/shard_map/ppermute | solution.py:396
  64.9 12.9 %collective-permute-start.6 = (bf16[96,2176]{1,0:T(8,128)(2,1)S(1)}, bf16[96,2176]{1,0:T(8,128)(2,1)S(1)}, u32[]{:S(2)}, u32[]{:S(2)}) collective-permute-start(bf16[96,2176]{1,0:T(8,128)(2,1)S(1)} %broadcast_select_fusion), channel_id=1, source_target_pairs={{0,2},{1,7},{2,4},{3,1},{4,6},{5,3},{6,0},{7,5},{8,10},{9,15},{10,... | collective-permute-start | bytes 1253384 | tf_op jit(solution)/shard_map/ppermute | solution.py:396
  70.5 11.5 %collective-permute-start.15 = (bf16[96,2048]{1,0:T(8,128)(2,1)S(1)}, bf16[96,2048]{1,0:T(8,128)(2,1)S(1)}, u32[]{:S(2)}, u32[]{:S(2)}) collective-permute-start(bf16[96,2048]{1,0:T(8,128)(2,1)S(1)} %broadcast_select_fusion.3), channel_id=1, source_target_pairs={{0,2},{1,7},{2,4},{3,1},{4,6},{5,3},{6,0},{7,5},{8,10},{9,15},{10,... | collective-permute-start | bytes 1179656 | tf_op jit(solution)/shard_map/ppermute | solution.py:396
  70.7 15.9 %collective-permute-start.13 = (bf16[96,2048]{1,0:T(8,128)(2,1)S(1)}, bf16[96,2048]{1,0:T(8,128)(2,1)S(1)}, u32[]{:S(2)}, u32[]{:S(2)}) collective-permute-start(bf16[96,2048]{1,0:T(8,128)(2,1)S(1)} %collective-permute-done.10.refs_12_), channel_id=1, source_target_pairs={{0,2},{1,3},{2,4},{3,5},{4,6},{5,7},{6,0},{7,1},{8,10},{9,11},{10,... | collective-permute-start | bytes 1179656 | tf_op jit(solution)/shard_map/ppermute | solution.py:396
  73.1 17.7 %collective-permute-start.14 = (bf16[96,2048]{1,0:T(8,128)(2,1)S(1)}, bf16[96,2048]{1,0:T(8,128)(2,1)S(1)}, u32[]{:S(2)}, u32[]{:S(2)}) collective-permute-start(bf16[96,2048]{1,0:T(8,128)(2,1)S(1)} %collective-permute-done.10.refs_12_), channel_id=1, source_target_pairs={{0,6},{1,7},{2,0},{3,1},{4,2},{5,3},{6,4},{7,5},{8,14},{9,15},{10,... | collective-permute-start | bytes 1179656 | tf_op jit(solution)/shard_map/ppermute | solution.py:396
  77.8 25.7 %copy-start.27 = (bf16[96,2176]{1,0:T(8,128)(2,1)}, bf16[96,2176]{1,0:T(8,128)(2,1)S(1)}, u32[]{:S(2)}) copy-start(bf16[96,2176]{1,0:T(8,128)(2,1)S(1)} %collective-permute-done.6.refs_7_) | copy-start | bytes 1253380
  77.8 28.0 %collective-permute-start.17 = (bf16[384,2048]{1,0:T(8,128)(2,1)S(1)}, bf16[384,2048]{1,0:T(8,128)(2,1)}, u32[]{:S(2)}, u32[]{:S(2)}) collective-permute-start(bf16[384,2048]{1,0:T(8,128)(2,1)S(1)} %pad_maximum_fusion.1), channel_id=1, source_target_pairs={{0,1},{1,0},{2,3},{3,2},{4,5},{5,4},{6,7},{7,6},{8,9},{9,8},{10,11... | collective-permute-start | bytes 4718600 | tf_op jit(solution)/shard_map/ppermute | solution.py:396
  82.0 21.5 %copy-start.23 = (bf16[96,2048]{1,0:T(8,128)(2,1)}, bf16[96,2048]{1,0:T(8,128)(2,1)S(1)}, u32[]{:S(2)}) copy-start(bf16[96,2048]{1,0:T(8,128)(2,1)S(1)} %collective-permute-done.15.refs_17_) | copy-start | bytes 1179652
  82.0 21.4 %collective-permute-start.8 = (bf16[288,2176]{1,0:T(8,128)(2,1)S(1)}, bf16[288,2176]{1,0:T(8,128)(2,1)S(1)}, u32[]{:S(2)}, u32[]{:S(2)}) collective-permute-start(bf16[288,2176]{1,0:T(8,128)(2,1)S(1)} %pad_maximum_fusion.2), channel_id=1, source_target_pairs={{0,1},{1,0},{2,3},{3,2},{4,5},{5,4},{6,7},{7,6},{8,9},{9,8},{10,11... | collective-permute-start | bytes 3760136 | tf_op jit(solution)/shard_map/ppermute | solution.py:396
  86.6 5.6 %collective-permute-start.9 = (bf16[96,2176]{1,0:T(8,128)(2,1)S(1)}, bf16[96,2176]{1,0:T(8,128)(2,1)S(1)}, u32[]{:S(2)}, u32[]{:S(2)}) collective-permute-start(bf16[96,2176]{1,0:T(8,128)(2,1)S(1)} %collective-permute-done.6.refs_7_), channel_id=1, source_target_pairs={{0,1},{1,0},{2,3},{3,2},{4,5},{5,4},{6,7},{7,6},{8,9},{9,8},{10,11... | collective-permute-start | bytes 1253384 | tf_op jit(solution)/shard_map/ppermute | solution.py:396
  90.9 12.6 %collective-permute-start.18 = (bf16[288,2048]{1,0:T(8,128)(2,1)S(1)}, bf16[288,2048]{1,0:T(8,128)(2,1)S(1)}, u32[]{:S(2)}, u32[]{:S(2)}) collective-permute-start(bf16[288,2048]{1,0:T(8,128)(2,1)S(1)} %pad_maximum_fusion.3), channel_id=1, source_target_pairs={{0,1},{1,0},{2,3},{3,2},{4,5},{5,4},{6,7},{7,6},{8,9},{9,8},{10,11... | collective-permute-start | bytes 3538952 | tf_op jit(solution)/shard_map/ppermute | solution.py:396
  92.2 7.7 %collective-permute-start.16 = (bf16[96,2048]{1,0:T(8,128)(2,1)S(1)}, bf16[96,2048]{1,0:T(8,128)(2,1)S(1)}, u32[]{:S(2)}, u32[]{:S(2)}) collective-permute-start(bf16[96,2048]{1,0:T(8,128)(2,1)S(1)} %broadcast_select_fusion.2), channel_id=1, source_target_pairs={{0,2},{1,7},{2,4},{3,1},{4,6},{5,3},{6,0},{7,5},{8,10},{9,15},{10,... | collective-permute-start | bytes 1179656 | tf_op jit(solution)/shard_map/ppermute | solution.py:396
  99.9 3.6 %collective-permute-start.19 = (bf16[96,2048]{1,0:T(8,128)(2,1)S(1)}, bf16[96,2048]{1,0:T(8,128)(2,1)S(1)}, u32[]{:S(2)}, u32[]{:S(2)}) collective-permute-start(bf16[96,2048]{1,0:T(8,128)(2,1)S(1)} %collective-permute-done.16.refs_18_), channel_id=1, source_target_pairs={{0,1},{1,0},{2,3},{3,2},{4,5},{5,4},{6,7},{7,6},{8,9},{9,8},{10,11... | collective-permute-start | bytes 1179656 | tf_op jit(solution)/shard_map/ppermute | solution.py:396
  (27 other events, 301.0 us)
